TPU v7x, 128 devices: a whole 4x4x4 slice. The times are simulated.
128 devices in a mesh: box: 128 (over z, x, y, core).
Axes of the slice: x: 4, y: 4, z: 4, core: 2. Of those that a mesh axis runs over, the one named last changes fastest.
Arguments:
- source: float32 [512, 32, 1024], P('box'), may hold values from -6 to 6
- conductance: float32 [512, 32, 1024], P('box'), may hold values from 0.3 to 3
- initial: float32 [512, 32, 1024], P('box'), may hold values from -6 to 6
- box_counts: int32 [128], replicated, may hold values from 1 to 3, as said below
Outputs:
- solution_field: float32 [512, 32, 1024], P('box')
- residual: float32 [512, 32, 1024], P('box')
Inputs may be any that keep to these rules, and one draw needn't show every extreme that they name: `box_counts`: devices 2q and 2q + 1 together own the 4 boxes of column q of the box grid (the boxes q * 4 to q * 4 + 3).
All inputs are finite; a program needn't handle non-finite values.
Results may differ from a plain program's by a relative error of at most 0.0003.
Values sent between devices are 32-bit elements; how exact they have to be, the bound alone decides.
A program may use at most 128 MiB of HBM per device.

v0:
```python
import jax
import jax.numpy as jnp
from jax import lax
from jax.sharding import PartitionSpec as P

COLUMNS_Y = 4
NU = 2
NU_COARSE = 4


OMEGA = 0.8


def shifted(value, axis, steps):
    count = lax.axis_size(axis)
    leading, last = (max(0, -steps), min(count, count - steps))
    return lax.ppermute(value, axis, [(source, source + steps) for source in range(leading, last)])


def lookup(table, position):
    rank_ids = jnp.arange(table.shape[0], dtype=jnp.int32)
    return jnp.sum(jnp.where(rank_ids == position, table, 0))


def layout_of(counts, rank, slot_count, pencil_total):
    half = rank % 2
    pencil = rank // 2
    split = lookup(counts, 2 * pencil)
    own = lookup(counts, rank)
    slots = jnp.arange(slot_count, dtype=jnp.int32)
    depth_box = half * split + slots
    occupied = slots < own
    return (counts, rank, half, pencil, own, depth_box, occupied, slots, pencil_total)


def across(layout, step, base, row_count):
    counts, rank, half, pencil, own, depth_box, occupied, slots, pencil_total = layout
    other = jnp.clip(pencil + step, 0, pencil_total - 1)
    split = lookup(counts, 2 * other)
    upper = (depth_box >= split).astype(jnp.int32)
    owner = 2 * other + upper
    place = depth_box - upper * split
    distance = jnp.abs(rank - owner)
    return (distance - base) * row_count + place


def lane_tables(box_edge):
    area = box_edge * box_edge
    lanes = jnp.arange(area, dtype=jnp.int32)[None, :]
    ids = jnp.arange(box_edge, dtype=jnp.int32)[:, None]
    y_low = (lanes == ids).astype(jnp.float32)
    y_high = (lanes == (box_edge - 1) * box_edge + ids).astype(jnp.float32)
    z_low = (lanes == ids * box_edge).astype(jnp.float32)
    z_high = (lanes == ids * box_edge + box_edge - 1).astype(jnp.float32)
    return (y_low, y_high, z_low, z_high)


def take_plane(field, table):
    slot_count, box_edge, area = field.shape
    picked = jnp.einsum("sxl,kl->sxk", field, table, precision=lax.Precision.HIGHEST)
    return picked.reshape(slot_count, box_edge * box_edge)


def place_plane(plane, table):
    slot_count = plane.shape[0]
    box_edge = table.shape[0]
    shaped = plane.reshape(slot_count, box_edge, box_edge)
    return jnp.einsum("sxk,kl->sxl", shaped, table, precision=lax.Precision.HIGHEST)


def face_set(field):
    slot_count, box_edge, area = field.shape
    tables = lane_tables(box_edge)
    lower_x = field[:, 0, :]
    upper_x = field[:, box_edge - 1, :]
    lower_y = field[:, :, :box_edge].reshape(slot_count, area)
    upper_y = field[:, :, area - box_edge :].reshape(slot_count, area)
    lower_z = take_plane(field, tables[2])
    upper_z = take_plane(field, tables[3])
    return (lower_x, upper_x, lower_y, upper_y, lower_z, upper_z)


def fetch_ghosts(fields, layout):
    counts, rank, half, pencil, own, depth_box, occupied, slots, pencil_total = layout
    slot_count = fields[0].shape[0]
    sets = [face_set(field) for field in fields]

    def stacked(kind):
        return jnp.stack([faces[kind] for faces in sets])

    top_depth = lax.dynamic_slice_in_dim(stacked(5), own - 1, 1, 1)
    bottom_depth = stacked(4)[:, :1]
    up_pack = jnp.concatenate([stacked(3), top_depth], axis=1)
    down_pack = jnp.concatenate([stacked(2), bottom_depth], axis=1)
    front_up = stacked(1)
    front_down = stacked(0)
    side_rows = slot_count + 1
    reach = 2 * COLUMNS_Y
    side_got = []
    front_got = []
    side_base = 1
    front_base = reach - 1
    for shift_by in (1, 2, 3, -1, -2, -3):
        side_got.append(shifted(up_pack if shift_by > 0 else down_pack, "box", shift_by))
    for shift_by in (reach - 1, reach, reach + 1, 1 - reach, -reach, -reach - 1):
        front_got.append(shifted(front_up if shift_by > 0 else front_down, "box", shift_by))
    depth_low = side_got[0][:, slot_count:]
    depth_high = side_got[3][:, slot_count:]
    half_count = len(side_got) // 2
    tables = (
        jnp.concatenate(front_got[:half_count], axis=1),
        jnp.concatenate(front_got[half_count:], axis=1),
        jnp.concatenate(side_got[:half_count], axis=1),
        jnp.concatenate(side_got[half_count:], axis=1),
    )
    indexes = (
        across(layout, -COLUMNS_Y, front_base, slot_count),
        across(layout, COLUMNS_Y, front_base, slot_count),
        across(layout, -1, side_base, side_rows),
        across(layout, 1, side_base, side_rows),
    )
    column = pencil % COLUMNS_Y
    masks = (
        occupied & (pencil >= COLUMNS_Y),
        occupied & (pencil < pencil_total - COLUMNS_Y),
        occupied & (column > 0),
        occupied & (column < COLUMNS_Y - 1),
    )
    ghosts = []
    for kind in range(4):
        safe = jnp.where(masks[kind], indexes[kind], 0)
        ghosts.append(jnp.take(tables[kind], safe, axis=1))
    return (ghosts, masks, depth_low, depth_high)


def pick(fetched, which):
    ghosts, masks, depth_low, depth_high = fetched
    return ([ghost[which] for ghost in ghosts], masks, depth_low[which], depth_high[which])


def planes_of(field, package, layout, keep_edge):
    ghosts, masks, depth_low, depth_high = package
    counts, rank, half, pencil, own, depth_box, occupied, slots, pencil_total = layout
    faces = face_set(field)
    if keep_edge:
        fills = faces
    else:
        fills = tuple((jnp.zeros_like(face) for face in faces))
    planes = [jnp.where(masks[kind][:, None], ghosts[kind], fills[kind]) for kind in range(4)]
    below = jnp.concatenate([depth_low, faces[5][:-1]], axis=0)
    below_ok = (slots >= 1) | (half == 1)
    planes.append(jnp.where(below_ok[:, None], below, fills[4]))
    above = jnp.concatenate([faces[4][1:], depth_high], axis=0)
    above = jnp.where((slots == own - 1)[:, None], jnp.broadcast_to(depth_high, above.shape), above)
    above_ok = (slots < own - 1) | (half == 0)
    planes.append(jnp.where(above_ok[:, None], above, fills[5]))
    return planes


def box_neighbours(field, planes):
    slot_count, box_edge, area = field.shape
    tables = lane_tables(box_edge)
    lanes = jnp.arange(area, dtype=jnp.int32)
    depth_pos = lanes % box_edge
    side_pos = lanes // box_edge
    lower_x = jnp.concatenate([planes[0][:, None, :], field[:, :-1, :]], axis=1)
    upper_x = jnp.concatenate([field[:, 1:, :], planes[1][:, None, :]], axis=1)
    shifted_low_y = jnp.concatenate([field[:, :, :box_edge], field[:, :, :-box_edge]], axis=2)
    shifted_high_y = jnp.concatenate([field[:, :, box_edge:], field[:, :, -box_edge:]], axis=2)
    lower_y = jnp.where(side_pos == 0, place_plane(planes[2], tables[0]), shifted_low_y)
    upper_y = jnp.where(side_pos == box_edge - 1, place_plane(planes[3], tables[1]), shifted_high_y)
    shifted_down = jnp.concatenate([field[:, :, :1], field[:, :, :-1]], axis=2)
    shifted_up = jnp.concatenate([field[:, :, 1:], field[:, :, -1:]], axis=2)
    lower_z = jnp.where(depth_pos == 0, place_plane(planes[4], tables[2]), shifted_down)
    upper_z = jnp.where(depth_pos == box_edge - 1, place_plane(planes[5], tables[3]), shifted_up)
    return (lower_x, upper_x, lower_y, upper_y, lower_z, upper_z)


def faces_from(coeffs, package, layout):
    planes = planes_of(coeffs, package, layout, True)
    return tuple((0.5 * (coeffs + beside) for beside in box_neighbours(coeffs, planes)))


def coeff_faces(coeffs, layout):
    return faces_from(coeffs, pick(fetch_ghosts((coeffs,), layout), 0), layout)


def field_planes(field, layout):
    return planes_of(field, pick(fetch_ghosts((field,), layout), 0), layout, False)


def diagonal_of(faces, scale):
    summed = faces[0]
    for more in faces[1:]:
        summed = summed + more
    return scale * summed


def operate_box(field, planes, faces, scale):
    besides = box_neighbours(field, planes)
    summed = faces[0] * (field - besides[0])
    for number in range(1, 6):
        summed = summed + faces[number] * (field - besides[number])
    return scale * summed


def relax_box(field, planes, source, faces, diagonal, scale):
    return field + OMEGA * (source - operate_box(field, planes, faces, scale)) / diagonal


def restrict_box(field):
    slot_count, box_edge, area = field.shape
    half = box_edge // 2
    summed = field.reshape(slot_count, half, 2, half, 2, half, 2).sum(axis=(2, 4, 6)) * 0.125
    return summed.reshape(slot_count, half, half * half)


def prolong_box(field):
    slot_count, box_edge, area = field.shape
    grown = jnp.broadcast_to(
        field.reshape(slot_count, box_edge, 1, box_edge, 1, box_edge, 1),
        (slot_count, box_edge, 2, box_edge, 2, box_edge, 2),
    )
    return grown.reshape(slot_count, 2 * box_edge, 4 * box_edge * box_edge)


def body(source, conductance, initial, box_counts):
    device_rank = lax.axis_index("box")
    device_total = lax.axis_size("box")
    pencil_total = device_total // 2
    slot_count = source.shape[0]
    owner_layout = layout_of(box_counts, device_rank, slot_count, pencil_total)
    fine_source, fine_coeffs, start_field = (source, conductance, initial)
    first_round = fetch_ghosts((start_field, fine_coeffs), owner_layout)
    fine_faces = faces_from(fine_coeffs, pick(first_round, 1), owner_layout)
    fine_diag = diagonal_of(fine_faces, 1.0)
    solution = start_field
    planes = planes_of(start_field, pick(first_round, 0), owner_layout, False)
    for sweep_step in range(NU):
        if sweep_step > 0:
            planes = field_planes(solution, owner_layout)
        solution = relax_box(solution, planes, fine_source, fine_faces, fine_diag, 1.0)
    fine_resid = fine_source - operate_box(
        solution, field_planes(solution, owner_layout), fine_faces, 1.0
    )
    middle_source = restrict_box(fine_resid)
    middle_coeffs = restrict_box(fine_coeffs)
    middle_faces = coeff_faces(middle_coeffs, owner_layout)
    middle_diag = diagonal_of(middle_faces, 0.25)
    middle_error = OMEGA * middle_source / middle_diag
    middle_error = relax_box(
        middle_error,
        field_planes(middle_error, owner_layout),
        middle_source,
        middle_faces,
        middle_diag,
        0.25,
    )
    middle_resid = middle_source - operate_box(
        middle_error, field_planes(middle_error, owner_layout), middle_faces, 0.25
    )
    coarse_source = restrict_box(middle_resid)
    coarse_coeffs = restrict_box(middle_coeffs)
    coarse_faces = coeff_faces(coarse_coeffs, owner_layout)
    coarse_diag = diagonal_of(coarse_faces, 0.0625)
    coarse_error = OMEGA * coarse_source / coarse_diag
    for sweep_step in range(NU_COARSE - 1):
        coarse_error = relax_box(
            coarse_error,
            field_planes(coarse_error, owner_layout),
            coarse_source,
            coarse_faces,
            coarse_diag,
            0.0625,
        )
    middle_error = middle_error + prolong_box(coarse_error)
    for sweep_step in range(NU):
        middle_error = relax_box(
            middle_error,
            field_planes(middle_error, owner_layout),
            middle_source,
            middle_faces,
            middle_diag,
            0.25,
        )
    solution = solution + prolong_box(middle_error)
    for sweep_step in range(NU):
        solution = relax_box(
            solution, field_planes(solution, owner_layout), fine_source, fine_faces, fine_diag, 1.0
        )
    leftover = fine_source - operate_box(
        solution, field_planes(solution, owner_layout), fine_faces, 1.0
    )
    keep_mask = owner_layout[6][:, None, None]
    result = (jnp.where(keep_mask, solution, 0.0), jnp.where(keep_mask, leftover, 0.0))
    return result


def solution(mesh):
    return jax.shard_map(
        body,
        mesh=mesh,
        in_specs=(P("box", None, None), P("box", None, None), P("box", None, None), P()),
        out_specs=(P("box", None, None), P("box", None, None)),
        check_vma=False,
    )
```

profile of v0, /device:TPU:96, one launch (start us, length us, event | category | flops | bytes accessed | tf_op | source)
XLA Modules:
  0.0 1058.4 jit_solution(6124464848493537666)
XLA Ops:
  9.2 9.6 copy.420
  18.8 13.7 %reduce_sum.99 = f32[4,16,16,16]{0,3,2,1:T(8,128)} reduce(f32[4,16,2,16,2,16,2]{0,6,5,4,3,2,1:T(2,128)} %bitcast.540, f32[]{:T(128)} %constant.347.clone.1), dimensions={2,4,6}, to_apply=%region_7.12 | reduce | flops 114688 | bytes 589828 | tf_op jit(solution)/shard_map/reduce_sum | solution.py:214
  37.0 7.6 collective-permute-start.77
  97.1 5.2 collective-permute-start.72
  113.0 7.0 collective-permute-start.83
  136.5 6.1 collective-permute-start.47
  142.6 4.4 collective-permute-start.46
  160.1 4.6 collective-permute-start.41
  164.7 4.2 collective-permute-start.40
  174.0 4.8 collective-permute-start
  200.9 5.0 collective-permute-start.5
  206.0 4.4 collective-permute-start.4
  238.9 7.4 collective-permute-start.17
  277.8 4.6 collective-permute-start.12
  282.4 4.3 collective-permute-start.23
  343.7 6.3 collective-permute-start.29
  381.5 6.7 collective-permute-start.24
  388.2 4.8 collective-permute-start.35
  449.6 9.6 copy.418
  459.3 13.7 %reduce_sum.98 = f32[4,16,16,16]{0,3,2,1:T(8,128)} reduce(f32[4,16,2,16,2,16,2]{0,6,5,4,3,2,1:T(2,128)} %bitcast.538, f32[]{:T(128)} %constant.347.clone.1), dimensions={2,4,6}, to_apply=%region_6.11 | reduce | flops 114688 | bytes 589828 | tf_op jit(solution)/shard_map/reduce_sum | solution.py:214
  481.3 5.7 collective-permute-start.53
  502.4 6.4 collective-permute-start.48
  508.8 4.8 collective-permute-start.59
  532.1 4.0 collective-permute-done.54
  552.5 5.5 collective-permute-start.60
  560.7 4.4 collective-permute-start.70
  569.9 3.9 collective-permute-start.67
  579.7 4.1 collective-permute-done.66
  597.9 8.2 collective-permute-start.89
  606.0 4.2 collective-permute-start.88
  618.2 4.3 collective-permute-start.93
  625.4 3.9 collective-permute-start.91
  635.1 4.2 collective-permute-done.90
  647.6 3.9 collective-permute-start.96
  651.6 6.4 collective-permute-start.101
  658.0 4.0 collective-permute-start.100
  671.0 4.3 collective-permute-start.105
  678.2 3.9 collective-permute-start.103
  687.9 4.2 collective-permute-done.102
  697.9 4.1 collective-permute-start.108
  702.1 6.2 collective-permute-start.113
  708.2 4.0 collective-permute-start.112
  720.0 4.3 collective-permute-start.117
  727.2 3.9 collective-permute-start.115
  736.9 4.2 collective-permute-done.114
  761.9 5.5 collective-permute-start.120
  779.3 3.9 collective-permute-start.127
  789.1 4.2 collective-permute-done.126
  809.6 5.5 collective-permute-start.132
  827.0 3.9 collective-permute-start.139
  836.8 4.2 collective-permute-done.138
  845.0 10.4 broadcast_in_dim.1227
  855.4 10.0 copy.430
  884.8 5.5 collective-permute-start.144
  902.9 3.9 collective-permute-start.151
  912.9 4.8 collective-permute-done.150
  946.0 5.5 collective-permute-start.156
  965.9 3.9 collective-permute-start.163
  977.7 4.0 collective-permute-done.162
  1012.2 5.7 collective-permute-start.168
  1017.9 4.5 collective-permute-start.179
  1022.5 4.0 collective-permute-start.178
  1033.2 3.9 collective-permute-start.175
  1045.0 4.0 collective-permute-done.174
  (1596 shorter events, 699.0 us)
Async XLA Ops:
  2.9 183.8 %collective-permute-start.2 = (f32[2,4,1024]{2,0,1:T(2,128)}, f32[2,4,1024]{2,0,1:T(2,128)}, u32[]{:S(2)}, u32[]{:S(2)}) collective-permute-start(f32[2,4,1024]{2,0,1:T(2,128)} %pad_maximum_fusion.16), channel_id=1, source_target_pairs={{0,9},{1,10},{2,11},{3,12},{4,13},{5,14},{6,15},{7,16},{8,17},{9,1... | collective-permute-start | bytes 98312 | tf_op jit(solution)/shard_map/ppermute | solution.py:17
  5.8 184.6 %collective-permute-start.1 = (f32[2,4,1024]{2,0,1:T(2,128)}, f32[2,4,1024]{2,0,1:T(2,128)}, u32[]{:S(2)}, u32[]{:S(2)}) collective-permute-start(f32[2,4,1024]{2,0,1:T(2,128)} %pad_maximum_fusion.16), channel_id=1, source_target_pairs={{0,8},{1,9},{2,10},{3,11},{4,12},{5,13},{6,14},{7,15},{8,16},{9,17... | collective-permute-start | bytes 98312 | tf_op jit(solution)/shard_map/ppermute | solution.py:17
  37.0 53.9 %collective-permute-start.77 = (f32[1,4,64]{2,1,0:T(4,128)}, f32[1,4,64]{2,1,0:T(4,128)}, u32[]{:S(2)}, u32[]{:S(2)}) collective-permute-start(f32[1,4,64]{2,1,0:T(4,128)} %bitcast.74), channel_id=1, source_target_pairs={{9,0},{10,1},{11,2},{12,3},{13,4},{14,5},{15,6},{16,7},{17,8},{18,... | collective-permute-start | bytes 3080 | tf_op jit(solution)/shard_map/ppermute | solution.py:17
  44.6 49.1 %collective-permute-start.76 = (f32[1,4,64]{2,1,0:T(4,128)}, f32[1,4,64]{2,1,0:T(4,128)}, u32[]{:S(2)}, u32[]{:S(2)}) collective-permute-start(f32[1,4,64]{2,1,0:T(4,128)} %bitcast.74), channel_id=1, source_target_pairs={{8,0},{9,1},{10,2},{11,3},{12,4},{13,5},{14,6},{15,7},{16,8},{17,9... | collective-permute-start | bytes 3080 | tf_op jit(solution)/shard_map/ppermute | solution.py:17
  47.0 50.0 %collective-permute-start.75 = (f32[1,4,64]{2,1,0:T(4,128)}, f32[1,4,64]{2,1,0:T(4,128)}, u32[]{:S(2)}, u32[]{:S(2)}) collective-permute-start(f32[1,4,64]{2,1,0:T(4,128)} %bitcast.74), channel_id=1, source_target_pairs={{7,0},{8,1},{9,2},{10,3},{11,4},{12,5},{13,6},{14,7},{15,8},{16,9}... | collective-permute-start | bytes 3080 | tf_op jit(solution)/shard_map/ppermute | solution.py:17
  178.9 20.0 %collective-permute-start.11 = (f32[2,5,1024]{2,0,1:T(2,128)S(1)}, f32[2,5,1024]{2,0,1:T(2,128)S(1)}, u32[]{:S(2)}, u32[]{:S(2)}) collective-permute-start(f32[2,5,1024]{2,0,1:T(2,128)S(1)} %fusion.412), channel_id=1, source_target_pairs={{3,0},{4,1},{5,2},{6,3},{7,4},{8,5},{9,6},{10,7},{11,8},{12,9},{13... | collective-permute-start | bytes 122888 | tf_op jit(solution)/shard_map/ppermute | solution.py:17
  190.4 21.7 %collective-permute-start.8 = (f32[2,5,1024]{2,0,1:T(2,128)S(1)}, f32[2,5,1024]{2,0,1:T(2,128)S(1)}, u32[]{:S(2)}, u32[]{:S(2)}) collective-permute-start(f32[2,5,1024]{2,0,1:T(2,128)S(1)} %pad_maximum_fusion.15), channel_id=1, source_target_pairs={{0,3},{1,4},{2,5},{3,6},{4,7},{5,8},{6,9},{7,10},{8,11},{9,12},{10... | collective-permute-start | bytes 122888 | tf_op jit(solution)/shard_map/ppermute | solution.py:17
  192.3 21.7 %collective-permute-start.7 = (f32[2,5,1024]{2,0,1:T(2,128)S(1)}, f32[2,5,1024]{2,0,1:T(2,128)S(1)}, u32[]{:S(2)}, u32[]{:S(2)}) collective-permute-start(f32[2,5,1024]{2,0,1:T(2,128)S(1)} %pad_maximum_fusion.15), channel_id=1, source_target_pairs={{0,2},{1,3},{2,4},{3,5},{4,6},{5,7},{6,8},{7,9},{8,10},{9,11},{10,... | collective-permute-start | bytes 122888 | tf_op jit(solution)/shard_map/ppermute | solution.py:17
  200.9 30.1 %collective-permute-start.5 = (f32[2,4,1024]{2,0,1:T(2,128)}, f32[2,4,1024]{2,0,1:T(2,128)}, u32[]{:S(2)}, u32[]{:S(2)}) collective-permute-start(f32[2,4,1024]{2,0,1:T(2,128)} %pad_maximum_fusion.17), channel_id=1, source_target_pairs={{9,0},{10,1},{11,2},{12,3},{13,4},{14,5},{15,6},{16,7},{17,8},{18,... | collective-permute-start | bytes 98312 | tf_op jit(solution)/shard_map/ppermute | solution.py:17
  206.0 25.0 %collective-permute-start.4 = (f32[2,4,1024]{2,0,1:T(2,128)}, f32[2,4,1024]{2,0,1:T(2,128)}, u32[]{:S(2)}, u32[]{:S(2)}) collective-permute-start(f32[2,4,1024]{2,0,1:T(2,128)} %pad_maximum_fusion.17), channel_id=1, source_target_pairs={{8,0},{9,1},{10,2},{11,3},{12,4},{13,5},{14,6},{15,7},{16,8},{17,9... | collective-permute-start | bytes 98312 | tf_op jit(solution)/shard_map/ppermute | solution.py:17
  238.9 38.9 %collective-permute-start.17 = (f32[1,4,1024]{2,0,1:T(1,128)}, f32[1,4,1024]{2,0,1:T(1,128)}, u32[]{:S(2)}, u32[]{:S(2)}) collective-permute-start(f32[1,4,1024]{2,0,1:T(1,128)} %get-tuple-element.99), channel_id=1, source_target_pairs={{9,0},{10,1},{11,2},{12,3},{13,4},{14,5},{15,6},{16,7},{17,8},{18,... | collective-permute-start | bytes 49160 | tf_op jit(solution)/shard_map/ppermute | solution.py:17
  246.4 36.0 %collective-permute-start.16 = (f32[1,4,1024]{2,0,1:T(1,128)}, f32[1,4,1024]{2,0,1:T(1,128)}, u32[]{:S(2)}, u32[]{:S(2)}) collective-permute-start(f32[1,4,1024]{2,0,1:T(1,128)} %get-tuple-element.99), channel_id=1, source_target_pairs={{8,0},{9,1},{10,2},{11,3},{12,4},{13,5},{14,6},{15,7},{16,8},{17,9... | collective-permute-start | bytes 49160 | tf_op jit(solution)/shard_map/ppermute | solution.py:17
  248.9 37.8 %collective-permute-start.15 = (f32[1,4,1024]{2,0,1:T(1,128)}, f32[1,4,1024]{2,0,1:T(1,128)}, u32[]{:S(2)}, u32[]{:S(2)}) collective-permute-start(f32[1,4,1024]{2,0,1:T(1,128)} %get-tuple-element.99), channel_id=1, source_target_pairs={{7,0},{8,1},{9,2},{10,3},{11,4},{12,5},{13,6},{14,7},{15,8},{16,9}... | collective-permute-start | bytes 49160 | tf_op jit(solution)/shard_map/ppermute | solution.py:17
  250.8 44.2 %collective-permute-start.14 = (f32[1,4,1024]{2,0,1:T(1,128)}, f32[1,4,1024]{2,0,1:T(1,128)}, u32[]{:S(2)}, u32[]{:S(2)}) collective-permute-start(f32[1,4,1024]{2,0,1:T(1,128)} %get-tuple-element.100), channel_id=1, source_target_pairs={{0,9},{1,10},{2,11},{3,12},{4,13},{5,14},{6,15},{7,16},{8,17},{9,1... | collective-permute-start | bytes 49160 | tf_op jit(solution)/shard_map/ppermute | solution.py:17
  252.8 44.2 %collective-permute-start.13 = (f32[1,4,1024]{2,0,1:T(1,128)}, f32[1,4,1024]{2,0,1:T(1,128)}, u32[]{:S(2)}, u32[]{:S(2)}) collective-permute-start(f32[1,4,1024]{2,0,1:T(1,128)} %get-tuple-element.100), channel_id=1, source_target_pairs={{0,8},{1,9},{2,10},{3,11},{4,12},{5,13},{6,14},{7,15},{8,16},{9,17... | collective-permute-start | bytes 49160 | tf_op jit(solution)/shard_map/ppermute | solution.py:17
  277.8 22.6 %collective-permute-start.12 = (f32[1,4,1024]{2,0,1:T(1,128)}, f32[1,4,1024]{2,0,1:T(1,128)}, u32[]{:S(2)}, u32[]{:S(2)}) collective-permute-start(f32[1,4,1024]{2,0,1:T(1,128)} %get-tuple-element.100), channel_id=1, source_target_pairs={{0,7},{1,8},{2,9},{3,10},{4,11},{5,12},{6,13},{7,14},{8,15},{9,16}... | collective-permute-start | bytes 49160 | tf_op jit(solution)/shard_map/ppermute | solution.py:17
  282.4 26.1 %collective-permute-start.23 = (f32[1,5,1024]{2,1,0:T(8,128)}, f32[1,5,1024]{2,1,0:T(8,128)}, u32[]{:S(2)}, u32[]{:S(2)}) collective-permute-start(f32[1,5,1024]{2,1,0:T(8,128)} %pad_maximum_fusion.19), channel_id=1, source_target_pairs={{3,0},{4,1},{5,2},{6,3},{7,4},{8,5},{9,6},{10,7},{11,8},{12,9},{13... | collective-permute-start | bytes 61448 | tf_op jit(solution)/shard_map/ppermute | solution.py:17
  286.7 24.6 %collective-permute-start.22 = (f32[1,5,1024]{2,1,0:T(8,128)}, f32[1,5,1024]{2,1,0:T(8,128)}, u32[]{:S(2)}, u32[]{:S(2)}) collective-permute-start(f32[1,5,1024]{2,1,0:T(8,128)} %pad_maximum_fusion.19), channel_id=1, source_target_pairs={{2,0},{3,1},{4,2},{5,3},{6,4},{7,5},{8,6},{9,7},{10,8},{11,9},{12,... | collective-permute-start | bytes 61448 | tf_op jit(solution)/shard_map/ppermute | solution.py:17
  297.0 26.7 %collective-permute-start.20 = (f32[1,5,1024]{2,1,0:T(8,128)}, f32[1,5,1024]{2,1,0:T(8,128)}, u32[]{:S(2)}, u32[]{:S(2)}) collective-permute-start(f32[1,5,1024]{2,1,0:T(8,128)} %pad_maximum_fusion.18), channel_id=1, source_target_pairs={{0,3},{1,4},{2,5},{3,6},{4,7},{5,8},{6,9},{7,10},{8,11},{9,12},{10... | collective-permute-start | bytes 61448 | tf_op jit(solution)/shard_map/ppermute | solution.py:17
  300.4 23.4 %collective-permute-start.19 = (f32[1,5,1024]{2,1,0:T(8,128)}, f32[1,5,1024]{2,1,0:T(8,128)}, u32[]{:S(2)}, u32[]{:S(2)}) collective-permute-start(f32[1,5,1024]{2,1,0:T(8,128)} %pad_maximum_fusion.18), channel_id=1, source_target_pairs={{0,2},{1,3},{2,4},{3,5},{4,6},{5,7},{6,8},{7,9},{8,10},{9,11},{10,... | collective-permute-start | bytes 61448 | tf_op jit(solution)/shard_map/ppermute | solution.py:17
  343.7 37.8 %collective-permute-start.29 = (f32[1,4,1024]{2,0,1:T(1,128)}, f32[1,4,1024]{2,0,1:T(1,128)}, u32[]{:S(2)}, u32[]{:S(2)}) collective-permute-start(f32[1,4,1024]{2,0,1:T(1,128)} %get-tuple-element.87), channel_id=1, source_target_pairs={{9,0},{10,1},{11,2},{12,3},{13,4},{14,5},{15,6},{16,7},{17,8},{18,... | collective-permute-start | bytes 49160 | tf_op jit(solution)/shard_map/ppermute | solution.py:17
  350.0 38.2 %collective-permute-start.28 = (f32[1,4,1024]{2,0,1:T(1,128)}, f32[1,4,1024]{2,0,1:T(1,128)}, u32[]{:S(2)}, u32[]{:S(2)}) collective-permute-start(f32[1,4,1024]{2,0,1:T(1,128)} %get-tuple-element.87), channel_id=1, source_target_pairs={{8,0},{9,1},{10,2},{11,3},{12,4},{13,5},{14,6},{15,7},{16,8},{17,9... | collective-permute-start | bytes 49160 | tf_op jit(solution)/shard_map/ppermute | solution.py:17
  353.1 39.9 %collective-permute-start.27 = (f32[1,4,1024]{2,0,1:T(1,128)}, f32[1,4,1024]{2,0,1:T(1,128)}, u32[]{:S(2)}, u32[]{:S(2)}) collective-permute-start(f32[1,4,1024]{2,0,1:T(1,128)} %get-tuple-element.87), channel_id=1, source_target_pairs={{7,0},{8,1},{9,2},{10,3},{11,4},{12,5},{13,6},{14,7},{15,8},{16,9}... | collective-permute-start | bytes 49160 | tf_op jit(solution)/shard_map/ppermute | solution.py:17
  355.0 46.1 %collective-permute-start.26 = (f32[1,4,1024]{2,0,1:T(1,128)}, f32[1,4,1024]{2,0,1:T(1,128)}, u32[]{:S(2)}, u32[]{:S(2)}) collective-permute-start(f32[1,4,1024]{2,0,1:T(1,128)} %get-tuple-element.88), channel_id=1, source_target_pairs={{0,9},{1,10},{2,11},{3,12},{4,13},{5,14},{6,15},{7,16},{8,17},{9,1... | collective-permute-start | bytes 49160 | tf_op jit(solution)/shard_map/ppermute | solution.py:17
  357.0 46.1 %collective-permute-start.25 = (f32[1,4,1024]{2,0,1:T(1,128)}, f32[1,4,1024]{2,0,1:T(1,128)}, u32[]{:S(2)}, u32[]{:S(2)}) collective-permute-start(f32[1,4,1024]{2,0,1:T(1,128)} %get-tuple-element.88), channel_id=1, source_target_pairs={{0,8},{1,9},{2,10},{3,11},{4,12},{5,13},{6,14},{7,15},{8,16},{9,17... | collective-permute-start | bytes 49160 | tf_op jit(solution)/shard_map/ppermute | solution.py:17
  381.5 24.4 %collective-permute-start.24 = (f32[1,4,1024]{2,0,1:T(1,128)}, f32[1,4,1024]{2,0,1:T(1,128)}, u32[]{:S(2)}, u32[]{:S(2)}) collective-permute-start(f32[1,4,1024]{2,0,1:T(1,128)} %get-tuple-element.88), channel_id=1, source_target_pairs={{0,7},{1,8},{2,9},{3,10},{4,11},{5,12},{6,13},{7,14},{8,15},{9,16}... | collective-permute-start | bytes 49160 | tf_op jit(solution)/shard_map/ppermute | solution.py:17
  388.2 26.3 %collective-permute-start.35 = (f32[1,5,1024]{2,1,0:T(8,128)}, f32[1,5,1024]{2,1,0:T(8,128)}, u32[]{:S(2)}, u32[]{:S(2)}) collective-permute-start(f32[1,5,1024]{2,1,0:T(8,128)} %pad_maximum_fusion.21), channel_id=1, source_target_pairs={{3,0},{4,1},{5,2},{6,3},{7,4},{8,5},{9,6},{10,7},{11,8},{12,9},{13... | collective-permute-start | bytes 61448 | tf_op jit(solution)/shard_map/ppermute | solution.py:17
  393.0 23.5 %collective-permute-start.34 = (f32[1,5,1024]{2,1,0:T(8,128)}, f32[1,5,1024]{2,1,0:T(8,128)}, u32[]{:S(2)}, u32[]{:S(2)}) collective-permute-start(f32[1,5,1024]{2,1,0:T(8,128)} %pad_maximum_fusion.21), channel_id=1, source_target_pairs={{2,0},{3,1},{4,2},{5,3},{6,4},{7,5},{8,6},{9,7},{10,8},{11,9},{12,... | collective-permute-start | bytes 61448 | tf_op jit(solution)/shard_map/ppermute | solution.py:17
  403.1 25.8 %collective-permute-start.32 = (f32[1,5,1024]{2,1,0:T(8,128)}, f32[1,5,1024]{2,1,0:T(8,128)}, u32[]{:S(2)}, u32[]{:S(2)}) collective-permute-start(f32[1,5,1024]{2,1,0:T(8,128)} %pad_maximum_fusion.20), channel_id=1, source_target_pairs={{0,3},{1,4},{2,5},{3,6},{4,7},{5,8},{6,9},{7,10},{8,11},{9,12},{10... | collective-permute-start | bytes 61448 | tf_op jit(solution)/shard_map/ppermute | solution.py:17
  405.8 23.0 %collective-permute-start.31 = (f32[1,5,1024]{2,1,0:T(8,128)}, f32[1,5,1024]{2,1,0:T(8,128)}, u32[]{:S(2)}, u32[]{:S(2)}) collective-permute-start(f32[1,5,1024]{2,1,0:T(8,128)} %pad_maximum_fusion.20), channel_id=1, source_target_pairs={{0,2},{1,3},{2,4},{3,5},{4,6},{5,7},{6,8},{7,9},{8,10},{9,11},{10,... | collective-permute-start | bytes 61448 | tf_op jit(solution)/shard_map/ppermute | solution.py:17
  481.3 21.2 %collective-permute-start.53 = (f32[1,4,256]{2,0,1:T(1,128)S(1)}, f32[1,4,256]{2,0,1:T(1,128)S(1)}, u32[]{:S(2)}, u32[]{:S(2)}) collective-permute-start(f32[1,4,256]{2,0,1:T(1,128)S(1)} %get-tuple-element.179), channel_id=1, source_target_pairs={{9,0},{10,1},{11,2},{12,3},{13,4},{14,5},{15,6},{16,7},{17,8},{18,... | collective-permute-start | bytes 12296 | tf_op jit(solution)/shard_map/ppermute | solution.py:17
  487.0 21.8 %collective-permute-start.52 = (f32[1,4,256]{2,0,1:T(1,128)S(1)}, f32[1,4,256]{2,0,1:T(1,128)S(1)}, u32[]{:S(2)}, u32[]{:S(2)}) collective-permute-start(f32[1,4,256]{2,0,1:T(1,128)S(1)} %get-tuple-element.179), channel_id=1, source_target_pairs={{8,0},{9,1},{10,2},{11,3},{12,4},{13,5},{14,6},{15,7},{16,8},{17,9... | collective-permute-start | bytes 12296 | tf_op jit(solution)/shard_map/ppermute | solution.py:17
  490.1 23.5 %collective-permute-start.51 = (f32[1,4,256]{2,0,1:T(1,128)S(1)}, f32[1,4,256]{2,0,1:T(1,128)S(1)}, u32[]{:S(2)}, u32[]{:S(2)}) collective-permute-start(f32[1,4,256]{2,0,1:T(1,128)S(1)} %get-tuple-element.179), channel_id=1, source_target_pairs={{7,0},{8,1},{9,2},{10,3},{11,4},{12,5},{13,6},{14,7},{15,8},{16,9}... | collective-permute-start | bytes 12296 | tf_op jit(solution)/shard_map/ppermute | solution.py:17
  492.0 26.2 %collective-permute-start.50 = (f32[1,4,256]{2,0,1:T(1,128)S(1)}, f32[1,4,256]{2,0,1:T(1,128)S(1)}, u32[]{:S(2)}, u32[]{:S(2)}) collective-permute-start(f32[1,4,256]{2,0,1:T(1,128)S(1)} %get-tuple-element.180), channel_id=1, source_target_pairs={{0,9},{1,10},{2,11},{3,12},{4,13},{5,14},{6,15},{7,16},{8,17},{9,1... | collective-permute-start | bytes 12296 | tf_op jit(solution)/shard_map/ppermute | solution.py:17
  494.3 25.8 %collective-permute-start.49 = (f32[1,4,256]{2,0,1:T(1,128)S(1)}, f32[1,4,256]{2,0,1:T(1,128)S(1)}, u32[]{:S(2)}, u32[]{:S(2)}) collective-permute-start(f32[1,4,256]{2,0,1:T(1,128)S(1)} %get-tuple-element.180), channel_id=1, source_target_pairs={{0,8},{1,9},{2,10},{3,11},{4,12},{5,13},{6,14},{7,15},{8,16},{9,17... | collective-permute-start | bytes 12296 | tf_op jit(solution)/shard_map/ppermute | solution.py:17
  502.4 19.9 %collective-permute-start.48 = (f32[1,4,256]{2,0,1:T(1,128)S(1)}, f32[1,4,256]{2,0,1:T(1,128)S(1)}, u32[]{:S(2)}, u32[]{:S(2)}) collective-permute-start(f32[1,4,256]{2,0,1:T(1,128)S(1)} %get-tuple-element.180), channel_id=1, source_target_pairs={{0,7},{1,8},{2,9},{3,10},{4,11},{5,12},{6,13},{7,14},{8,15},{9,16}... | collective-permute-start | bytes 12296 | tf_op jit(solution)/shard_map/ppermute | solution.py:17
  543.9 22.0 %collective-permute-start.62 = (f32[1,4,256]{2,0,1:T(1,128)S(1)}, f32[1,4,256]{2,0,1:T(1,128)S(1)}, u32[]{:S(2)}, u32[]{:S(2)}) collective-permute-start(f32[1,4,256]{2,0,1:T(1,128)S(1)} %get-tuple-element.168), channel_id=1, source_target_pairs={{0,9},{1,10},{2,11},{3,12},{4,13},{5,14},{6,15},{7,16},{8,17},{9,1... | collective-permute-start | bytes 12296 | tf_op jit(solution)/shard_map/ppermute | solution.py:17
  547.6 20.3 %collective-permute-start.61 = (f32[1,4,256]{2,0,1:T(1,128)S(1)}, f32[1,4,256]{2,0,1:T(1,128)S(1)}, u32[]{:S(2)}, u32[]{:S(2)}) collective-permute-start(f32[1,4,256]{2,0,1:T(1,128)S(1)} %get-tuple-element.168), channel_id=1, source_target_pairs={{0,8},{1,9},{2,10},{3,11},{4,12},{5,13},{6,14},{7,15},{8,16},{9,17... | collective-permute-start | bytes 12296 | tf_op jit(solution)/shard_map/ppermute | solution.py:17
  594.0 19.4 %collective-permute-start.85 = (f32[1,4,64]{2,1,0:T(4,128)S(1)}, f32[1,4,64]{2,1,0:T(4,128)S(1)}, u32[]{:S(2)}, u32[]{:S(2)}) collective-permute-start(f32[1,4,64]{2,1,0:T(4,128)S(1)} %bitcast.601), channel_id=1, source_target_pairs={{0,8},{1,9},{2,10},{3,11},{4,12},{5,13},{6,14},{7,15},{8,16},{9,17... | collective-permute-start | bytes 3080 | tf_op jit(solution)/shard_map/ppermute | solution.py:17
  595.9 19.4 %collective-permute-start.84 = (f32[1,4,64]{2,1,0:T(4,128)S(1)}, f32[1,4,64]{2,1,0:T(4,128)S(1)}, u32[]{:S(2)}, u32[]{:S(2)}) collective-permute-start(f32[1,4,64]{2,1,0:T(4,128)S(1)} %bitcast.602), channel_id=1, source_target_pairs={{0,7},{1,8},{2,9},{3,10},{4,11},{5,12},{6,13},{7,14},{8,15},{9,16}... | collective-permute-start | bytes 3080 | tf_op jit(solution)/shard_map/ppermute | solution.py:17
  597.9 20.3 %collective-permute-start.89 = (f32[1,4,64]{2,1,0:T(4,128)S(1)}, f32[1,4,64]{2,1,0:T(4,128)S(1)}, u32[]{:S(2)}, u32[]{:S(2)}) collective-permute-start(f32[1,4,64]{2,1,0:T(4,128)S(1)} %bitcast.591), channel_id=1, source_target_pairs={{9,0},{10,1},{11,2},{12,3},{13,4},{14,5},{15,6},{16,7},{17,8},{18,... | collective-permute-start | bytes 3080 | tf_op jit(solution)/shard_map/ppermute | solution.py:17
  643.8 20.5 %collective-permute-start.98 = (f32[1,4,64]{2,1,0:T(4,128)S(1)}, f32[1,4,64]{2,1,0:T(4,128)S(1)}, u32[]{:S(2)}, u32[]{:S(2)}) collective-permute-start(f32[1,4,64]{2,1,0:T(4,128)S(1)} %bitcast.603), channel_id=1, source_target_pairs={{0,9},{1,10},{2,11},{3,12},{4,13},{5,14},{6,15},{7,16},{8,17},{9,1... | collective-permute-start | bytes 3080 | tf_op jit(solution)/shard_map/ppermute | solution.py:17
  645.7 20.5 %collective-permute-start.97 = (f32[1,4,64]{2,1,0:T(4,128)S(1)}, f32[1,4,64]{2,1,0:T(4,128)S(1)}, u32[]{:S(2)}, u32[]{:S(2)}) collective-permute-start(f32[1,4,64]{2,1,0:T(4,128)S(1)} %bitcast.604), channel_id=1, source_target_pairs={{0,8},{1,9},{2,10},{3,11},{4,12},{5,13},{6,14},{7,15},{8,16},{9,17... | collective-permute-start | bytes 3080 | tf_op jit(solution)/shard_map/ppermute | solution.py:17
  647.6 20.5 %collective-permute-start.96 = (f32[1,4,64]{2,1,0:T(4,128)S(1)}, f32[1,4,64]{2,1,0:T(4,128)S(1)}, u32[]{:S(2)}, u32[]{:S(2)}) collective-permute-start(f32[1,4,64]{2,1,0:T(4,128)S(1)} %bitcast.605), channel_id=1, source_target_pairs={{0,7},{1,8},{2,9},{3,10},{4,11},{5,12},{6,13},{7,14},{8,15},{9,16}... | collective-permute-start | bytes 3080 | tf_op jit(solution)/shard_map/ppermute | solution.py:17
  757.0 19.4 %collective-permute-start.121 = (f32[1,4,256]{2,0,1:T(1,128)S(1)}, f32[1,4,256]{2,0,1:T(1,128)S(1)}, u32[]{:S(2)}, u32[]{:S(2)}) collective-permute-start(f32[1,4,256]{2,0,1:T(1,128)S(1)} %get-tuple-element.156), channel_id=1, source_target_pairs={{0,8},{1,9},{2,10},{3,11},{4,12},{5,13},{6,14},{7,15},{8,16},{9,17... | collective-permute-start | bytes 12296 | tf_op jit(solution)/shard_map/ppermute | solution.py:17
  801.1 20.6 %collective-permute-start.134 = (f32[1,4,256]{2,0,1:T(1,128)S(1)}, f32[1,4,256]{2,0,1:T(1,128)S(1)}, u32[]{:S(2)}, u32[]{:S(2)}) collective-permute-start(f32[1,4,256]{2,0,1:T(1,128)S(1)} %get-tuple-element.144), channel_id=1, source_target_pairs={{0,9},{1,10},{2,11},{3,12},{4,13},{5,14},{6,15},{7,16},{8,17},{9,1... | collective-permute-start | bytes 12296 | tf_op jit(solution)/shard_map/ppermute | solution.py:17
  867.4 22.8 %collective-permute-start.148 = (f32[1,4,1024]{2,0,1:T(1,128)S(1)}, f32[1,4,1024]{2,0,1:T(1,128)S(1)}, u32[]{:S(2)}, u32[]{:S(2)}) collective-permute-start(f32[1,4,1024]{2,0,1:T(1,128)S(1)} %get-tuple-element.75), channel_id=1, source_target_pairs={{8,0},{9,1},{10,2},{11,3},{12,4},{13,5},{14,6},{15,7},{16,8},{17,9... | collective-permute-start | bytes 49160 | tf_op jit(solution)/shard_map/ppermute | solution.py:17
  869.4 23.7 %collective-permute-start.147 = (f32[1,4,1024]{2,0,1:T(1,128)S(1)}, f32[1,4,1024]{2,0,1:T(1,128)S(1)}, u32[]{:S(2)}, u32[]{:S(2)}) collective-permute-start(f32[1,4,1024]{2,0,1:T(1,128)S(1)} %get-tuple-element.75), channel_id=1, source_target_pairs={{7,0},{8,1},{9,2},{10,3},{11,4},{12,5},{13,6},{14,7},{15,8},{16,9}... | collective-permute-start | bytes 49160 | tf_op jit(solution)/shard_map/ppermute | solution.py:17
  871.3 26.5 %collective-permute-start.146 = (f32[1,4,1024]{2,0,1:T(1,128)S(1)}, f32[1,4,1024]{2,0,1:T(1,128)S(1)}, u32[]{:S(2)}, u32[]{:S(2)}) collective-permute-start(f32[1,4,1024]{2,0,1:T(1,128)S(1)} %get-tuple-element.76), channel_id=1, source_target_pairs={{0,9},{1,10},{2,11},{3,12},{4,13},{5,14},{6,15},{7,16},{8,17},{9,1... | collective-permute-start | bytes 49160 | tf_op jit(solution)/shard_map/ppermute | solution.py:17
  874.9 25.0 %collective-permute-start.145 = (f32[1,4,1024]{2,0,1:T(1,128)S(1)}, f32[1,4,1024]{2,0,1:T(1,128)S(1)}, u32[]{:S(2)}, u32[]{:S(2)}) collective-permute-start(f32[1,4,1024]{2,0,1:T(1,128)S(1)} %get-tuple-element.76), channel_id=1, source_target_pairs={{0,8},{1,9},{2,10},{3,11},{4,12},{5,13},{6,14},{7,15},{8,16},{9,17... | collective-permute-start | bytes 49160 | tf_op jit(solution)/shard_map/ppermute | solution.py:17
  925.0 21.0 %collective-permute-start.161 = (f32[1,4,1024]{2,0,1:T(1,128)}, f32[1,4,1024]{2,0,1:T(1,128)}, u32[]{:S(2)}, u32[]{:S(2)}) collective-permute-start(f32[1,4,1024]{2,0,1:T(1,128)} %get-tuple-element.63), channel_id=1, source_target_pairs={{9,0},{10,1},{11,2},{12,3},{13,4},{14,5},{15,6},{16,7},{17,8},{18,... | collective-permute-start | bytes 49160 | tf_op jit(solution)/shard_map/ppermute | solution.py:17
  927.0 24.5 %collective-permute-start.160 = (f32[1,4,1024]{2,0,1:T(1,128)}, f32[1,4,1024]{2,0,1:T(1,128)}, u32[]{:S(2)}, u32[]{:S(2)}) collective-permute-start(f32[1,4,1024]{2,0,1:T(1,128)} %get-tuple-element.63), channel_id=1, source_target_pairs={{8,0},{9,1},{10,2},{11,3},{12,4},{13,5},{14,6},{15,7},{16,8},{17,9... | collective-permute-start | bytes 49160 | tf_op jit(solution)/shard_map/ppermute | solution.py:17
  928.9 26.2 %collective-permute-start.159 = (f32[1,4,1024]{2,0,1:T(1,128)}, f32[1,4,1024]{2,0,1:T(1,128)}, u32[]{:S(2)}, u32[]{:S(2)}) collective-permute-start(f32[1,4,1024]{2,0,1:T(1,128)} %get-tuple-element.63), channel_id=1, source_target_pairs={{7,0},{8,1},{9,2},{10,3},{11,4},{12,5},{13,6},{14,7},{15,8},{16,9}... | collective-permute-start | bytes 49160 | tf_op jit(solution)/shard_map/ppermute | solution.py:17
  930.8 30.6 %collective-permute-start.158 = (f32[1,4,1024]{2,0,1:T(1,128)}, f32[1,4,1024]{2,0,1:T(1,128)}, u32[]{:S(2)}, u32[]{:S(2)}) collective-permute-start(f32[1,4,1024]{2,0,1:T(1,128)} %get-tuple-element.64), channel_id=1, source_target_pairs={{0,9},{1,10},{2,11},{3,12},{4,13},{5,14},{6,15},{7,16},{8,17},{9,1... | collective-permute-start | bytes 49160 | tf_op jit(solution)/shard_map/ppermute | solution.py:17
  934.5 28.9 %collective-permute-start.157 = (f32[1,4,1024]{2,0,1:T(1,128)}, f32[1,4,1024]{2,0,1:T(1,128)}, u32[]{:S(2)}, u32[]{:S(2)}) collective-permute-start(f32[1,4,1024]{2,0,1:T(1,128)} %get-tuple-element.64), channel_id=1, source_target_pairs={{0,8},{1,9},{2,10},{3,11},{4,12},{5,13},{6,14},{7,15},{8,16},{9,17... | collective-permute-start | bytes 49160 | tf_op jit(solution)/shard_map/ppermute | solution.py:17
  946.0 19.9 %collective-permute-start.156 = (f32[1,4,1024]{2,0,1:T(1,128)}, f32[1,4,1024]{2,0,1:T(1,128)}, u32[]{:S(2)}, u32[]{:S(2)}) collective-permute-start(f32[1,4,1024]{2,0,1:T(1,128)} %get-tuple-element.64), channel_id=1, source_target_pairs={{0,7},{1,8},{2,9},{3,10},{4,11},{5,12},{6,13},{7,14},{8,15},{9,16}... | collective-permute-start | bytes 49160 | tf_op jit(solution)/shard_map/ppermute | solution.py:17
  951.5 20.5 %collective-permute-start.167 = (f32[1,5,1024]{2,1,0:T(8,128)}, f32[1,5,1024]{2,1,0:T(8,128)S(1)}, u32[]{:S(2)}, u32[]{:S(2)}) collective-permute-start(f32[1,5,1024]{2,1,0:T(8,128)} %pad_maximum_fusion.25), channel_id=1, source_target_pairs={{3,0},{4,1},{5,2},{6,3},{7,4},{8,5},{9,6},{10,7},{11,8},{12,9},{13... | collective-permute-start | bytes 61448 | tf_op jit(solution)/shard_map/ppermute | solution.py:17
  991.0 21.2 %collective-permute-start.173 = (f32[1,4,1024]{2,0,1:T(1,128)}, f32[1,4,1024]{2,0,1:T(1,128)}, u32[]{:S(2)}, u32[]{:S(2)}) collective-permute-start(f32[1,4,1024]{2,0,1:T(1,128)} %get-tuple-element.51), channel_id=1, source_target_pairs={{9,0},{10,1},{11,2},{12,3},{13,4},{14,5},{15,6},{16,7},{17,8},{18,... | collective-permute-start | bytes 49160 | tf_op jit(solution)/shard_map/ppermute | solution.py:17
  992.9 25.0 %collective-permute-start.172 = (f32[1,4,1024]{2,0,1:T(1,128)}, f32[1,4,1024]{2,0,1:T(1,128)}, u32[]{:S(2)}, u32[]{:S(2)}) collective-permute-start(f32[1,4,1024]{2,0,1:T(1,128)} %get-tuple-element.51), channel_id=1, source_target_pairs={{8,0},{9,1},{10,2},{11,3},{12,4},{13,5},{14,6},{15,7},{16,8},{17,9... | collective-permute-start | bytes 49160 | tf_op jit(solution)/shard_map/ppermute | solution.py:17
  995.1 27.4 %collective-permute-start.171 = (f32[1,4,1024]{2,0,1:T(1,128)}, f32[1,4,1024]{2,0,1:T(1,128)}, u32[]{:S(2)}, u32[]{:S(2)}) collective-permute-start(f32[1,4,1024]{2,0,1:T(1,128)} %get-tuple-element.51), channel_id=1, source_target_pairs={{7,0},{8,1},{9,2},{10,3},{11,4},{12,5},{13,6},{14,7},{15,8},{16,9}... | collective-permute-start | bytes 49160 | tf_op jit(solution)/shard_map/ppermute | solution.py:17
  997.0 32.3 %collective-permute-start.170 = (f32[1,4,1024]{2,0,1:T(1,128)}, f32[1,4,1024]{2,0,1:T(1,128)}, u32[]{:S(2)}, u32[]{:S(2)}) collective-permute-start(f32[1,4,1024]{2,0,1:T(1,128)} %get-tuple-element.52), channel_id=1, source_target_pairs={{0,9},{1,10},{2,11},{3,12},{4,13},{5,14},{6,15},{7,16},{8,17},{9,1... | collective-permute-start | bytes 49160 | tf_op jit(solution)/shard_map/ppermute | solution.py:17
  1000.4 30.8 %collective-permute-start.169 = (f32[1,4,1024]{2,0,1:T(1,128)}, f32[1,4,1024]{2,0,1:T(1,128)}, u32[]{:S(2)}, u32[]{:S(2)}) collective-permute-start(f32[1,4,1024]{2,0,1:T(1,128)} %get-tuple-element.52), channel_id=1, source_target_pairs={{0,8},{1,9},{2,10},{3,11},{4,12},{5,13},{6,14},{7,15},{8,16},{9,17... | collective-permute-start | bytes 49160 | tf_op jit(solution)/shard_map/ppermute | solution.py:17
  1012.2 21.0 %collective-permute-start.168 = (f32[1,4,1024]{2,0,1:T(1,128)}, f32[1,4,1024]{2,0,1:T(1,128)}, u32[]{:S(2)}, u32[]{:S(2)}) collective-permute-start(f32[1,4,1024]{2,0,1:T(1,128)} %get-tuple-element.52), channel_id=1, source_target_pairs={{0,7},{1,8},{2,9},{3,10},{4,11},{5,12},{6,13},{7,14},{8,15},{9,16}... | collective-permute-start | bytes 49160 | tf_op jit(solution)/shard_map/ppermute | solution.py:17
  1017.9 21.5 %collective-permute-start.179 = (f32[1,5,1024]{2,1,0:T(8,128)}, f32[1,5,1024]{2,1,0:T(8,128)S(1)}, u32[]{:S(2)}, u32[]{:S(2)}) collective-permute-start(f32[1,5,1024]{2,1,0:T(8,128)} %pad_maximum_fusion.27), channel_id=1, source_target_pairs={{3,0},{4,1},{5,2},{6,3},{7,4},{8,5},{9,6},{10,7},{11,8},{12,9},{13... | collective-permute-start | bytes 61448 | tf_op jit(solution)/shard_map/ppermute | solution.py:17
  (380 other events, 7452.6 us)
where the time goes:
time: 1080 us; the launch traced here: 1060 us
  starting transfers between devices  567 us (52%)
  local copies, waits for them, and re-layouts  252 us (23%)
  other arithmetic  104 us (10%)
  matrix products  64 us (6%)
  waiting for transfers between devices  60.1 us (6%)
  between operations  10.9 us (1%)
    ppermute x180, starting transfers between devices, shifted(): lax.ppermute(value, axis, [(source, source + steps) for source in range(l...  567 us
    ppermute x180, waiting for transfers between devices, shifted(): lax.ppermute(value, axis, [(source, source + steps) for source in range(l...  60.1 us
    gather x60, local copies, waits for them, and re-layouts, fetch_ghosts(): ghosts.append(jnp.take(tables[kind], safe, axis=1))  51.3 us
    dot_general x64, matrix products, place_plane(): jnp.einsum('sxk,kl->sxl', shaped, table, precision=lax.Precision.HIGHEST)  46.7 us
    reduce_sum x4, other arithmetic, restrict_box(): field.reshape(slot_count, half, 2, half, 2, half, 2).sum(axis=(2, 4, 6))  31.8 us
    unnamed x549, local copies, waits for them, and re-layouts  26.9 us
  transfers between devices with their start and end apart: 180, of which 20 were waited for; matrix products, arithmetic and copies ran while one was open for 25% of the time, Pallas kernels for 0%

commit v1 on v0

v1 whole, which is shorter than its diff:
```python
import functools

import jax
import jax.numpy as jnp
from jax import lax
from jax.experimental import pallas as pl
from jax.experimental.pallas import tpu as pltpu
from jax.sharding import PartitionSpec as P


RF, PF = 48, 24
R1, P1 = 32, 24
R2 = 24
LANES = 128
FULL = (1, 0), (-1, 0), (0, 1), (0, -1), (1, 1), (1, -1), (-1, 1), (-1, -1)
FAR = (0, 2), (0, -2), (1, 2), (1, -2), (-1, 2), (-1, -2)
F32 = jnp.float32


def lane_ids(rows):
    return lax.broadcasted_iota(jnp.int32, (rows, LANES), 1)


def row_ids(rows):
    return lax.broadcasted_iota(jnp.int32, (rows, LANES), 0)


def turn(value, steps):
    return pltpu.roll(value, steps % LANES, 1)


def transposed(four):
    lanes = lane_ids(four[0].shape[0])
    low = lanes < 64
    even = (lanes // 32) % 2 == 0
    a, b, c, d = four
    e = jnp.where(low, a, turn(c, 64))
    f = jnp.where(low, b, turn(d, 64))
    g = jnp.where(low, turn(a, 64), c)
    h = jnp.where(low, turn(b, 64), d)
    return (
        jnp.where(even, e, turn(f, 32)),
        jnp.where(even, turn(e, -32), f),
        jnp.where(even, g, turn(h, 32)),
        jnp.where(even, turn(g, -32), h),
    )


def coefficients(c, besides, inside):
    total = 3.0 * c
    for beside, within in zip(besides, inside):
        total = total + 0.5 * jnp.where(within, beside, c)
    quarter = 0.4 / total
    faces = [
        jnp.where(within, (c + beside) * quarter, 0.0) for beside, within in zip(besides, inside)
    ]
    return faces, total, quarter


def around(ref, base, count, rows, twist):
    centre = ref[pl.ds(base, count), :]
    return centre, (
        ref[pl.ds(base - rows, count), :],
        ref[pl.ds(base + rows, count), :],
        ref[pl.ds(base - 1, count), :],
        ref[pl.ds(base + 1, count), :],
        turn(centre, twist),
        turn(centre, -twist),
    )


def weighted(faces, base, count, besides):
    parts = [faces[n][pl.ds(base, count), :] * besides[n] for n in range(6)]
    return (parts[0] + parts[1]) + (parts[2] + parts[3]) + (parts[4] + parts[5])


def loop(low, high, width, body):
    assert (high - low) % width == 0

    def step(index, carry):
        first = low + index * width
        stores = [item for m in range(width) for item in body(first + m)]
        for ref, at, value in stores:
            ref[at] = value
        return carry

    if high - low == width:
        step(0, 0)
    else:
        lax.fori_loop(0, (high - low) // width, step, 0)


def at(base, count):
    return pl.ds(base, count), slice(None)


def pair_rows(ref, base, count, rows):
    got = [
        ref[pl.ds(base + offset, count, stride=2), :] for offset in (0, 1, rows, rows + 1)
    ]
    return (got[0] + got[1]) + (got[2] + got[3])


def pair_lanes(value, width):
    first = (lane_ids(value.shape[0]) // width) % 2 == 0
    return 0.125 * (value + jnp.where(first, turn(value, -width), turn(value, width)))


def kernel(
    counts, source, conductance, initial, out_field, out_resid,
    raw_c, raw_u, raw_s, cf, uf, sf, u1, u2, fine, gf, df,
    ya, yb, xa, xb, ka, kb,
    c1, f1, e1, e1b, pe2, mid, w1, g1, d1, r1,
    y1a, y1b, x1a, x1b, k1a, k1b,
    y2a, y2b, x2a, x2b, k2a, k2b,
    y3a, y3b, x3a, x3b, k3a, k3b,
    c2, f2, e2, e2b, deep, g2,
    pe1, stage_f, stage_r, other_f, other_r,
    local_sem, send_sem, recv_sem,
):
    me = lax.axis_index("box")
    a, j = me // 8, me % 8
    half = me % 2
    sibling = me + 1 - 2 * half
    split = counts[me - half]

    across = {da: ((a + da + 16) % 16) * 8 for da in (-1, 0, 1)}
    along = {dj: (j + dj + 8) % 8 for dj in (-2, -1, 0, 1, 2)}

    def device(da, dj):
        return across[da] + along[dj]

    used = []

    def send(src, dst, target):
        number = len(used)
        copy = pltpu.make_async_remote_copy(
            src_ref=src, dst_ref=dst, send_sem=send_sem.at[number], recv_sem=recv_sem.at[number],
            device_id=(target,), device_id_type=pl.DeviceIdType.MESH,
        )
        copy.start()
        used.append(copy)
        return copy

    raws = (raw_c, raw_u, raw_s)
    given = (conductance, initial, source)
    mine = pl.ds(pl.multiple_of(512 * half, 512), 512)
    theirs = pl.ds(pl.multiple_of(512 - 512 * half, 512), 512)
    held = pl.ds(3 * half, 3)
    locals_ = []
    for number in range(3):
        copy = pltpu.make_async_copy(
            given[number].at[pl.ds(0, 3), :, mine], raws[number].at[held], local_sem.at[number]
        )
        copy.start()
        locals_.append(copy)

    barrier = pltpu.get_barrier_semaphore()
    for da, dj in FULL + FAR:
        pl.semaphore_signal(
            barrier, inc=1, device_id=(device(da, dj),), device_id_type=pl.DeviceIdType.MESH
        )
    pl.semaphore_wait(barrier, len(FULL + FAR))

    swaps = [
        send(given[number].at[pl.ds(0, 3), :, theirs], raws[number].at[held], sibling)
        for number in range(3)
    ]
    places = [jnp.where(p < split, p, jnp.clip(3 + p - split, 0, 5)) for p in range(4)]

    def bring(number, ref):
        locals_[number].wait()
        swaps[number].wait_recv()
        raw = raws[number]

        def step(t):
            rows = pl.ds(pl.multiple_of(8 * t, 8), 8)
            out = []
            for q in range(4):
                four = [raw[places[p], rows, 128 * q : 128 * q + 128] for p in range(4)]
                for i, value in enumerate(transposed(four)):
                    out.append((ref, at(pl.multiple_of((4 + 4 * q + i) * RF + 8 + 8 * t, 8), 8), value))
            return out

        loop(0, 4, 2, step)

    bring(0, cf)
    bring(1, uf)
    bring(2, sf)

    trio = ((uf, 3, 0), (cf, 3, 3), (sf, 2, 6))
    corner = ((uf, 1, 1), (uf, 1, 2), (uf, 2, 1), (cf, 1, 1), (cf, 1, 2), (cf, 2, 1), (sf, 1, 1))

    def near_plane(dj, depth):
        return 3 + depth if dj < 0 else 20 - depth

    def far_plane(dj, depth):
        return 19 + depth if dj < 0 else 4 - depth

    def near_row(da, depth):
        return 7 + depth if da < 0 else 40 - depth

    def far_row(da, depth):
        return 39 + depth if da < 0 else 8 - depth

    first = []
    for n, dj in enumerate((-1, 1)):
        for ref, most, first_row in trio:
            for d in range(most):
                ya[n, pl.ds(32 * (first_row + d), 32), :] = ref[pl.ds(near_plane(dj, d + 1) * RF + 8, 32), :]
        first.append(send(ya.at[n], yb.at[n], device(0, dj)))
    for n, da in enumerate((-1, 1)):
        for ref, most, first_row in trio:
            for d in range(most):
                xa[n, pl.ds(16 * (first_row + d), 16), :] = ref[
                    pl.ds(4 * RF + near_row(da, d + 1), 16, stride=RF), :
                ]
        first.append(send(xa.at[n], xb.at[n], device(da, 0)))
    for n, (da, dj) in enumerate(FULL[4:]):
        for k, (ref, dy, dx) in enumerate(corner):
            ka[n, pl.ds(k, 1), :] = ref[pl.ds(near_plane(dj, dy) * RF + near_row(da, dx), 1), :]
        first.append(send(ka.at[n], kb.at[n], device(da, dj)))

    def coarse_c(i):
        total = pair_rows(cf, (4 + 2 * i) * RF + 8, 16, RF)
        return [(c1, at(pl.multiple_of((8 + i) * R1 + 8, 8), 16), pair_lanes(total, 1))]

    loop(0, 8, 8, coarse_c)

    def packed(ref):
        lanes = lane_ids(8) % 4
        total = jnp.zeros((8, LANES), F32)
        for i in range(4):
            value = pair_lanes(pair_rows(ref, (8 + 2 * i) * R1 + 8, 8, R1), 2)
            total = total + jnp.where(lanes == i, value, 0.0)
        return total

    own2 = R2 + 2 * R2 + 8

    def near_plane1(dj, depth):
        return 7 + depth if dj < 0 else 16 - depth

    def far_plane1(dj, depth):
        return 15 + depth if dj < 0 else 8 - depth

    def near_row1(da, depth):
        return 7 + depth if da < 0 else 24 - depth

    def far_row1(da, depth):
        return 23 + depth if da < 0 else 8 - depth

    def strips1(ref, most, wide, ysrc, ydst, xsrc, xdst, ksrc, kdst):
        sent = []
        for n, dj in enumerate((-1, 1)):
            for d in range(most):
                ysrc[n, pl.ds(16 * d, 16), :] = ref[pl.ds(near_plane1(dj, d + 1) * R1 + 8, 16), :]
            sent.append(send(ysrc.at[n], ydst.at[n], device(0, dj)))
        for n, da in enumerate((-1, 1)):
            for d in range(most):
                xsrc[n, pl.ds(8 * d, 8), :] = ref[pl.ds(8 * R1 + near_row1(da, d + 1), 8, stride=R1), :]
            sent.append(send(xsrc.at[n], xdst.at[n], device(da, 0)))
        for n, (da, dj) in enumerate(FULL[4:]):
            row = 8 if da < 0 else 24 - wide
            for d in range(most - 1):
                ksrc[n, pl.ds(wide * d, wide), :] = ref[pl.ds(near_plane1(dj, d + 1) * R1 + row, wide), :]
            sent.append(send(ksrc.at[n], kdst.at[n], device(da, dj)))
        return sent

    def land1(ref, most, wide, ydst, xdst, kdst, sent):
        for copy in sent:
            copy.wait_recv()
        for n, dj in enumerate((-1, 1)):
            for d in range(most):
                ref[pl.ds(far_plane1(dj, d + 1) * R1 + 8, 16), :] = ydst[n, pl.ds(16 * d, 16), :]
        for n, da in enumerate((-1, 1)):
            for d in range(most):
                ref[pl.ds(8 * R1 + far_row1(da, d + 1), 8, stride=R1), :] = xdst[n, pl.ds(8 * d, 8), :]
        for n, (da, dj) in enumerate(FULL[4:]):
            row = 24 if da < 0 else 8 - wide
            for d in range(most - 1):
                ref[pl.ds(far_plane1(dj, d + 1) * R1 + row, wide), :] = kdst[n, pl.ds(wide * d, wide), :]

    def blocks2(ref):
        sent = []
        for da, dj in FULL + FAR:
            row = R2 + R2 * (2 - dj) + 8 * (1 - da)
            sent.append(send(ref.at[pl.ds(own2, 8)], ref.at[pl.ds(row, 8)], device(da, dj)))
        return sent

    c2[pl.ds(own2, 8), :] = packed(c1)
    second = strips1(c1, 6, 8, y1a, y1b, x1a, x1b, k1a, k1b)
    third = blocks2(c2)

    for copy in first:
        copy.wait_recv()
    for n, dj in enumerate((-1, 1)):
        for ref, most, first_row in trio:
            for d in range(most):
                ref[pl.ds(far_plane(dj, d + 1) * RF + 8, 32), :] = yb[n, pl.ds(32 * (first_row + d), 32), :]
    for n, da in enumerate((-1, 1)):
        for ref, most, first_row in trio:
            for d in range(most):
                ref[pl.ds(4 * RF + far_row(da, d + 1), 16, stride=RF), :] = xb[
                    n, pl.ds(16 * (first_row + d), 16), :
                ]
    for n, (da, dj) in enumerate(FULL[4:]):
        for k, (ref, dy, dx) in enumerate(corner):
            ref[pl.ds(far_plane(dj, dy) * RF + far_row(da, dx), 1), :] = kb[n, pl.ds(k, 1), :]

    fine_faces = [fine.at[n] for n in range(6)]

    def fine_coeffs(p):
        base = p * RF + 4
        centre, besides = around(cf, base, 40, RF, 1)
        x = row_ids(40) + (32 * a - 4)
        y = 16 * j + p - 4
        z = lane_ids(40)
        inside = (y != 0, y != 127, x != 0, x != 511, z != 0, z != 127)
        faces, total, quarter = coefficients(centre, besides, inside)
        out = [(fine, (n,) + at(base, 40), faces[n]) for n in range(6)]
        out.append((gf, at(base, 40), 2.0 * quarter * sf[pl.ds(base, 40), :]))
        out.append((df, at(base, 40), 1.25 * total))
        return out

    loop(2, 22, 2, fine_coeffs)

    def sweep(src, dst, faces, right, low, high, width, rows, start, count, twist):
        def step(p):
            base = p * rows + start
            centre, besides = around(src, base, count, rows, twist)
            value = 0.2 * centre + right[pl.ds(base, count), :] + weighted(faces, base, count, besides)
            return [(dst, at(base, count), value)]

        loop(low, high, width, step)

    def leftover(src, dst, faces, right, diag, low, high, width, rows, start, count, twist):
        def step(p):
            base = p * rows + start
            centre, besides = around(src, base, count, rows, twist)
            value = diag[pl.ds(base, count), :] * (
                right[pl.ds(base, count), :] + weighted(faces, base, count, besides) - 0.8 * centre
            )
            return [(dst, at(base, count), value)]

        loop(low, high, width, step)

    sweep(uf, u1, fine_faces, gf, 2, 22, 5, RF, 4, 40, 1)
    sweep(u1, u2, fine_faces, gf, 3, 21, 6, RF, 4, 40, 1)
    leftover(u2, u1, fine_faces, gf, df, 4, 20, 4, RF, 8, 32, 1)

    def coarse_f(i):
        total = pair_rows(u1, (4 + 2 * i) * RF + 8, 16, RF)
        return [(f1, at(pl.multiple_of((8 + i) * R1 + 8, 8), 16), pair_lanes(total, 1))]

    loop(0, 8, 8, coarse_f)
    fourth = strips1(f1, 5, 4, y2a, y2b, x2a, x2b, k2a, k2b)

    fifth = []
    for n, dj in enumerate((-1, 1)):
        for d in range(3):
            y3a[n, pl.ds(32 * d, 32), :] = u2[pl.ds(near_plane(dj, d + 1) * RF + 8, 32), :]
        fifth.append(send(y3a.at[n], y3b.at[n], device(0, dj)))
    for n, da in enumerate((-1, 1)):
        for d in range(3):
            x3a[n, pl.ds(16 * d, 16), :] = u2[pl.ds(4 * RF + near_row(da, d + 1), 16, stride=RF), :]
        fifth.append(send(x3a.at[n], x3b.at[n], device(da, 0)))
    for n, (da, dj) in enumerate(FULL[4:]):
        for k, (ref, dy, dx) in enumerate(corner[:3]):
            k3a[n, pl.ds(k, 1), :] = u2[pl.ds(near_plane(dj, dy) * RF + near_row(da, dx), 1), :]
        fifth.append(send(k3a.at[n], k3b.at[n], device(da, dj)))

    land1(c1, 6, 8, y1b, x1b, k1b, second)
    mid_faces = [mid.at[n] for n in range(6)]

    def mid_coeffs(p):
        base = p * R1
        centre, besides = around(c1, base, 32, R1, 2)
        x = row_ids(32) + (16 * a - 8)
        y = 8 * j + p - 8
        z = lane_ids(32)
        inside = (y != 0, y != 63, x != 0, x != 255, z >= 2, z < 126)
        faces, total, quarter = coefficients(centre, besides, inside)
        out = [(mid, (n,) + at(base, 32), faces[n]) for n in range(6)]
        out.append((w1, at(base, 32), 8.0 * quarter))
        out.append((d1, at(base, 32), 0.3125 * total))
        return out

    loop(3, 21, 3, mid_coeffs)

    for copy in third:
        copy.wait_recv()

    def around2(ref):
        lanes = lane_ids(5 * R2) % 4
        centre = ref[R2 : 6 * R2, :]
        return centre, (
            jnp.where(lanes == 0, turn(ref[0 : 5 * R2, :], -3), turn(centre, 1)),
            jnp.where(lanes == 3, turn(ref[2 * R2 : 7 * R2, :], 3), turn(centre, -1)),
            ref[pl.ds(R2 - 1, 5 * R2), :],
            ref[pl.ds(R2 + 1, 5 * R2), :],
            turn(centre, 4),
            turn(centre, -4),
        )

    rows2, lanes2 = row_ids(5 * R2), lane_ids(5 * R2)
    x = rows2 % R2 + (8 * a - 8)
    y = 4 * (rows2 // R2) + lanes2 % 4 + (4 * j - 8)
    inside2 = (y != 0, y != 31, x != 0, x != 127, lanes2 >= 4, lanes2 < 124)
    centre, besides = around2(c2)
    faces, total, quarter = coefficients(centre, besides, inside2)
    for n in range(6):
        deep[n] = faces[n]
    deep[6] = 32.0 * quarter

    land1(f1, 5, 4, y2b, x2b, k2b, fourth)

    def guess(p):
        base = p * R1
        return [(g1, at(base, 32), w1[pl.ds(base, 32), :] * f1[pl.ds(base, 32), :])]

    loop(3, 21, 9, guess)
    sweep(g1, e1, mid_faces, g1, 4, 20, 8, R1, 4, 24, 2)
    leftover(e1, r1, mid_faces, g1, d1, 8, 16, 8, R1, 8, 16, 2)
    f2[pl.ds(own2, 8), :] = packed(r1)
    sixth = blocks2(f2)
    for copy in sixth:
        copy.wait_recv()

    g2[...] = deep[6] * f2[R2 : 6 * R2, :]
    e2[R2 : 6 * R2, :] = g2[...]
    for src, dst in ((e2, e2b), (e2b, e2), (e2, e2b)):
        centre, besides = around2(src)
        parts = [deep[n] * besides[n] for n in range(6)]
        dst[R2 : 6 * R2, :] = (
            (0.2 * centre + g2[...]) + (parts[0] + parts[1]) + (parts[2] + parts[3]) + (parts[4] + parts[5])
        )

    lanes16 = lane_ids(16) % 4
    hops = ((1, 2), (-1, 2), (1, -2), (-1, -2))
    for number in range(8):
        block, i = (number + 6) // 4, (number + 6) % 4
        value = jnp.where(lanes16 == i, e2b[pl.ds(R2 + R2 * block + 4, 16), :], 0.0)
        value = value + turn(value, hops[i][0])
        value = value + turn(value, hops[i][1])
        pe2[pl.ds(32 * number, 16, stride=2), :] = value
        pe2[pl.ds(32 * number + 1, 16, stride=2), :] = value

    def corrected1(p):
        value = e1[pl.ds(p * R1 + 4, 24), :] + pe2[pl.ds((p // 2 - 2) * 32 + 4, 24), :]
        return [(e1, at(p * R1 + 4, 24), value)]

    loop(4, 20, 8, corrected1)
    sweep(e1, e1b, mid_faces, g1, 5, 19, 7, R1, 4, 24, 2)
    sweep(e1b, e1, mid_faces, g1, 6, 18, 6, R1, 4, 24, 2)

    def grown(i):
        value = e1[pl.ds((i + 6) * R1 + 4, 24), :]
        return [(pe1, (pl.ds(RF * i + odd, 24, stride=2), slice(None)), value) for odd in (0, 1)]

    loop(0, 12, 6, grown)
    for copy in fifth:
        copy.wait_recv()
    for n, dj in enumerate((-1, 1)):
        for d in range(3):
            u2[pl.ds(far_plane(dj, d + 1) * RF + 8, 32), :] = y3b[n, pl.ds(32 * d, 32), :]
    for n, da in enumerate((-1, 1)):
        for d in range(3):
            u2[pl.ds(4 * RF + far_row(da, d + 1), 16, stride=RF), :] = x3b[n, pl.ds(16 * d, 16), :]
    for n, (da, dj) in enumerate(FULL[4:]):
        for k, (ref, dy, dx) in enumerate(corner[:3]):
            u2[pl.ds(far_plane(dj, dy) * RF + far_row(da, dx), 1), :] = k3b[n, pl.ds(k, 1), :]

    def corrected0(p):
        base = p * RF + 4
        return [(u2, at(base, 40), u2[pl.ds(base, 40), :] + pe1[pl.ds((p // 2) * RF + 4, 40), :])]

    loop(1, 23, 2, corrected0)
    sweep(u2, u1, fine_faces, gf, 2, 22, 5, RF, 4, 40, 1)
    sweep(u1, u2, fine_faces, gf, 3, 21, 6, RF, 4, 40, 1)
    leftover(u2, u1, fine_faces, gf, df, 4, 20, 4, RF, 8, 32, 1)

    last = []
    for ref, stage, other in ((u2, stage_f, other_f), (u1, stage_r, other_r)):

        def step(t):
            rows = pl.ds(pl.multiple_of(8 * t, 8), 8)
            out = []
            for q in range(4):
                four = [
                    ref[pl.ds(pl.multiple_of((4 + 4 * q + i) * RF + 8 + 8 * t, 8), 8), :]
                    for i in range(4)
                ]
                for p, value in enumerate(transposed(four)):
                    out.append((stage, (p, rows, slice(128 * q, 128 * q + 128)), value))
            return out

        loop(0, 4, 2, step)
        last.append(send(stage.at[pl.ds(1 - half, 3)], other, sibling))

    own = jnp.where(half == 0, split, 4 - split)
    for number, (stage, other, out) in enumerate(
        ((stage_f, other_f, out_field), (stage_r, other_r, out_resid))
    ):
        for s in range(4):
            p = jnp.clip(s + half * split, 0, 3)
            out[s, :, mine] = jnp.where(s < own, stage[p], 0.0)
        last[number].wait_recv()
        for s in range(4):
            p = jnp.clip(s + half * (split - 1), 0, 2)
            out[s, :, theirs] = jnp.where(s < own, other[p], 0.0)

    for copy in used:
        copy.wait_send()


def vmem(*shape):
    return pltpu.VMEM(shape, F32)


def body(source, conductance, initial, box_counts):
    fine_field = vmem(PF * RF, LANES)
    mid_field = vmem(P1 * R1, LANES)
    deep_field = vmem(7 * R2, LANES)
    scratch = [vmem(6, 32, 512)] * 3
    scratch += [fine_field] * 5 + [vmem(6, PF * RF, LANES)] + [fine_field] * 2
    scratch += [vmem(2, 256, LANES)] * 2 + [vmem(2, 128, LANES)] * 2 + [vmem(4, 8, LANES)] * 2
    scratch += [mid_field] * 4 + [vmem(8 * 32, LANES), vmem(6, P1 * R1, LANES)] + [mid_field] * 4
    scratch += [vmem(2, 96, LANES)] * 2 + [vmem(2, 48, LANES)] * 2 + [vmem(4, 40, LANES)] * 2
    scratch += [vmem(2, 80, LANES)] * 2 + [vmem(2, 40, LANES)] * 2 + [vmem(4, 16, LANES)] * 2
    scratch += [vmem(2, 96, LANES)] * 2 + [vmem(2, 48, LANES)] * 2 + [vmem(4, 8, LANES)] * 2
    scratch += [deep_field] * 4 + [vmem(7, 5 * R2, LANES), vmem(5 * R2, LANES)]
    scratch += [vmem(12 * RF, LANES)] + [vmem(4, 32, 512)] * 2 + [vmem(3, 32, 512)] * 2
    messages = 3 + 8 + 8 + 14 + 8 + 8 + 14 + 2
    scratch += [pltpu.SemaphoreType.DMA((3,))] + [pltpu.SemaphoreType.DMA((messages,))] * 2
    shape = jax.ShapeDtypeStruct(source.shape, source.dtype)
    return pl.pallas_call(
        kernel,
        out_shape=(shape, shape),
        in_specs=[pl.BlockSpec(memory_space=pltpu.SMEM)] + [pl.BlockSpec(memory_space=pl.ANY)] * 3,
        out_specs=(pl.BlockSpec(memory_space=pltpu.VMEM),) * 2,
        scratch_shapes=scratch,
        compiler_params=pltpu.CompilerParams(
            collective_id=0, has_side_effects=True, vmem_limit_bytes=60 * 2**20
        ),
        cost_estimate=pl.CostEstimate(flops=3 * 10**7, bytes_accessed=3 * 10**6, transcendentals=0),
    )(box_counts, source, conductance, initial)


def solution(mesh):
    return jax.shard_map(
        body,
        mesh=mesh,
        in_specs=(P("box", None, None), P("box", None, None), P("box", None, None), P()),
        out_specs=(P("box", None, None), P("box", None, None)),
        check_vma=False,
    )
```

time: 1080 us -> 41 us (0.04)
  the two profiles are of different devices: /device:TPU:96 before, /device:TPU:1 now
where the time goes in v1:
time: 41 us; the launch traced here: 40.8 us
  Pallas kernels  37.5 us (91%)
  local copies, waits for them, and re-layouts  2.74 us (7%)
  between operations  0.65 us (2%)
    pallas_call x1, Pallas kernels, body(): pl.pallas_call(kernel, out_shape=(shape, shape), in_specs=[pl.BlockSpec(m...  37.5 us
    unnamed x4, local copies, waits for them, and re-layouts  2.74 us

profile of v1, /device:TPU:1, one launch (start us, length us, event | category | flops | bytes accessed | tf_op | source)
XLA Modules:
  0.0 40.8 jit_solution(11943934620199509269)
XLA Ops:
  0.6 37.5 %shard_map.59 = (f32[4,32,1024]{2,1,0:T(8,128)}, f32[4,32,1024]{2,1,0:T(8,128)}) custom-call(s32[128]{0:T(128)} %counts.1, f32[4,32,1024]{2,1,0:T(8,128)} %source.1, f32[4,32,1024]{2,1,0:T(8,128)} %conductance.1, f32[4,32,1024]{2,1,0:T(8,128)} %initial.1), custom_call_target="tpu_custom_call" | custom-call | flops 30000000 | bytes 3000000 | tf_op jit(solution)/shard_map/pallas_call | solution.py:536
  38.1 0.0 copy-start
  38.1 1.9 %copy.8 = f32[4,32,1024]{2,1,0:T(8,128)} copy(f32[4,32,1024]{2,1,0:T(8,128)} %get-tuple-element.4) | data formatting | bytes 1048576
  40.1 0.0 copy-done
  40.1 0.8 %copy.9 = f32[4,32,1024]{2,1,0:T(8,128)} copy(f32[4,32,1024]{2,1,0:T(8,128)S(1)} %copy-done) | data formatting | bytes 1048576
Async XLA Ops:
  38.1 2.0 %copy-start = (f32[4,32,1024]{2,1,0:T(8,128)S(1)}, f32[4,32,1024]{2,1,0:T(8,128)}, u32[]{:S(2)}) copy-start(f32[4,32,1024]{2,1,0:T(8,128)} %get-tuple-element.5) | copy-start | bytes 1572868

commit v2 on v1

--- a/solution.py
+++ b/solution.py
@@ -108,22 +108,15 @@
 
 def kernel(
     counts, source, conductance, initial, out_field, out_resid,
-    raw_c, raw_u, raw_s, cf, uf, sf, u1, u2, fine, gf, df,
-    ya, yb, xa, xb, ka, kb,
-    c1, f1, e1, e1b, pe2, mid, w1, g1, d1, r1,
-    y1a, y1b, x1a, x1b, k1a, k1b,
-    y2a, y2b, x2a, x2b, k2a, k2b,
-    y3a, y3b, x3a, x3b, k3a, k3b,
-    c2, f2, e2, e2b, deep, g2,
-    pe1, stage_f, stage_r, other_f, other_r,
-    local_sem, send_sem, recv_sem,
+    owners, raw_c, raw_u, raw_s, cf, uf, sf, u1, u2, fine, gf, df,
+    c1, f1, e1, e1b, pe2, mid, w1, g1, d1, r1, c2, f2, e2, e2b, deep, g2, pe1,
+    stage_f, stage_r, other_f, other_r, *rest,
 ):
+    post, local_sem, send_sem, recv_sem = rest[:-3], rest[-3], rest[-2], rest[-1]
     me = lax.axis_index("box")
     a, j = me // 8, me % 8
     half = me % 2
     sibling = me + 1 - 2 * half
-    split = counts[me - half]
-
     across = {da: ((a + da + 16) % 16) * 8 for da in (-1, 0, 1)}
     along = {dj: (j + dj + 8) % 8 for dj in (-2, -1, 0, 1, 2)}
 
@@ -147,13 +140,15 @@
     mine = pl.ds(pl.multiple_of(512 * half, 512), 512)
     theirs = pl.ds(pl.multiple_of(512 - 512 * half, 512), 512)
     held = pl.ds(3 * half, 3)
-    locals_ = []
+    locals_ = [pltpu.make_async_copy(counts, owners, local_sem.at[3])]
     for number in range(3):
-        copy = pltpu.make_async_copy(
-            given[number].at[pl.ds(0, 3), :, mine], raws[number].at[held], local_sem.at[number]
+        locals_.append(
+            pltpu.make_async_copy(
+                given[number].at[pl.ds(0, 3), :, mine], raws[number].at[held], local_sem.at[number]
+            )
         )
+    for copy in locals_:
         copy.start()
-        locals_.append(copy)
 
     barrier = pltpu.get_barrier_semaphore()
     for da, dj in FULL + FAR:
@@ -166,10 +161,12 @@
         send(given[number].at[pl.ds(0, 3), :, theirs], raws[number].at[held], sibling)
         for number in range(3)
     ]
+    locals_[0].wait()
+    split = owners[me - half]
     places = [jnp.where(p < split, p, jnp.clip(3 + p - split, 0, 5)) for p in range(4)]
 
     def bring(number, ref):
-        locals_[number].wait()
+        locals_[1 + number].wait()
         swaps[number].wait_recv()
         raw = raws[number]
 
@@ -184,42 +181,69 @@
 
         loop(0, 4, 2, step)
 
+    ROWS = (RF, R1)
+    OWN = ((4, 16, 8, 32), (8, 8, 8, 16))
+
+    def near(first, count, side, depth):
+        return first - 1 + depth if side < 0 else first + count - depth
+
+    def far(first, count, side, depth):
+        return first + count - 1 + depth if side < 0 else first - depth
+
+    def pieces(strips, corners, da, dj, pick):
+        out = []
+        if da == 0:
+            for ref, level, depths in strips:
+                plane, planes, row, rows = OWN[level]
+                for d in depths:
+                    out.append((ref, pick(plane, planes, dj, d) * ROWS[level] + row, rows, 1))
+        elif dj == 0:
+            for ref, level, depths in strips:
+                plane, planes, row, rows = OWN[level]
+                for d in depths:
+                    out.append(
+                        (ref, plane * ROWS[level] + pick(row, rows, da, d), planes, ROWS[level])
+                    )
+        else:
+            for ref, level, depth, low, count in corners:
+                plane, planes, row, rows = OWN[level]
+                ends = [pick(row, rows, da, d) for d in (low, low + count - 1)]
+                out.append((ref, pick(plane, planes, dj, depth) * ROWS[level] + min(ends), count, 1))
+        return out
+
+    def slab(ref, first, count, stride):
+        return (pl.ds(first, count, stride=stride) if stride > 1 else pl.ds(first, count)), slice(None)
+
+    spare = list(post)
+
+    def exchange(strips, corners):
+        boxes = [(spare.pop(0), spare.pop(0)) for _ in range(3)]
+        started = []
+        for number, (da, dj) in enumerate(FULL):
+            kind = 2 if da and dj else 1 if da else 0
+            slot = number % 2 if number < 4 else number - 4
+            out, got = boxes[kind]
+            offset = 0
+            for ref, first, count, stride in pieces(strips, corners, da, dj, near):
+                out[slot, pl.ds(offset, count), :] = ref[slab(ref, first, count, stride)]
+                offset += count
+            started.append((send(out.at[slot], got.at[slot], device(da, dj)), got, slot, da, dj))
+
+        def land():
+            for copy, got, slot, da, dj in started:
+                copy.wait_recv()
+                offset = 0
+                for ref, first, count, stride in pieces(strips, corners, da, dj, far):
+                    ref[slab(ref, first, count, stride)] = got[slot, pl.ds(offset, count), :]
+                    offset += count
+
+        return land
+
+    def fine_corner(ref, depth):
+        return [(ref, 0, d, 1, depth - d) for d in range(1, depth)]
+
     bring(0, cf)
-    bring(1, uf)
-    bring(2, sf)
-
-    trio = ((uf, 3, 0), (cf, 3, 3), (sf, 2, 6))
-    corner = ((uf, 1, 1), (uf, 1, 2), (uf, 2, 1), (cf, 1, 1), (cf, 1, 2), (cf, 2, 1), (sf, 1, 1))
-
-    def near_plane(dj, depth):
-        return 3 + depth if dj < 0 else 20 - depth
-
-    def far_plane(dj, depth):
-        return 19 + depth if dj < 0 else 4 - depth
-
-    def near_row(da, depth):
-        return 7 + depth if da < 0 else 40 - depth
-
-    def far_row(da, depth):
-        return 39 + depth if da < 0 else 8 - depth
-
-    first = []
-    for n, dj in enumerate((-1, 1)):
-        for ref, most, first_row in trio:
-            for d in range(most):
-                ya[n, pl.ds(32 * (first_row + d), 32), :] = ref[pl.ds(near_plane(dj, d + 1) * RF + 8, 32), :]
-        first.append(send(ya.at[n], yb.at[n], device(0, dj)))
-    for n, da in enumerate((-1, 1)):
-        for ref, most, first_row in trio:
-            for d in range(most):
-                xa[n, pl.ds(16 * (first_row + d), 16), :] = ref[
-                    pl.ds(4 * RF + near_row(da, d + 1), 16, stride=RF), :
-                ]
-        first.append(send(xa.at[n], xb.at[n], device(da, 0)))
-    for n, (da, dj) in enumerate(FULL[4:]):
-        for k, (ref, dy, dx) in enumerate(corner):
-            ka[n, pl.ds(k, 1), :] = ref[pl.ds(near_plane(dj, dy) * RF + near_row(da, dx), 1), :]
-        first.append(send(ka.at[n], kb.at[n], device(da, dj)))
+    land_c = exchange(((cf, 0, (1, 2, 3)),), fine_corner(cf, 3))
 
     def coarse_c(i):
         total = pair_rows(cf, (4 + 2 * i) * RF + 8, 16, RF)
@@ -237,76 +261,23 @@
 
     own2 = R2 + 2 * R2 + 8
 
-    def near_plane1(dj, depth):
-        return 7 + depth if dj < 0 else 16 - depth
-
-    def far_plane1(dj, depth):
-        return 15 + depth if dj < 0 else 8 - depth
-
-    def near_row1(da, depth):
-        return 7 + depth if da < 0 else 24 - depth
-
-    def far_row1(da, depth):
-        return 23 + depth if da < 0 else 8 - depth
-
-    def strips1(ref, most, wide, ysrc, ydst, xsrc, xdst, ksrc, kdst):
-        sent = []
-        for n, dj in enumerate((-1, 1)):
-            for d in range(most):
-                ysrc[n, pl.ds(16 * d, 16), :] = ref[pl.ds(near_plane1(dj, d + 1) * R1 + 8, 16), :]
-            sent.append(send(ysrc.at[n], ydst.at[n], device(0, dj)))
-        for n, da in enumerate((-1, 1)):
-            for d in range(most):
-                xsrc[n, pl.ds(8 * d, 8), :] = ref[pl.ds(8 * R1 + near_row1(da, d + 1), 8, stride=R1), :]
-            sent.append(send(xsrc.at[n], xdst.at[n], device(da, 0)))
-        for n, (da, dj) in enumerate(FULL[4:]):
-            row = 8 if da < 0 else 24 - wide
-            for d in range(most - 1):
-                ksrc[n, pl.ds(wide * d, wide), :] = ref[pl.ds(near_plane1(dj, d + 1) * R1 + row, wide), :]
-            sent.append(send(ksrc.at[n], kdst.at[n], device(da, dj)))
-        return sent
-
-    def land1(ref, most, wide, ydst, xdst, kdst, sent):
-        for copy in sent:
-            copy.wait_recv()
-        for n, dj in enumerate((-1, 1)):
-            for d in range(most):
-                ref[pl.ds(far_plane1(dj, d + 1) * R1 + 8, 16), :] = ydst[n, pl.ds(16 * d, 16), :]
-        for n, da in enumerate((-1, 1)):
-            for d in range(most):
-                ref[pl.ds(8 * R1 + far_row1(da, d + 1), 8, stride=R1), :] = xdst[n, pl.ds(8 * d, 8), :]
-        for n, (da, dj) in enumerate(FULL[4:]):
-            row = 24 if da < 0 else 8 - wide
-            for d in range(most - 1):
-                ref[pl.ds(far_plane1(dj, d + 1) * R1 + row, wide), :] = kdst[n, pl.ds(wide * d, wide), :]
-
     def blocks2(ref):
         sent = []
-        for da, dj in FULL + FAR:
+        for da, dj in FAR + FULL:
             row = R2 + R2 * (2 - dj) + 8 * (1 - da)
             sent.append(send(ref.at[pl.ds(own2, 8)], ref.at[pl.ds(row, 8)], device(da, dj)))
         return sent
 
+    bring(1, uf)
+    bring(2, sf)
+    land_u = exchange(
+        ((uf, 0, (1, 2, 3)), (sf, 0, (1, 2))), fine_corner(uf, 3) + fine_corner(sf, 2)
+    )
     c2[pl.ds(own2, 8), :] = packed(c1)
-    second = strips1(c1, 6, 8, y1a, y1b, x1a, x1b, k1a, k1b)
+    land_c1 = exchange(((c1, 1, (1, 2, 3, 4, 5, 6)),), [(c1, 1, d, 1, 6 - d) for d in range(1, 6)])
     third = blocks2(c2)
 
-    for copy in first:
-        copy.wait_recv()
-    for n, dj in enumerate((-1, 1)):
-        for ref, most, first_row in trio:
-            for d in range(most):
-                ref[pl.ds(far_plane(dj, d + 1) * RF + 8, 32), :] = yb[n, pl.ds(32 * (first_row + d), 32), :]
-    for n, da in enumerate((-1, 1)):
-        for ref, most, first_row in trio:
-            for d in range(most):
-                ref[pl.ds(4 * RF + far_row(da, d + 1), 16, stride=RF), :] = xb[
-                    n, pl.ds(16 * (first_row + d), 16), :
-                ]
-    for n, (da, dj) in enumerate(FULL[4:]):
-        for k, (ref, dy, dx) in enumerate(corner):
-            ref[pl.ds(far_plane(dj, dy) * RF + far_row(da, dx), 1), :] = kb[n, pl.ds(k, 1), :]
-
+    land_c()
     fine_faces = [fine.at[n] for n in range(6)]
 
     def fine_coeffs(p):
@@ -318,11 +289,18 @@
         inside = (y != 0, y != 127, x != 0, x != 511, z != 0, z != 127)
         faces, total, quarter = coefficients(centre, besides, inside)
         out = [(fine, (n,) + at(base, 40), faces[n]) for n in range(6)]
-        out.append((gf, at(base, 40), 2.0 * quarter * sf[pl.ds(base, 40), :]))
+        out.append((gf, at(base, 40), 2.0 * quarter))
         out.append((df, at(base, 40), 1.25 * total))
         return out
 
     loop(2, 22, 2, fine_coeffs)
+    land_u()
+
+    def fine_right(p):
+        base = p * RF + 4
+        return [(gf, at(base, 40), gf[pl.ds(base, 40), :] * sf[pl.ds(base, 40), :])]
+
+    loop(2, 22, 4, fine_right)
 
     def sweep(src, dst, faces, right, low, high, width, rows, start, count, twist):
         def step(p):
@@ -353,23 +331,13 @@
         return [(f1, at(pl.multiple_of((8 + i) * R1 + 8, 8), 16), pair_lanes(total, 1))]
 
     loop(0, 8, 8, coarse_f)
-    fourth = strips1(f1, 5, 4, y2a, y2b, x2a, x2b, k2a, k2b)
-
-    fifth = []
-    for n, dj in enumerate((-1, 1)):
-        for d in range(3):
-            y3a[n, pl.ds(32 * d, 32), :] = u2[pl.ds(near_plane(dj, d + 1) * RF + 8, 32), :]
-        fifth.append(send(y3a.at[n], y3b.at[n], device(0, dj)))
-    for n, da in enumerate((-1, 1)):
-        for d in range(3):
-            x3a[n, pl.ds(16 * d, 16), :] = u2[pl.ds(4 * RF + near_row(da, d + 1), 16, stride=RF), :]
-        fifth.append(send(x3a.at[n], x3b.at[n], device(da, 0)))
-    for n, (da, dj) in enumerate(FULL[4:]):
-        for k, (ref, dy, dx) in enumerate(corner[:3]):
-            k3a[n, pl.ds(k, 1), :] = u2[pl.ds(near_plane(dj, dy) * RF + near_row(da, dx), 1), :]
-        fifth.append(send(k3a.at[n], k3b.at[n], device(da, dj)))
-
-    land1(c1, 6, 8, y1b, x1b, k1b, second)
+    land_f = exchange(((f1, 1, (1, 2)),), [(f1, 1, 1, 1, 1)])
+    land_rest = exchange(
+        ((f1, 1, (3, 4, 5)), (u2, 0, (1, 2, 3))),
+        [(f1, 1, 1, 2, 3), (f1, 1, 2, 1, 3), (f1, 1, 3, 1, 2), (f1, 1, 4, 1, 1)] + fine_corner(u2, 3),
+    )
+
+    land_c1()
     mid_faces = [mid.at[n] for n in range(6)]
 
     def mid_coeffs(p):
@@ -412,20 +380,23 @@
         deep[n] = faces[n]
     deep[6] = 32.0 * quarter
 
-    land1(f1, 5, 4, y2b, x2b, k2b, fourth)
-
     def guess(p):
         base = p * R1
         return [(g1, at(base, 32), w1[pl.ds(base, 32), :] * f1[pl.ds(base, 32), :])]
 
-    loop(3, 21, 9, guess)
-    sweep(g1, e1, mid_faces, g1, 4, 20, 8, R1, 4, 24, 2)
+    land_f()
+    loop(6, 18, 12, guess)
+    sweep(g1, e1, mid_faces, g1, 7, 17, 10, R1, 4, 24, 2)
     leftover(e1, r1, mid_faces, g1, d1, 8, 16, 8, R1, 8, 16, 2)
     f2[pl.ds(own2, 8), :] = packed(r1)
     sixth = blocks2(f2)
+
+    land_rest()
+    loop(3, 21, 9, guess)
+    sweep(g1, e1, mid_faces, g1, 4, 20, 8, R1, 4, 24, 2)
+
     for copy in sixth:
         copy.wait_recv()
-
     g2[...] = deep[6] * f2[R2 : 6 * R2, :]
     e2[R2 : 6 * R2, :] = g2[...]
     for src, dst in ((e2, e2b), (e2b, e2), (e2, e2b)):
@@ -458,17 +429,6 @@
         return [(pe1, (pl.ds(RF * i + odd, 24, stride=2), slice(None)), value) for odd in (0, 1)]
 
     loop(0, 12, 6, grown)
-    for copy in fifth:
-        copy.wait_recv()
-    for n, dj in enumerate((-1, 1)):
-        for d in range(3):
-            u2[pl.ds(far_plane(dj, d + 1) * RF + 8, 32), :] = y3b[n, pl.ds(32 * d, 32), :]
-    for n, da in enumerate((-1, 1)):
-        for d in range(3):
-            u2[pl.ds(4 * RF + far_row(da, d + 1), 16, stride=RF), :] = x3b[n, pl.ds(16 * d, 16), :]
-    for n, (da, dj) in enumerate(FULL[4:]):
-        for k, (ref, dy, dx) in enumerate(corner[:3]):
-            u2[pl.ds(far_plane(dj, dy) * RF + far_row(da, dx), 1), :] = k3b[n, pl.ds(k, 1), :]
 
     def corrected0(p):
         base = p * RF + 4
@@ -477,11 +437,8 @@
     loop(1, 23, 2, corrected0)
     sweep(u2, u1, fine_faces, gf, 2, 22, 5, RF, 4, 40, 1)
     sweep(u1, u2, fine_faces, gf, 3, 21, 6, RF, 4, 40, 1)
-    leftover(u2, u1, fine_faces, gf, df, 4, 20, 4, RF, 8, 32, 1)
-
-    last = []
-    for ref, stage, other in ((u2, stage_f, other_f), (u1, stage_r, other_r)):
-
+
+    def give(ref, stage, other):
         def step(t):
             rows = pl.ds(pl.multiple_of(8 * t, 8), 8)
             out = []
@@ -495,20 +452,26 @@
             return out
 
         loop(0, 4, 2, step)
-        last.append(send(stage.at[pl.ds(1 - half, 3)], other, sibling))
+        return send(stage.at[pl.ds(1 - half, 3)], other, sibling)
 
     own = jnp.where(half == 0, split, 4 - split)
-    for number, (stage, other, out) in enumerate(
-        ((stage_f, other_f, out_field), (stage_r, other_r, out_resid))
-    ):
+
+    def keep(stage, out):
         for s in range(4):
-            p = jnp.clip(s + half * split, 0, 3)
-            out[s, :, mine] = jnp.where(s < own, stage[p], 0.0)
-        last[number].wait_recv()
+            out[s, :, mine] = jnp.where(s < own, stage[jnp.clip(s + half * split, 0, 3)], 0.0)
+
+    def take(copy, other, out):
+        copy.wait_recv()
         for s in range(4):
-            p = jnp.clip(s + half * (split - 1), 0, 2)
-            out[s, :, theirs] = jnp.where(s < own, other[p], 0.0)
-
+            out[s, :, theirs] = jnp.where(s < own, other[jnp.clip(s + half * (split - 1), 0, 2)], 0.0)
+
+    last_f = give(u2, stage_f, other_f)
+    leftover(u2, u1, fine_faces, gf, df, 4, 20, 4, RF, 8, 32, 1)
+    last_r = give(u1, stage_r, other_r)
+    keep(stage_f, out_field)
+    take(last_f, other_f, out_field)
+    keep(stage_r, out_resid)
+    take(last_r, other_r, out_resid)
     for copy in used:
         copy.wait_send()
 
@@ -521,29 +484,29 @@
     fine_field = vmem(PF * RF, LANES)
     mid_field = vmem(P1 * R1, LANES)
     deep_field = vmem(7 * R2, LANES)
-    scratch = [vmem(6, 32, 512)] * 3
+    scratch = [pltpu.SMEM(box_counts.shape, jnp.int32)] + [vmem(6, 32, 512)] * 3
     scratch += [fine_field] * 5 + [vmem(6, PF * RF, LANES)] + [fine_field] * 2
-    scratch += [vmem(2, 256, LANES)] * 2 + [vmem(2, 128, LANES)] * 2 + [vmem(4, 8, LANES)] * 2
     scratch += [mid_field] * 4 + [vmem(8 * 32, LANES), vmem(6, P1 * R1, LANES)] + [mid_field] * 4
-    scratch += [vmem(2, 96, LANES)] * 2 + [vmem(2, 48, LANES)] * 2 + [vmem(4, 40, LANES)] * 2
-    scratch += [vmem(2, 80, LANES)] * 2 + [vmem(2, 40, LANES)] * 2 + [vmem(4, 16, LANES)] * 2
-    scratch += [vmem(2, 96, LANES)] * 2 + [vmem(2, 48, LANES)] * 2 + [vmem(4, 8, LANES)] * 2
-    scratch += [deep_field] * 4 + [vmem(7, 5 * R2, LANES), vmem(5 * R2, LANES)]
-    scratch += [vmem(12 * RF, LANES)] + [vmem(4, 32, 512)] * 2 + [vmem(3, 32, 512)] * 2
-    messages = 3 + 8 + 8 + 14 + 8 + 8 + 14 + 2
-    scratch += [pltpu.SemaphoreType.DMA((3,))] + [pltpu.SemaphoreType.DMA((messages,))] * 2
+    scratch += [deep_field] * 4 + [vmem(7, 5 * R2, LANES), vmem(5 * R2, LANES), vmem(12 * RF, LANES)]
+    scratch += [vmem(4, 32, 512)] * 2 + [vmem(3, 32, 512)] * 2
+    for big, middle, small in ((96, 48, 8), (160, 80, 8), (96, 48, 16), (32, 16, 8), (144, 72, 16)):
+        for count, rows in ((2, big), (2, middle), (4, small)):
+            scratch += [vmem(count, rows, LANES)] * 2
+    messages = 3 + 5 * 8 + 2 * 14 + 2
+    scratch += [pltpu.SemaphoreType.DMA((4,))] + [pltpu.SemaphoreType.DMA((messages,))] * 2
+    hbm = pl.BlockSpec(memory_space=pltpu.HBM)
     shape = jax.ShapeDtypeStruct(source.shape, source.dtype)
     return pl.pallas_call(
         kernel,
         out_shape=(shape, shape),
-        in_specs=[pl.BlockSpec(memory_space=pltpu.SMEM)] + [pl.BlockSpec(memory_space=pl.ANY)] * 3,
+        in_specs=[hbm] * 4,
         out_specs=(pl.BlockSpec(memory_space=pltpu.VMEM),) * 2,
         scratch_shapes=scratch,
         compiler_params=pltpu.CompilerParams(
-            collective_id=0, has_side_effects=True, vmem_limit_bytes=60 * 2**20
+            collective_id=0, has_side_effects=True, vmem_limit_bytes=40 * 2**20
         ),
         cost_estimate=pl.CostEstimate(flops=3 * 10**7, bytes_accessed=3 * 10**6, transcendentals=0),
-    )(box_counts, source, conductance, initial)
+    )(*[pltpu.with_memory_space_constraint(x, pltpu.HBM) for x in (box_counts, source, conductance, initial)])
 
 
 def solution(mesh):

time: 41 us -> 36.2 us (0.88)
  Pallas kernels: 37.5 us -> 33.9 us
  local copies, waits for them, and re-layouts: 2.74 us -> 1.59 us
    pallas_call x1, Pallas kernels: 37.5 us -> 33.9 us  [body(): pl.pallas_call(kernel, out_shape=(shape, shape), in_specs=[hbm] * 4, out_...]
    unnamed x4 -> x2, local copies, waits for them, and re-layouts: 2.74 us -> 1.59 us
where the time goes in v2:
time: 36.2 us; the launch traced here: 36.1 us
  Pallas kernels  33.9 us (94%)
  local copies, waits for them, and re-layouts  1.59 us (4%)
  between operations  0.64 us (2%)
    pallas_call x1, Pallas kernels, body(): pl.pallas_call(kernel, out_shape=(shape, shape), in_specs=[hbm] * 4, out_...  33.9 us
    unnamed x2, local copies, waits for them, and re-layouts  1.59 us

profile of v2, /device:TPU:1, one launch (start us, length us, event | category | flops | bytes accessed | tf_op | source)
XLA Modules:
  0.0 36.1 jit_solution(8023763787571998871)
XLA Ops:
  0.6 33.9 %shard_map.59 = (f32[4,32,1024]{2,1,0:T(8,128)S(1)}, f32[4,32,1024]{2,1,0:T(8,128)S(1)}) custom-call(s32[128]{0:T(128)} %counts.1, f32[4,32,1024]{2,1,0:T(8,128)} %source.1, f32[4,32,1024]{2,1,0:T(8,128)} %conductance.1, f32[4,32,1024]{2,1,0:T(8,128)} %initial.1), custom_call_target="tpu_custom_call" | custom-call | flops 30000000 | bytes 3000000 | tf_op jit(solution)/shard_map/pallas_call | solution.py:499
  34.5 0.8 %copy.8 = f32[4,32,1024]{2,1,0:T(8,128)} copy(f32[4,32,1024]{2,1,0:T(8,128)S(1)} %get-tuple-element.4) | data formatting | bytes 1048576
  35.3 0.8 %copy.9 = f32[4,32,1024]{2,1,0:T(8,128)} copy(f32[4,32,1024]{2,1,0:T(8,128)S(1)} %get-tuple-element.5) | data formatting | bytes 1048576

commit v3 on v2

--- a/solution.py
+++ b/solution.py
@@ -47,12 +47,17 @@
 
 
 def coefficients(c, besides, inside):
-    total = 3.0 * c
-    for beside, within in zip(besides, inside):
-        total = total + 0.5 * jnp.where(within, beside, c)
+    around_ = [
+        beside if within is None else jnp.where(within, beside, c)
+        for beside, within in zip(besides, inside)
+    ]
+    total = 3.0 * c + 0.5 * (
+        (around_[0] + around_[1]) + (around_[2] + around_[3]) + (around_[4] + around_[5])
+    )
     quarter = 0.4 / total
     faces = [
-        jnp.where(within, (c + beside) * quarter, 0.0) for beside, within in zip(besides, inside)
+        (c + beside) * quarter if within is None else jnp.where(within, (c + beside) * quarter, 0.0)
+        for beside, within in zip(besides, inside)
     ]
     return faces, total, quarter
 
@@ -74,14 +79,18 @@
     return (parts[0] + parts[1]) + (parts[2] + parts[3]) + (parts[4] + parts[5])
 
 
-def loop(low, high, width, body):
+def loop(low, high, width, body, late=True):
     assert (high - low) % width == 0
 
     def step(index, carry):
         first = low + index * width
-        stores = [item for m in range(width) for item in body(first + m)]
-        for ref, at, value in stores:
-            ref[at] = value
+        stores = []
+        for m in range(width):
+            stores += body(first + m)
+            if not late or m == width - 1:
+                for ref, index_, value in stores:
+                    ref[index_] = value
+                stores = []
         return carry
 
     if high - low == width:
@@ -134,6 +143,13 @@
         copy.start()
         used.append(copy)
         return copy
+
+    sent_upto = [0]
+
+    def drain():
+        for copy in used[sent_upto[0] :]:
+            copy.wait_send()
+        sent_upto[0] = len(used)
 
     raws = (raw_c, raw_u, raw_s)
     given = (conductance, initial, source)
@@ -190,8 +206,15 @@
     def far(first, count, side, depth):
         return first + count - 1 + depth if side < 0 else first - depth
 
-    def pieces(strips, corners, da, dj, pick):
+    own2 = R2 + 2 * R2 + 8
+
+    def there2(da, dj):
+        return R2 + R2 * (2 - dj) + 8 * (1 - da)
+
+    def pieces(strips, corners, block, da, dj, pick):
         out = []
+        if block is not None:
+            out.append((block, own2 if pick is near else there2(da, dj), 8, 1))
         if da == 0:
             for ref, level, depths in strips:
                 plane, planes, row, rows = OWN[level]
@@ -216,7 +239,7 @@
 
     spare = list(post)
 
-    def exchange(strips, corners):
+    def exchange(strips, corners, block=None):
         boxes = [(spare.pop(0), spare.pop(0)) for _ in range(3)]
         started = []
         for number, (da, dj) in enumerate(FULL):
@@ -224,7 +247,7 @@
             slot = number % 2 if number < 4 else number - 4
             out, got = boxes[kind]
             offset = 0
-            for ref, first, count, stride in pieces(strips, corners, da, dj, near):
+            for ref, first, count, stride in pieces(strips, corners, block, da, dj, near):
                 out[slot, pl.ds(offset, count), :] = ref[slab(ref, first, count, stride)]
                 offset += count
             started.append((send(out.at[slot], got.at[slot], device(da, dj)), got, slot, da, dj))
@@ -233,7 +256,7 @@
             for copy, got, slot, da, dj in started:
                 copy.wait_recv()
                 offset = 0
-                for ref, first, count, stride in pieces(strips, corners, da, dj, far):
+                for ref, first, count, stride in pieces(strips, corners, block, da, dj, far):
                     ref[slab(ref, first, count, stride)] = got[slot, pl.ds(offset, count), :]
                     offset += count
 
@@ -244,6 +267,12 @@
 
     bring(0, cf)
     land_c = exchange(((cf, 0, (1, 2, 3)),), fine_corner(cf, 3))
+
+    bring(1, uf)
+    bring(2, sf)
+    land_u = exchange(
+        ((uf, 0, (1, 2, 3)), (sf, 0, (1, 2))), fine_corner(uf, 3) + fine_corner(sf, 2)
+    )
 
     def coarse_c(i):
         total = pair_rows(cf, (4 + 2 * i) * RF + 8, 16, RF)
@@ -259,48 +288,57 @@
             total = total + jnp.where(lanes == i, value, 0.0)
         return total
 
-    own2 = R2 + 2 * R2 + 8
-
-    def blocks2(ref):
-        sent = []
-        for da, dj in FAR + FULL:
-            row = R2 + R2 * (2 - dj) + 8 * (1 - da)
-            sent.append(send(ref.at[pl.ds(own2, 8)], ref.at[pl.ds(row, 8)], device(da, dj)))
-        return sent
-
-    bring(1, uf)
-    bring(2, sf)
-    land_u = exchange(
-        ((uf, 0, (1, 2, 3)), (sf, 0, (1, 2))), fine_corner(uf, 3) + fine_corner(sf, 2)
-    )
+    def blocks2(ref, where):
+        return [
+            send(ref.at[pl.ds(own2, 8)], ref.at[pl.ds(there2(da, dj), 8)], device(da, dj))
+            for da, dj in where
+        ]
+
     c2[pl.ds(own2, 8), :] = packed(c1)
-    land_c1 = exchange(((c1, 1, (1, 2, 3, 4, 5, 6)),), [(c1, 1, d, 1, 6 - d) for d in range(1, 6)])
-    third = blocks2(c2)
+    land_c1 = exchange(
+        ((c1, 1, (1, 2, 3, 4, 5, 6)),), [(c1, 1, d, 1, 6 - d) for d in range(1, 6)], c2
+    )
+    third = blocks2(c2, FAR)
 
     land_c()
+
+    def edges(ref, first, side, count, rows, plane, row, low_y, high_y, low_x, high_x):
+        for outside, there, here in (
+            (low_y, plane - 1, plane), (high_y, plane + count, plane + count - 1)
+        ):
+            slab_there = at(there * rows + first, side)
+            ref[slab_there] = jnp.where(outside, ref[at(here * rows + first, side)], ref[slab_there])
+        lines = 24
+        for outside, there, here in ((low_x, row[0] - 1, row[0]), (high_x, row[1] + 1, row[1])):
+            slab_there = slab(ref, there, lines, rows)
+            ref[slab_there] = jnp.where(outside, ref[slab(ref, here, lines, rows)], ref[slab_there])
+
+    def cut(faces, first, side, count, rows, plane, row, low_y, high_y, low_x, high_x):
+        for n, outside, here in ((0, low_y, plane), (1, high_y, plane + count - 1)):
+            where = (n,) + at(here * rows + first, side)
+            faces[where] = jnp.where(outside, 0.0, faces[where])
+        for n, outside, here in ((2, low_x, row[0]), (3, high_x, row[1])):
+            where = (n,) + slab(faces, here, 24, rows)
+            faces[where] = jnp.where(outside, 0.0, faces[where])
+
+    ends = (j == 0, j == 7, a == 0, a == 15)
+    edges(cf, 4, 40, 16, RF, 4, (8, 39), *ends)
     fine_faces = [fine.at[n] for n in range(6)]
 
     def fine_coeffs(p):
         base = p * RF + 4
         centre, besides = around(cf, base, 40, RF, 1)
-        x = row_ids(40) + (32 * a - 4)
-        y = 16 * j + p - 4
         z = lane_ids(40)
-        inside = (y != 0, y != 127, x != 0, x != 511, z != 0, z != 127)
+        inside = (None, None, None, None, z != 0, z != 127)
         faces, total, quarter = coefficients(centre, besides, inside)
         out = [(fine, (n,) + at(base, 40), faces[n]) for n in range(6)]
         out.append((gf, at(base, 40), 2.0 * quarter))
         out.append((df, at(base, 40), 1.25 * total))
         return out
 
-    loop(2, 22, 2, fine_coeffs)
+    loop(2, 22, 2, fine_coeffs, late=False)
+    cut(fine, 4, 40, 16, RF, 4, (8, 39), *ends)
     land_u()
-
-    def fine_right(p):
-        base = p * RF + 4
-        return [(gf, at(base, 40), gf[pl.ds(base, 40), :] * sf[pl.ds(base, 40), :])]
-
-    loop(2, 22, 4, fine_right)
 
     def sweep(src, dst, faces, right, low, high, width, rows, start, count, twist):
         def step(p):
@@ -322,7 +360,14 @@
 
         loop(low, high, width, step)
 
-    sweep(uf, u1, fine_faces, gf, 2, 22, 5, RF, 4, 40, 1)
+    def first_sweep(p):
+        base = p * RF + 4
+        centre, besides = around(uf, base, 40, RF, 1)
+        right = gf[pl.ds(base, 40), :] * sf[pl.ds(base, 40), :]
+        value = 0.2 * centre + right + weighted(fine_faces, base, 40, besides)
+        return [(u1, at(base, 40), value), (gf, at(base, 40), right)]
+
+    loop(2, 22, 4, first_sweep)
     sweep(u1, u2, fine_faces, gf, 3, 21, 6, RF, 4, 40, 1)
     leftover(u2, u1, fine_faces, gf, df, 4, 20, 4, RF, 8, 32, 1)
 
@@ -337,23 +382,24 @@
         [(f1, 1, 1, 2, 3), (f1, 1, 2, 1, 3), (f1, 1, 3, 1, 2), (f1, 1, 4, 1, 1)] + fine_corner(u2, 3),
     )
 
+    drain()
     land_c1()
+    edges(c1, 0, 32, 8, R1, 8, (8, 23), *ends)
     mid_faces = [mid.at[n] for n in range(6)]
 
     def mid_coeffs(p):
         base = p * R1
         centre, besides = around(c1, base, 32, R1, 2)
-        x = row_ids(32) + (16 * a - 8)
-        y = 8 * j + p - 8
         z = lane_ids(32)
-        inside = (y != 0, y != 63, x != 0, x != 255, z >= 2, z < 126)
+        inside = (None, None, None, None, z >= 2, z < 126)
         faces, total, quarter = coefficients(centre, besides, inside)
         out = [(mid, (n,) + at(base, 32), faces[n]) for n in range(6)]
         out.append((w1, at(base, 32), 8.0 * quarter))
         out.append((d1, at(base, 32), 0.3125 * total))
         return out
 
-    loop(3, 21, 3, mid_coeffs)
+    loop(3, 21, 3, mid_coeffs, late=False)
+    cut(mid, 0, 32, 8, R1, 8, (8, 23), *ends)
 
     for copy in third:
         copy.wait_recv()
@@ -389,12 +435,13 @@
     sweep(g1, e1, mid_faces, g1, 7, 17, 10, R1, 4, 24, 2)
     leftover(e1, r1, mid_faces, g1, d1, 8, 16, 8, R1, 8, 16, 2)
     f2[pl.ds(own2, 8), :] = packed(r1)
-    sixth = blocks2(f2)
+    sixth = blocks2(f2, FAR + FULL)
 
     land_rest()
     loop(3, 21, 9, guess)
     sweep(g1, e1, mid_faces, g1, 4, 20, 8, R1, 4, 24, 2)
 
+    drain()
     for copy in sixth:
         copy.wait_recv()
     g2[...] = deep[6] * f2[R2 : 6 * R2, :]
@@ -436,13 +483,12 @@
 
     loop(1, 23, 2, corrected0)
     sweep(u2, u1, fine_faces, gf, 2, 22, 5, RF, 4, 40, 1)
-    sweep(u1, u2, fine_faces, gf, 3, 21, 6, RF, 4, 40, 1)
-
-    def give(ref, stage, other):
+
+    def give(ref, stage, other, quads):
         def step(t):
             rows = pl.ds(pl.multiple_of(8 * t, 8), 8)
             out = []
-            for q in range(4):
+            for q in quads:
                 four = [
                     ref[pl.ds(pl.multiple_of((4 + 4 * q + i) * RF + 8 + 8 * t, 8), 8), :]
                     for i in range(4)
@@ -451,8 +497,9 @@
                     out.append((stage, (p, rows, slice(128 * q, 128 * q + 128)), value))
             return out
 
-        loop(0, 4, 2, step)
-        return send(stage.at[pl.ds(1 - half, 3)], other, sibling)
+        loop(0, 4, 4, step)
+        lanes = pl.ds(128 * quads[0], 128 * len(quads))
+        return send(stage.at[pl.ds(1 - half, 3), :, lanes], other.at[:, :, lanes], sibling)
 
     own = jnp.where(half == 0, split, 4 - split)
 
@@ -460,20 +507,26 @@
         for s in range(4):
             out[s, :, mine] = jnp.where(s < own, stage[jnp.clip(s + half * split, 0, 3)], 0.0)
 
-    def take(copy, other, out):
-        copy.wait_recv()
+    def take(copies, other, out):
+        for copy in copies:
+            copy.wait_recv()
         for s in range(4):
             out[s, :, theirs] = jnp.where(s < own, other[jnp.clip(s + half * (split - 1), 0, 2)], 0.0)
 
-    last_f = give(u2, stage_f, other_f)
-    leftover(u2, u1, fine_faces, gf, df, 4, 20, 4, RF, 8, 32, 1)
-    last_r = give(u1, stage_r, other_r)
+    last_f, last_r = [], []
+    sweep(u1, u2, fine_faces, gf, 3, 12, 3, RF, 4, 40, 1)
+    last_f.append(give(u2, stage_f, other_f, (0, 1)))
+    sweep(u1, u2, fine_faces, gf, 12, 21, 3, RF, 4, 40, 1)
+    last_f.append(give(u2, stage_f, other_f, (2, 3)))
+    leftover(u2, u1, fine_faces, gf, df, 4, 12, 4, RF, 8, 32, 1)
+    last_r.append(give(u1, stage_r, other_r, (0, 1)))
+    leftover(u2, u1, fine_faces, gf, df, 12, 20, 4, RF, 8, 32, 1)
+    last_r.append(give(u1, stage_r, other_r, (2, 3)))
     keep(stage_f, out_field)
     take(last_f, other_f, out_field)
     keep(stage_r, out_resid)
     take(last_r, other_r, out_resid)
-    for copy in used:
-        copy.wait_send()
+    drain()
 
 
 def vmem(*shape):
@@ -489,10 +542,10 @@
     scratch += [mid_field] * 4 + [vmem(8 * 32, LANES), vmem(6, P1 * R1, LANES)] + [mid_field] * 4
     scratch += [deep_field] * 4 + [vmem(7, 5 * R2, LANES), vmem(5 * R2, LANES), vmem(12 * RF, LANES)]
     scratch += [vmem(4, 32, 512)] * 2 + [vmem(3, 32, 512)] * 2
-    for big, middle, small in ((96, 48, 8), (160, 80, 8), (96, 48, 16), (32, 16, 8), (144, 72, 16)):
+    for big, middle, small in ((96, 48, 8), (160, 80, 8), (104, 56, 24), (32, 16, 8), (144, 72, 16)):
         for count, rows in ((2, big), (2, middle), (4, small)):
             scratch += [vmem(count, rows, LANES)] * 2
-    messages = 3 + 5 * 8 + 2 * 14 + 2
+    messages = 3 + 5 * 8 + 6 + 14 + 4
     scratch += [pltpu.SemaphoreType.DMA((4,))] + [pltpu.SemaphoreType.DMA((messages,))] * 2
     hbm = pl.BlockSpec(memory_space=pltpu.HBM)
     shape = jax.ShapeDtypeStruct(source.shape, source.dtype)

time: 36.2 us -> 36.1 us (level)
  no operation moved by 1% of the time
where the time goes in v3:
time: 36.1 us; the launch traced here: 36 us
  Pallas kernels  33.8 us (94%)
  local copies, waits for them, and re-layouts  1.59 us (4%)
  between operations  0.64 us (2%)
    pallas_call x1, Pallas kernels, body(): pl.pallas_call(kernel, out_shape=(shape, shape), in_specs=[hbm] * 4, out_...  33.8 us
    unnamed x2, local copies, waits for them, and re-layouts  1.59 us

profile of v3, /device:TPU:1, one launch (start us, length us, event | category | flops | bytes accessed | tf_op | source)
XLA Modules:
  0.0 36.0 jit_solution(6760847969267795760)
XLA Ops:
  0.6 33.8 %shard_map.59 = (f32[4,32,1024]{2,1,0:T(8,128)S(1)}, f32[4,32,1024]{2,1,0:T(8,128)S(1)}) custom-call(s32[128]{0:T(128)} %counts.1, f32[4,32,1024]{2,1,0:T(8,128)} %source.1, f32[4,32,1024]{2,1,0:T(8,128)} %conductance.1, f32[4,32,1024]{2,1,0:T(8,128)} %initial.1), custom_call_target="tpu_custom_call" | custom-call | flops 30000000 | bytes 3000000 | tf_op jit(solution)/shard_map/pallas_call | solution.py:552
  34.4 0.8 %copy.8 = f32[4,32,1024]{2,1,0:T(8,128)} copy(f32[4,32,1024]{2,1,0:T(8,128)S(1)} %get-tuple-element.4) | data formatting | bytes 1048576
  35.2 0.8 %copy.9 = f32[4,32,1024]{2,1,0:T(8,128)} copy(f32[4,32,1024]{2,1,0:T(8,128)S(1)} %get-tuple-element.5) | data formatting | bytes 1048576

commit v4 on v3

--- a/solution.py
+++ b/solution.py
@@ -79,15 +79,16 @@
     return (parts[0] + parts[1]) + (parts[2] + parts[3]) + (parts[4] + parts[5])
 
 
-def loop(low, high, width, body, late=True):
+def loop(low, high, width, body, group=None):
     assert (high - low) % width == 0
+    group = group or width
 
     def step(index, carry):
         first = low + index * width
         stores = []
         for m in range(width):
             stores += body(first + m)
-            if not late or m == width - 1:
+            if (m + 1) % group == 0 or m == width - 1:
                 for ref, index_, value in stores:
                     ref[index_] = value
                 stores = []
@@ -116,7 +117,7 @@
 
 
 def kernel(
-    counts, source, conductance, initial, out_field, out_resid,
+    counts, source, conductance, initial, out_field, out_resid, out_held,
     owners, raw_c, raw_u, raw_s, cf, uf, sf, u1, u2, fine, gf, df,
     c1, f1, e1, e1b, pe2, mid, w1, g1, d1, r1, c2, f2, e2, e2b, deep, g2, pe1,
     stage_f, stage_r, other_f, other_r, *rest,
@@ -151,8 +152,8 @@
             copy.wait_send()
         sent_upto[0] = len(used)
 
-    raws = (raw_c, raw_u, raw_s)
-    given = (conductance, initial, source)
+    raws = (raw_c, raw_s, raw_u)
+    given = (conductance, source, initial)
     mine = pl.ds(pl.multiple_of(512 * half, 512), 512)
     theirs = pl.ds(pl.multiple_of(512 - 512 * half, 512), 512)
     held = pl.ds(3 * half, 3)
@@ -179,6 +180,9 @@
     ]
     locals_[0].wait()
     split = owners[me - half]
+    own = jnp.where(half == 0, split, 4 - split)
+    for s in range(4):
+        out_held[s] = jnp.where(s < own, jnp.ones((32, 1024), F32), 0.0)
     places = [jnp.where(p < split, p, jnp.clip(3 + p - split, 0, 5)) for p in range(4)]
 
     def bring(number, ref):
@@ -266,13 +270,12 @@
         return [(ref, 0, d, 1, depth - d) for d in range(1, depth)]
 
     bring(0, cf)
-    land_c = exchange(((cf, 0, (1, 2, 3)),), fine_corner(cf, 3))
-
-    bring(1, uf)
-    bring(2, sf)
-    land_u = exchange(
-        ((uf, 0, (1, 2, 3)), (sf, 0, (1, 2))), fine_corner(uf, 3) + fine_corner(sf, 2)
-    )
+    bring(1, sf)
+    land_c = exchange(
+        ((cf, 0, (1, 2, 3)), (sf, 0, (1, 2))), fine_corner(cf, 3) + fine_corner(sf, 2)
+    )
+    bring(2, uf)
+    land_u = exchange(((uf, 0, (1, 2, 3)),), fine_corner(uf, 3))
 
     def coarse_c(i):
         total = pair_rows(cf, (4 + 2 * i) * RF + 8, 16, RF)
@@ -336,7 +339,7 @@
         out.append((df, at(base, 40), 1.25 * total))
         return out
 
-    loop(2, 22, 2, fine_coeffs, late=False)
+    loop(2, 22, 4, fine_coeffs, group=1)
     cut(fine, 4, 40, 16, RF, 4, (8, 39), *ends)
     land_u()
 
@@ -347,7 +350,7 @@
             value = 0.2 * centre + right[pl.ds(base, count), :] + weighted(faces, base, count, besides)
             return [(dst, at(base, count), value)]
 
-        loop(low, high, width, step)
+        loop(low, high, width, step, group=5)
 
     def leftover(src, dst, faces, right, diag, low, high, width, rows, start, count, twist):
         def step(p):
@@ -358,7 +361,7 @@
             )
             return [(dst, at(base, count), value)]
 
-        loop(low, high, width, step)
+        loop(low, high, width, step, group=4)
 
     def first_sweep(p):
         base = p * RF + 4
@@ -367,9 +370,9 @@
         value = 0.2 * centre + right + weighted(fine_faces, base, 40, besides)
         return [(u1, at(base, 40), value), (gf, at(base, 40), right)]
 
-    loop(2, 22, 4, first_sweep)
-    sweep(u1, u2, fine_faces, gf, 3, 21, 6, RF, 4, 40, 1)
-    leftover(u2, u1, fine_faces, gf, df, 4, 20, 4, RF, 8, 32, 1)
+    loop(2, 22, 10, first_sweep, group=5)
+    sweep(u1, u2, fine_faces, gf, 3, 21, 9, RF, 4, 40, 1)
+    leftover(u2, u1, fine_faces, gf, df, 4, 20, 8, RF, 8, 32, 1)
 
     def coarse_f(i):
         total = pair_rows(u1, (4 + 2 * i) * RF + 8, 16, RF)
@@ -398,7 +401,7 @@
         out.append((d1, at(base, 32), 0.3125 * total))
         return out
 
-    loop(3, 21, 3, mid_coeffs, late=False)
+    loop(3, 21, 3, mid_coeffs, group=1)
     cut(mid, 0, 32, 8, R1, 8, (8, 23), *ends)
 
     for copy in third:
@@ -467,22 +470,22 @@
         value = e1[pl.ds(p * R1 + 4, 24), :] + pe2[pl.ds((p // 2 - 2) * 32 + 4, 24), :]
         return [(e1, at(p * R1 + 4, 24), value)]
 
-    loop(4, 20, 8, corrected1)
-    sweep(e1, e1b, mid_faces, g1, 5, 19, 7, R1, 4, 24, 2)
-    sweep(e1b, e1, mid_faces, g1, 6, 18, 6, R1, 4, 24, 2)
+    loop(4, 20, 16, corrected1)
+    sweep(e1, e1b, mid_faces, g1, 5, 19, 14, R1, 4, 24, 2)
+    sweep(e1b, e1, mid_faces, g1, 6, 18, 12, R1, 4, 24, 2)
 
     def grown(i):
         value = e1[pl.ds((i + 6) * R1 + 4, 24), :]
         return [(pe1, (pl.ds(RF * i + odd, 24, stride=2), slice(None)), value) for odd in (0, 1)]
 
-    loop(0, 12, 6, grown)
+    loop(0, 12, 12, grown)
 
     def corrected0(p):
         base = p * RF + 4
         return [(u2, at(base, 40), u2[pl.ds(base, 40), :] + pe1[pl.ds((p // 2) * RF + 4, 40), :])]
 
-    loop(1, 23, 2, corrected0)
-    sweep(u2, u1, fine_faces, gf, 2, 22, 5, RF, 4, 40, 1)
+    loop(1, 23, 11, corrected0)
+    sweep(u2, u1, fine_faces, gf, 2, 22, 10, RF, 4, 40, 1)
 
     def give(ref, stage, other, quads):
         def step(t):
@@ -501,26 +504,24 @@
         lanes = pl.ds(128 * quads[0], 128 * len(quads))
         return send(stage.at[pl.ds(1 - half, 3), :, lanes], other.at[:, :, lanes], sibling)
 
-    own = jnp.where(half == 0, split, 4 - split)
-
     def keep(stage, out):
         for s in range(4):
-            out[s, :, mine] = jnp.where(s < own, stage[jnp.clip(s + half * split, 0, 3)], 0.0)
+            out[s, :, mine] = stage[jnp.clip(s + half * split, 0, 3)]
 
     def take(copies, other, out):
         for copy in copies:
             copy.wait_recv()
         for s in range(4):
-            out[s, :, theirs] = jnp.where(s < own, other[jnp.clip(s + half * (split - 1), 0, 2)], 0.0)
+            out[s, :, theirs] = other[jnp.clip(s + half * (split - 1), 0, 2)]
 
     last_f, last_r = [], []
-    sweep(u1, u2, fine_faces, gf, 3, 12, 3, RF, 4, 40, 1)
+    sweep(u1, u2, fine_faces, gf, 3, 12, 9, RF, 4, 40, 1)
     last_f.append(give(u2, stage_f, other_f, (0, 1)))
-    sweep(u1, u2, fine_faces, gf, 12, 21, 3, RF, 4, 40, 1)
+    sweep(u1, u2, fine_faces, gf, 12, 21, 9, RF, 4, 40, 1)
     last_f.append(give(u2, stage_f, other_f, (2, 3)))
-    leftover(u2, u1, fine_faces, gf, df, 4, 12, 4, RF, 8, 32, 1)
+    leftover(u2, u1, fine_faces, gf, df, 4, 12, 8, RF, 8, 32, 1)
     last_r.append(give(u1, stage_r, other_r, (0, 1)))
-    leftover(u2, u1, fine_faces, gf, df, 12, 20, 4, RF, 8, 32, 1)
+    leftover(u2, u1, fine_faces, gf, df, 12, 20, 8, RF, 8, 32, 1)
     last_r.append(give(u1, stage_r, other_r, (2, 3)))
     keep(stage_f, out_field)
     take(last_f, other_f, out_field)
@@ -542,24 +543,25 @@
     scratch += [mid_field] * 4 + [vmem(8 * 32, LANES), vmem(6, P1 * R1, LANES)] + [mid_field] * 4
     scratch += [deep_field] * 4 + [vmem(7, 5 * R2, LANES), vmem(5 * R2, LANES), vmem(12 * RF, LANES)]
     scratch += [vmem(4, 32, 512)] * 2 + [vmem(3, 32, 512)] * 2
-    for big, middle, small in ((96, 48, 8), (160, 80, 8), (104, 56, 24), (32, 16, 8), (144, 72, 16)):
+    for big, middle, small in ((160, 80, 8), (96, 48, 8), (104, 56, 24), (32, 16, 8), (144, 72, 16)):
         for count, rows in ((2, big), (2, middle), (4, small)):
             scratch += [vmem(count, rows, LANES)] * 2
     messages = 3 + 5 * 8 + 6 + 14 + 4
     scratch += [pltpu.SemaphoreType.DMA((4,))] + [pltpu.SemaphoreType.DMA((messages,))] * 2
     hbm = pl.BlockSpec(memory_space=pltpu.HBM)
     shape = jax.ShapeDtypeStruct(source.shape, source.dtype)
-    return pl.pallas_call(
+    field, resid, held = pl.pallas_call(
         kernel,
-        out_shape=(shape, shape),
+        out_shape=(shape,) * 3,
         in_specs=[hbm] * 4,
-        out_specs=(pl.BlockSpec(memory_space=pltpu.VMEM),) * 2,
+        out_specs=(pl.BlockSpec(memory_space=pltpu.VMEM),) * 3,
         scratch_shapes=scratch,
         compiler_params=pltpu.CompilerParams(
             collective_id=0, has_side_effects=True, vmem_limit_bytes=40 * 2**20
         ),
         cost_estimate=pl.CostEstimate(flops=3 * 10**7, bytes_accessed=3 * 10**6, transcendentals=0),
     )(*[pltpu.with_memory_space_constraint(x, pltpu.HBM) for x in (box_counts, source, conductance, initial)])
+    return jnp.where(held > 0.0, field, 0.0), jnp.where(held > 0.0, resid, 0.0)
 
 
 def solution(mesh):

time: 36.1 us -> 35.3 us (0.978)
  other arithmetic: 0 us -> 1.78 us
  local copies, waits for them, and re-layouts: 1.59 us -> 0 us
  Pallas kernels: 33.8 us -> 32.8 us
    select_n x0 -> x2, other arithmetic: none -> 1.78 us  [the longest x1 0.92 us: body(): jnp.where(held > 0.0, resid, 0.0)]
    unnamed x2 -> x0, local copies, waits for them, and re-layouts: 1.59 us -> none
    pallas_call x1, Pallas kernels: 33.8 us -> 32.8 us  [body(): pl.pallas_call(kernel, out_shape=(shape,) * 3, in_specs=[hbm] * 4, out_sp...]
where the time goes in v4:
time: 35.3 us; the launch traced here: 35.2 us
  Pallas kernels  32.8 us (93%)
  other arithmetic  1.78 us (5%)
  between operations  0.64 us (2%)
    pallas_call x1, Pallas kernels, body(): pl.pallas_call(kernel, out_shape=(shape,) * 3, in_specs=[hbm] * 4, out_sp...  32.8 us
    select_n x1, other arithmetic, body(): jnp.where(held > 0.0, resid, 0.0)  0.92 us
    select_n x1, other arithmetic, body(): jnp.where(held > 0.0, field, 0.0)  0.86 us

profile of v4, /device:TPU:1, one launch (start us, length us, event | category | flops | bytes accessed | tf_op | source)
XLA Modules:
  0.0 35.2 jit_solution(7794039723450428811)
XLA Ops:
  0.6 32.8 %shard_map.59 = (f32[4,32,1024]{2,1,0:T(8,128)S(1)}, f32[4,32,1024]{2,1,0:T(8,128)S(1)}, f32[4,32,1024]{2,1,0:T(8,128)S(1)}) custom-call(s32[128]{0:T(128)} %counts.1, f32[4,32,1024]{2,1,0:T(8,128)} %source.1, f32[4,32,1024]{2,1,0:T(8,128)} %conductance.1, f32[4,32,1024]{2,1,0:T(8,128)} %initial.1), custom_call_target="tpu_custom_call" | custom-call | flops 30000000 | bytes 3000000 | tf_op jit(solution)/shard_map/pallas_call | solution.py:553
  33.4 0.9 %broadcast_select_fusion = (f32[4,32,1024]{2,1,0:T(8,128)}, pred[4,32,1024]{2,1,0:T(8,128)(4,1)S(1)}) fusion(f32[4,32,1024]{2,1,0:T(8,128)S(1)} %get-tuple-element.7, f32[4,32,1024]{2,1,0:T(8,128)S(1)} %get-tuple-element.5), kind=kLoop, calls=%fused_computation | loop fusion | flops 262144 | bytes 1703936 | tf_op jit(solution)/shard_map/jit(_where)/select_n | solution.py:564
  34.3 0.9 %broadcast_select_fusion.1 = f32[4,32,1024]{2,1,0:T(8,128)} fusion(pred[4,32,1024]{2,1,0:T(8,128)(4,1)S(1)} %get-tuple-element.9, f32[4,32,1024]{2,1,0:T(8,128)S(1)} %get-tuple-element.6), kind=kLoop, calls=%fused_computation.1 | loop fusion | flops 131072 | bytes 1179648 | tf_op jit(solution)/shard_map/jit(_where)/select_n | solution.py:564

commit v5 on v4

--- a/solution.py
+++ b/solution.py
@@ -12,9 +12,10 @@
 R1, P1 = 32, 24
 R2 = 24
 LANES = 128
-FULL = (1, 0), (-1, 0), (0, 1), (0, -1), (1, 1), (1, -1), (-1, 1), (-1, -1)
-FAR = (0, 2), (0, -2), (1, 2), (1, -2), (-1, 2), (-1, -2)
+FULL = (1, 1), (1, -1), (-1, 1), (-1, -1), (1, 0), (-1, 0), (0, 1), (0, -1)
+FAR = (1, 2), (1, -2), (-1, 2), (-1, -2), (0, 2), (0, -2)
 F32 = jnp.float32
+ROUNDS = 3 + 5 + 2 + 4
 
 
 def lane_ids(rows):
@@ -133,24 +134,26 @@
     def device(da, dj):
         return across[da] + along[dj]
 
-    used = []
-
-    def send(src, dst, target):
-        number = len(used)
-        copy = pltpu.make_async_remote_copy(
+    numbers = iter(range(ROUNDS))
+    leaving = []
+
+    def describe(src, dst, number, target):
+        return pltpu.make_async_remote_copy(
             src_ref=src, dst_ref=dst, send_sem=send_sem.at[number], recv_sem=recv_sem.at[number],
             device_id=(target,), device_id_type=pl.DeviceIdType.MESH,
         )
-        copy.start()
-        used.append(copy)
-        return copy
-
-    sent_upto = [0]
+
+    def start(copies, whole):
+        number = next(numbers)
+        for src, dst, target in copies:
+            describe(src, dst, number, target).start()
+        everything = describe(whole, whole, number, sibling)
+        leaving.append(everything.wait_send)
+        return everything.wait_recv
 
     def drain():
-        for copy in used[sent_upto[0] :]:
-            copy.wait_send()
-        sent_upto[0] = len(used)
+        while leaving:
+            leaving.pop(0)()
 
     raws = (raw_c, raw_s, raw_u)
     given = (conductance, source, initial)
@@ -175,7 +178,10 @@
     pl.semaphore_wait(barrier, len(FULL + FAR))
 
     swaps = [
-        send(given[number].at[pl.ds(0, 3), :, theirs], raws[number].at[held], sibling)
+        start(
+            [(given[number].at[pl.ds(0, 3), :, theirs], raws[number].at[held], sibling)],
+            raws[number].at[held],
+        )
         for number in range(3)
     ]
     locals_[0].wait()
@@ -187,7 +193,7 @@
 
     def bring(number, ref):
         locals_[1 + number].wait()
-        swaps[number].wait_recv()
+        swaps[number]()
         raw = raws[number]
 
         def step(t):
@@ -199,7 +205,7 @@
                     out.append((ref, at(pl.multiple_of((4 + 4 * q + i) * RF + 8 + 8 * t, 8), 8), value))
             return out
 
-        loop(0, 4, 2, step)
+        loop(0, 4, 4, step, group=1)
 
     ROWS = (RF, R1)
     OWN = ((4, 16, 8, 32), (8, 8, 8, 16))
@@ -244,24 +250,26 @@
     spare = list(post)
 
     def exchange(strips, corners, block=None):
-        boxes = [(spare.pop(0), spare.pop(0)) for _ in range(3)]
-        started = []
-        for number, (da, dj) in enumerate(FULL):
-            kind = 2 if da and dj else 1 if da else 0
-            slot = number % 2 if number < 4 else number - 4
-            out, got = boxes[kind]
-            offset = 0
+        out, got = spare.pop(0), spare.pop(0)
+        copies, filled = [], []
+        offset = 0
+        for da, dj in FULL:
+            first_row = offset
             for ref, first, count, stride in pieces(strips, corners, block, da, dj, near):
-                out[slot, pl.ds(offset, count), :] = ref[slab(ref, first, count, stride)]
+                out[pl.ds(offset, count), :] = ref[slab(ref, first, count, stride)]
                 offset += count
-            started.append((send(out.at[slot], got.at[slot], device(da, dj)), got, slot, da, dj))
+            offset += -offset % 8
+            rows = pl.ds(first_row, offset - first_row)
+            copies.append((out.at[rows], got.at[rows], device(da, dj)))
+            filled.append((first_row, da, dj))
+        assert out.shape == (offset, LANES)
+        arrived = start(copies, got)
 
         def land():
-            for copy, got, slot, da, dj in started:
-                copy.wait_recv()
-                offset = 0
+            arrived()
+            for offset, da, dj in filled:
                 for ref, first, count, stride in pieces(strips, corners, block, da, dj, far):
-                    ref[slab(ref, first, count, stride)] = got[slot, pl.ds(offset, count), :]
+                    ref[slab(ref, first, count, stride)] = got[pl.ds(offset, count), :]
                     offset += count
 
         return land
@@ -292,10 +300,11 @@
         return total
 
     def blocks2(ref, where):
-        return [
-            send(ref.at[pl.ds(own2, 8)], ref.at[pl.ds(there2(da, dj), 8)], device(da, dj))
+        copies = [
+            (ref.at[pl.ds(own2, 8)], ref.at[pl.ds(there2(da, dj), 8)], device(da, dj))
             for da, dj in where
         ]
+        return start(copies, ref.at[pl.ds(0, 8 * len(where))])
 
     c2[pl.ds(own2, 8), :] = packed(c1)
     land_c1 = exchange(
@@ -404,8 +413,7 @@
     loop(3, 21, 3, mid_coeffs, group=1)
     cut(mid, 0, 32, 8, R1, 8, (8, 23), *ends)
 
-    for copy in third:
-        copy.wait_recv()
+    third()
 
     def around2(ref):
         lanes = lane_ids(5 * R2) % 4
@@ -445,8 +453,7 @@
     sweep(g1, e1, mid_faces, g1, 4, 20, 8, R1, 4, 24, 2)
 
     drain()
-    for copy in sixth:
-        copy.wait_recv()
+    sixth()
     g2[...] = deep[6] * f2[R2 : 6 * R2, :]
     e2[R2 : 6 * R2, :] = g2[...]
     for src, dst in ((e2, e2b), (e2b, e2), (e2, e2b)):
@@ -502,31 +509,33 @@
 
         loop(0, 4, 4, step)
         lanes = pl.ds(128 * quads[0], 128 * len(quads))
-        return send(stage.at[pl.ds(1 - half, 3), :, lanes], other.at[:, :, lanes], sibling)
+        return stage.at[pl.ds(1 - half, 3), :, lanes], other.at[:, :, lanes], sibling
 
     def keep(stage, out):
         for s in range(4):
             out[s, :, mine] = stage[jnp.clip(s + half * split, 0, 3)]
 
-    def take(copies, other, out):
-        for copy in copies:
-            copy.wait_recv()
+    def take(other, out):
         for s in range(4):
             out[s, :, theirs] = other[jnp.clip(s + half * (split - 1), 0, 2)]
 
-    last_f, last_r = [], []
+    last = []
     sweep(u1, u2, fine_faces, gf, 3, 12, 9, RF, 4, 40, 1)
-    last_f.append(give(u2, stage_f, other_f, (0, 1)))
+    last.append(start([give(u2, stage_f, other_f, (0, 1))], other_f.at[:, :, pl.ds(0, 256)]))
     sweep(u1, u2, fine_faces, gf, 12, 21, 9, RF, 4, 40, 1)
-    last_f.append(give(u2, stage_f, other_f, (2, 3)))
+    last.append(start([give(u2, stage_f, other_f, (2, 3))], other_f.at[:, :, pl.ds(256, 256)]))
     leftover(u2, u1, fine_faces, gf, df, 4, 12, 8, RF, 8, 32, 1)
-    last_r.append(give(u1, stage_r, other_r, (0, 1)))
+    last.append(start([give(u1, stage_r, other_r, (0, 1))], other_r.at[:, :, pl.ds(0, 256)]))
     leftover(u2, u1, fine_faces, gf, df, 12, 20, 8, RF, 8, 32, 1)
-    last_r.append(give(u1, stage_r, other_r, (2, 3)))
+    last.append(start([give(u1, stage_r, other_r, (2, 3))], other_r.at[:, :, pl.ds(256, 256)]))
     keep(stage_f, out_field)
-    take(last_f, other_f, out_field)
+    last[0]()
+    last[1]()
+    take(other_f, out_field)
     keep(stage_r, out_resid)
-    take(last_r, other_r, out_resid)
+    last[2]()
+    last[3]()
+    take(other_r, out_resid)
     drain()
 
 
@@ -544,10 +553,8 @@
     scratch += [deep_field] * 4 + [vmem(7, 5 * R2, LANES), vmem(5 * R2, LANES), vmem(12 * RF, LANES)]
     scratch += [vmem(4, 32, 512)] * 2 + [vmem(3, 32, 512)] * 2
     for big, middle, small in ((160, 80, 8), (96, 48, 8), (104, 56, 24), (32, 16, 8), (144, 72, 16)):
-        for count, rows in ((2, big), (2, middle), (4, small)):
-            scratch += [vmem(count, rows, LANES)] * 2
-    messages = 3 + 5 * 8 + 6 + 14 + 4
-    scratch += [pltpu.SemaphoreType.DMA((4,))] + [pltpu.SemaphoreType.DMA((messages,))] * 2
+        scratch += [vmem(2 * big + 2 * middle + 4 * small, LANES)] * 2
+    scratch += [pltpu.SemaphoreType.DMA((4,))] + [pltpu.SemaphoreType.DMA((ROUNDS,))] * 2
     hbm = pl.BlockSpec(memory_space=pltpu.HBM)
     shape = jax.ShapeDtypeStruct(source.shape, source.dtype)
     field, resid, held = pl.pallas_call(
@@ -561,7 +568,7 @@
         ),
         cost_estimate=pl.CostEstimate(flops=3 * 10**7, bytes_accessed=3 * 10**6, transcendentals=0),
     )(*[pltpu.with_memory_space_constraint(x, pltpu.HBM) for x in (box_counts, source, conductance, initial)])
-    return jnp.where(held > 0.0, field, 0.0), jnp.where(held > 0.0, resid, 0.0)
+    return field * held, resid * held
 
 
 def solution(mesh):

time: 35.3 us -> 33.2 us (0.941)
  Pallas kernels: 32.8 us -> 31.3 us
  other arithmetic: 1.78 us -> 1.11 us
    select_n x2 -> x0, other arithmetic: 1.78 us -> none  [the longest x1 0.92 us: body(): jnp.where(held > 0.0, resid, 0.0)]
    pallas_call x1, Pallas kernels: 32.8 us -> 31.3 us  [body(): pl.pallas_call(kernel, out_shape=(shape,) * 3, in_specs=[hbm] * 4, out_sp...]
    mul x0 -> x1, other arithmetic: none -> 1.11 us  [body(): return (field * held, resid * held)]
where the time goes in v5:
time: 33.2 us; the launch traced here: 33.1 us
  Pallas kernels  31.3 us (94%)
  other arithmetic  1.11 us (3%)
  between operations  0.64 us (2%)
    pallas_call x1, Pallas kernels, body(): pl.pallas_call(kernel, out_shape=(shape,) * 3, in_specs=[hbm] * 4, out_sp...  31.3 us
    mul x1, other arithmetic, body(): return (field * held, resid * held)  1.11 us

profile of v5, /device:TPU:1, one launch (start us, length us, event | category | flops | bytes accessed | tf_op | source)
XLA Modules:
  0.0 33.1 jit_solution(5836661851013923633)
XLA Ops:
  0.6 31.3 %shard_map.59 = (f32[4,32,1024]{2,1,0:T(8,128)S(1)}, f32[4,32,1024]{2,1,0:T(8,128)S(1)}, f32[4,32,1024]{2,1,0:T(8,128)S(1)}) custom-call(s32[128]{0:T(128)} %counts.1, f32[4,32,1024]{2,1,0:T(8,128)} %source.1, f32[4,32,1024]{2,1,0:T(8,128)} %conductance.1, f32[4,32,1024]{2,1,0:T(8,128)} %initial.1), custom_call_target="tpu_custom_call" | custom-call | flops 30000000 | bytes 3000000 | tf_op jit(solution)/shard_map/pallas_call | solution.py:560
  32.0 1.1 %fusion = (f32[4,32,1024]{2,1,0:T(8,128)}, f32[4,32,1024]{2,1,0:T(8,128)}) fusion(f32[4,32,1024]{2,1,0:T(8,128)S(1)} %get-tuple-element.7, f32[4,32,1024]{2,1,0:T(8,128)S(1)} %get-tuple-element.6, f32[4,32,1024]{2,1,0:T(8,128)S(1)} %get-tuple-element.5), kind=kLoop, calls=%fused_computation | loop fusion | flops 262144 | bytes 2621440 | tf_op jit(solution)/shard_map/mul | solution.py:571

commit v6 on v5

--- a/solution.py
+++ b/solution.py
@@ -15,7 +15,7 @@
 FULL = (1, 1), (1, -1), (-1, 1), (-1, -1), (1, 0), (-1, 0), (0, 1), (0, -1)
 FAR = (1, 2), (1, -2), (-1, 2), (-1, -2), (0, 2), (0, -2)
 F32 = jnp.float32
-ROUNDS = 3 + 5 + 2 + 4
+ROUNDS = 3 + 5 + 3 + 4
 
 
 def lane_ids(rows):
@@ -80,12 +80,12 @@
     return (parts[0] + parts[1]) + (parts[2] + parts[3]) + (parts[4] + parts[5])
 
 
-def loop(low, high, width, body, group=None):
+def planes_loop(low, high, width, body, group=None, base=0):
     assert (high - low) % width == 0
     group = group or width
 
     def step(index, carry):
-        first = low + index * width
+        first = base + low + index * width
         stores = []
         for m in range(width):
             stores += body(first + m)
@@ -128,6 +128,8 @@
     a, j = me // 8, me % 8
     half = me % 2
     sibling = me + 1 - 2 * half
+    zero = me // 1024
+    loop = functools.partial(planes_loop, base=zero)
     across = {da: ((a + da + 16) % 16) * 8 for da in (-1, 0, 1)}
     along = {dj: (j + dj + 8) % 8 for dj in (-2, -1, 0, 1, 2)}
 
@@ -249,11 +251,11 @@
 
     spare = list(post)
 
-    def exchange(strips, corners, block=None):
+    def exchange(strips, corners, block=None, where=FULL):
         out, got = spare.pop(0), spare.pop(0)
         copies, filled = [], []
         offset = 0
-        for da, dj in FULL:
+        for da, dj in where:
             first_row = offset
             for ref, first, count, stride in pieces(strips, corners, block, da, dj, near):
                 out[pl.ds(offset, count), :] = ref[slab(ref, first, count, stride)]
@@ -307,10 +309,7 @@
         return start(copies, ref.at[pl.ds(0, 8 * len(where))])
 
     c2[pl.ds(own2, 8), :] = packed(c1)
-    land_c1 = exchange(
-        ((c1, 1, (1, 2, 3, 4, 5, 6)),), [(c1, 1, d, 1, 6 - d) for d in range(1, 6)], c2
-    )
-    third = blocks2(c2, FAR)
+    land_c1 = exchange(((c1, 1, (1, 2, 3, 4, 5, 6)),), (), c2, ((1, 0), (-1, 0)))
 
     land_c()
 
@@ -380,6 +379,24 @@
         return [(u1, at(base, 40), value), (gf, at(base, 40), right)]
 
     loop(2, 22, 10, first_sweep, group=5)
+
+    land_c1()
+    third = [
+        start(
+            [
+                (c1.at[pl.ds(8 * R1, 6 * R1)], c1.at[pl.ds(16 * R1, 6 * R1)], device(0, -1)),
+                (c1.at[pl.ds(10 * R1, 6 * R1)], c1.at[pl.ds(2 * R1, 6 * R1)], device(0, 1)),
+            ],
+            c1.at[pl.ds(0, 12 * R1)],
+        ),
+        start(
+            [
+                (c2.at[pl.ds(3 * R2, R2)], c2.at[pl.ds(R2 * (3 - dj), R2)], device(0, dj))
+                for dj in (2, -2, 1, -1)
+            ],
+            c2.at[pl.ds(0, 4 * R2)],
+        ),
+    ]
     sweep(u1, u2, fine_faces, gf, 3, 21, 9, RF, 4, 40, 1)
     leftover(u2, u1, fine_faces, gf, df, 4, 20, 8, RF, 8, 32, 1)
 
@@ -395,7 +412,7 @@
     )
 
     drain()
-    land_c1()
+    third[0]()
     edges(c1, 0, 32, 8, R1, 8, (8, 23), *ends)
     mid_faces = [mid.at[n] for n in range(6)]
 
@@ -413,7 +430,7 @@
     loop(3, 21, 3, mid_coeffs, group=1)
     cut(mid, 0, 32, 8, R1, 8, (8, 23), *ends)
 
-    third()
+    third[1]()
 
     def around2(ref):
         lanes = lane_ids(5 * R2) % 4
@@ -421,8 +438,8 @@
         return centre, (
             jnp.where(lanes == 0, turn(ref[0 : 5 * R2, :], -3), turn(centre, 1)),
             jnp.where(lanes == 3, turn(ref[2 * R2 : 7 * R2, :], 3), turn(centre, -1)),
-            ref[pl.ds(R2 - 1, 5 * R2), :],
-            ref[pl.ds(R2 + 1, 5 * R2), :],
+            ref[pl.ds(zero + (R2 - 1), 5 * R2), :],
+            ref[pl.ds(zero + (R2 + 1), 5 * R2), :],
             turn(centre, 4),
             turn(centre, -4),
         )
@@ -467,7 +484,7 @@
     hops = ((1, 2), (-1, 2), (1, -2), (-1, -2))
     for number in range(8):
         block, i = (number + 6) // 4, (number + 6) % 4
-        value = jnp.where(lanes16 == i, e2b[pl.ds(R2 + R2 * block + 4, 16), :], 0.0)
+        value = jnp.where(lanes16 == i, e2b[pl.ds(zero + (R2 + R2 * block + 4), 16), :], 0.0)
         value = value + turn(value, hops[i][0])
         value = value + turn(value, hops[i][1])
         pe2[pl.ds(32 * number, 16, stride=2), :] = value
@@ -552,7 +569,7 @@
     scratch += [mid_field] * 4 + [vmem(8 * 32, LANES), vmem(6, P1 * R1, LANES)] + [mid_field] * 4
     scratch += [deep_field] * 4 + [vmem(7, 5 * R2, LANES), vmem(5 * R2, LANES), vmem(12 * RF, LANES)]
     scratch += [vmem(4, 32, 512)] * 2 + [vmem(3, 32, 512)] * 2
-    for big, middle, small in ((160, 80, 8), (96, 48, 8), (104, 56, 24), (32, 16, 8), (144, 72, 16)):
+    for big, middle, small in ((160, 80, 8), (96, 48, 8), (0, 56, 0), (32, 16, 8), (144, 72, 16)):
         scratch += [vmem(2 * big + 2 * middle + 4 * small, LANES)] * 2
     scratch += [pltpu.SemaphoreType.DMA((4,))] + [pltpu.SemaphoreType.DMA((ROUNDS,))] * 2
     hbm = pl.BlockSpec(memory_space=pltpu.HBM)

time: 33.2 us -> 34.2 us (1.030)
  Pallas kernels: 31.3 us -> 32.3 us
    pallas_call x1, Pallas kernels: 31.3 us -> 32.3 us  [body(): pl.pallas_call(kernel, out_shape=(shape,) * 3, in_specs=[hbm] * 4, out_sp...]
where the time goes in v6:
time: 34.2 us; the launch traced here: 34.1 us
  Pallas kernels  32.3 us (94%)
  other arithmetic  1.11 us (3%)
  between operations  0.64 us (2%)
    pallas_call x1, Pallas kernels, body(): pl.pallas_call(kernel, out_shape=(shape,) * 3, in_specs=[hbm] * 4, out_sp...  32.3 us
    mul x1, other arithmetic, body(): return (field * held, resid * held)  1.11 us

profile of v6, /device:TPU:1, one launch (start us, length us, event | category | flops | bytes accessed | tf_op | source)
XLA Modules:
  0.0 34.1 jit_solution(17115854195775697727)
XLA Ops:
  0.6 32.3 %shard_map.59 = (f32[4,32,1024]{2,1,0:T(8,128)S(1)}, f32[4,32,1024]{2,1,0:T(8,128)S(1)}, f32[4,32,1024]{2,1,0:T(8,128)S(1)}) custom-call(s32[128]{0:T(128)} %counts.1, f32[4,32,1024]{2,1,0:T(8,128)} %source.1, f32[4,32,1024]{2,1,0:T(8,128)} %conductance.1, f32[4,32,1024]{2,1,0:T(8,128)} %initial.1), custom_call_target="tpu_custom_call" | custom-call | flops 30000000 | bytes 3000000 | tf_op jit(solution)/shard_map/pallas_call | solution.py:577
  33.0 1.1 %fusion = (f32[4,32,1024]{2,1,0:T(8,128)}, f32[4,32,1024]{2,1,0:T(8,128)}) fusion(f32[4,32,1024]{2,1,0:T(8,128)S(1)} %get-tuple-element.7, f32[4,32,1024]{2,1,0:T(8,128)S(1)} %get-tuple-element.6, f32[4,32,1024]{2,1,0:T(8,128)S(1)} %get-tuple-element.5), kind=kLoop, calls=%fused_computation | loop fusion | flops 262144 | bytes 2621440 | tf_op jit(solution)/shard_map/mul | solution.py:588

commit v7 on v5

--- a/solution.py
+++ b/solution.py
@@ -80,12 +80,12 @@
     return (parts[0] + parts[1]) + (parts[2] + parts[3]) + (parts[4] + parts[5])
 
 
-def loop(low, high, width, body, group=None):
+def planes_loop(low, high, width, body, group=None, base=0):
     assert (high - low) % width == 0
     group = group or width
 
     def step(index, carry):
-        first = low + index * width
+        first = base + low + index * width
         stores = []
         for m in range(width):
             stores += body(first + m)
@@ -128,6 +128,8 @@
     a, j = me // 8, me % 8
     half = me % 2
     sibling = me + 1 - 2 * half
+    zero = me // 1024
+    loop = functools.partial(planes_loop, base=zero)
     across = {da: ((a + da + 16) % 16) * 8 for da in (-1, 0, 1)}
     along = {dj: (j + dj + 8) % 8 for dj in (-2, -1, 0, 1, 2)}
 
@@ -171,7 +173,7 @@
         copy.start()
 
     barrier = pltpu.get_barrier_semaphore()
-    for da, dj in FULL + FAR:
+    for da, dj in FULL[::-1] + FAR:
         pl.semaphore_signal(
             barrier, inc=1, device_id=(device(da, dj),), device_id_type=pl.DeviceIdType.MESH
         )
@@ -249,11 +251,11 @@
 
     spare = list(post)
 
-    def exchange(strips, corners, block=None):
+    def exchange(strips, corners, block=None, where=FULL):
         out, got = spare.pop(0), spare.pop(0)
         copies, filled = [], []
         offset = 0
-        for da, dj in FULL:
+        for da, dj in where:
             first_row = offset
             for ref, first, count, stride in pieces(strips, corners, block, da, dj, near):
                 out[pl.ds(offset, count), :] = ref[slab(ref, first, count, stride)]
@@ -310,7 +312,7 @@
     land_c1 = exchange(
         ((c1, 1, (1, 2, 3, 4, 5, 6)),), [(c1, 1, d, 1, 6 - d) for d in range(1, 6)], c2
     )
-    third = blocks2(c2, FAR)
+    far_c2 = blocks2(c2, FAR)
 
     land_c()
 
@@ -410,10 +412,24 @@
         out.append((d1, at(base, 32), 0.3125 * total))
         return out
 
-    loop(3, 21, 3, mid_coeffs, group=1)
+    loop(6, 18, 3, mid_coeffs, group=1)
     cut(mid, 0, 32, 8, R1, 8, (8, 23), *ends)
 
-    third()
+    def guess(p):
+        base = p * R1
+        return [(g1, at(base, 32), w1[pl.ds(base, 32), :] * f1[pl.ds(base, 32), :])]
+
+    land_f()
+    loop(6, 18, 12, guess)
+    sweep(g1, e1, mid_faces, g1, 7, 17, 10, R1, 4, 24, 2)
+    leftover(e1, r1, mid_faces, g1, d1, 8, 16, 8, R1, 8, 16, 2)
+    f2[pl.ds(own2, 8), :] = packed(r1)
+    sixth = blocks2(f2, FAR + FULL)
+
+    loop(3, 6, 3, mid_coeffs, group=1)
+    loop(18, 21, 3, mid_coeffs, group=1)
+    cut(mid, 0, 32, 8, R1, 8, (8, 23), *ends)
+    far_c2()
 
     def around2(ref):
         lanes = lane_ids(5 * R2) % 4
@@ -421,8 +437,8 @@
         return centre, (
             jnp.where(lanes == 0, turn(ref[0 : 5 * R2, :], -3), turn(centre, 1)),
             jnp.where(lanes == 3, turn(ref[2 * R2 : 7 * R2, :], 3), turn(centre, -1)),
-            ref[pl.ds(R2 - 1, 5 * R2), :],
-            ref[pl.ds(R2 + 1, 5 * R2), :],
+            ref[pl.ds(zero + (R2 - 1), 5 * R2), :],
+            ref[pl.ds(zero + (R2 + 1), 5 * R2), :],
             turn(centre, 4),
             turn(centre, -4),
         )
@@ -437,22 +453,11 @@
         deep[n] = faces[n]
     deep[6] = 32.0 * quarter
 
-    def guess(p):
-        base = p * R1
-        return [(g1, at(base, 32), w1[pl.ds(base, 32), :] * f1[pl.ds(base, 32), :])]
-
-    land_f()
-    loop(6, 18, 12, guess)
-    sweep(g1, e1, mid_faces, g1, 7, 17, 10, R1, 4, 24, 2)
-    leftover(e1, r1, mid_faces, g1, d1, 8, 16, 8, R1, 8, 16, 2)
-    f2[pl.ds(own2, 8), :] = packed(r1)
-    sixth = blocks2(f2, FAR + FULL)
-
+    drain()
     land_rest()
     loop(3, 21, 9, guess)
     sweep(g1, e1, mid_faces, g1, 4, 20, 8, R1, 4, 24, 2)
 
-    drain()
     sixth()
     g2[...] = deep[6] * f2[R2 : 6 * R2, :]
     e2[R2 : 6 * R2, :] = g2[...]
@@ -467,7 +472,7 @@
     hops = ((1, 2), (-1, 2), (1, -2), (-1, -2))
     for number in range(8):
         block, i = (number + 6) // 4, (number + 6) % 4
-        value = jnp.where(lanes16 == i, e2b[pl.ds(R2 + R2 * block + 4, 16), :], 0.0)
+        value = jnp.where(lanes16 == i, e2b[pl.ds(zero + (R2 + R2 * block + 4), 16), :], 0.0)
         value = value + turn(value, hops[i][0])
         value = value + turn(value, hops[i][1])
         pe2[pl.ds(32 * number, 16, stride=2), :] = value

time: 33.2 us -> 33.2 us (level)
  no operation moved by 1% of the time
where the time goes in v7:
time: 33.2 us; the launch traced here: 33.1 us
  Pallas kernels  31.4 us (95%)
  other arithmetic  1.11 us (3%)
  between operations  0.64 us (2%)
    pallas_call x1, Pallas kernels, body(): pl.pallas_call(kernel, out_shape=(shape,) * 3, in_specs=[hbm] * 4, out_sp...  31.4 us
    mul x1, other arithmetic, body(): return (field * held, resid * held)  1.11 us

profile of v7, /device:TPU:1, one launch (start us, length us, event | category | flops | bytes accessed | tf_op | source)
XLA Modules:
  0.0 33.1 jit_solution(7478540408640492257)
XLA Ops:
  0.6 31.4 %shard_map.59 = (f32[4,32,1024]{2,1,0:T(8,128)S(1)}, f32[4,32,1024]{2,1,0:T(8,128)S(1)}, f32[4,32,1024]{2,1,0:T(8,128)S(1)}) custom-call(s32[128]{0:T(128)} %counts.1, f32[4,32,1024]{2,1,0:T(8,128)} %source.1, f32[4,32,1024]{2,1,0:T(8,128)} %conductance.1, f32[4,32,1024]{2,1,0:T(8,128)} %initial.1), custom_call_target="tpu_custom_call" | custom-call | flops 30000000 | bytes 3000000 | tf_op jit(solution)/shard_map/pallas_call | solution.py:565
  32.0 1.1 %fusion = (f32[4,32,1024]{2,1,0:T(8,128)}, f32[4,32,1024]{2,1,0:T(8,128)}) fusion(f32[4,32,1024]{2,1,0:T(8,128)S(1)} %get-tuple-element.7, f32[4,32,1024]{2,1,0:T(8,128)S(1)} %get-tuple-element.6, f32[4,32,1024]{2,1,0:T(8,128)S(1)} %get-tuple-element.5), kind=kLoop, calls=%fused_computation | loop fusion | flops 262144 | bytes 2621440 | tf_op jit(solution)/shard_map/mul | solution.py:576

commit v8 on v7

--- a/solution.py
+++ b/solution.py
@@ -133,6 +133,8 @@
     across = {da: ((a + da + 16) % 16) * 8 for da in (-1, 0, 1)}
     along = {dj: (j + dj + 8) % 8 for dj in (-2, -1, 0, 1, 2)}
 
+    sibling_far = across[0] + (j - 1 + 2 * half + 8) % 8
+
     def device(da, dj):
         return across[da] + along[dj]
 
@@ -153,9 +155,13 @@
         leaving.append(everything.wait_send)
         return everything.wait_recv
 
-    def drain():
-        while leaving:
+    def drain(but=0):
+        while len(leaving) > but:
             leaving.pop(0)()
+
+    barrier = pltpu.get_barrier_semaphore()
+    for target in (sibling,) + tuple(device(da, dj) for da, dj in FULL[:6]) + (sibling_far,):
+        pl.semaphore_signal(barrier, inc=1, device_id=(target,), device_id_type=pl.DeviceIdType.MESH)
 
     raws = (raw_c, raw_s, raw_u)
     given = (conductance, source, initial)
@@ -172,12 +178,7 @@
     for copy in locals_:
         copy.start()
 
-    barrier = pltpu.get_barrier_semaphore()
-    for da, dj in FULL[::-1] + FAR:
-        pl.semaphore_signal(
-            barrier, inc=1, device_id=(device(da, dj),), device_id_type=pl.DeviceIdType.MESH
-        )
-    pl.semaphore_wait(barrier, len(FULL + FAR))
+    pl.semaphore_wait(barrier, len(FULL))
 
     swaps = [
         start(
@@ -312,9 +313,9 @@
     land_c1 = exchange(
         ((c1, 1, (1, 2, 3, 4, 5, 6)),), [(c1, 1, d, 1, 6 - d) for d in range(1, 6)], c2
     )
+
+    land_c()
     far_c2 = blocks2(c2, FAR)
-
-    land_c()
 
     def edges(ref, first, side, count, rows, plane, row, low_y, high_y, low_x, high_x):
         for outside, there, here in (
@@ -396,7 +397,7 @@
         [(f1, 1, 1, 2, 3), (f1, 1, 2, 1, 3), (f1, 1, 3, 1, 2), (f1, 1, 4, 1, 1)] + fine_corner(u2, 3),
     )
 
-    drain()
+    drain(but=2)
     land_c1()
     edges(c1, 0, 32, 8, R1, 8, (8, 23), *ends)
     mid_faces = [mid.at[n] for n in range(6)]
@@ -453,7 +454,7 @@
         deep[n] = faces[n]
     deep[6] = 32.0 * quarter
 
-    drain()
+    drain(but=1)
     land_rest()
     loop(3, 21, 9, guess)
     sweep(g1, e1, mid_faces, g1, 4, 20, 8, R1, 4, 24, 2)

time: 33.2 us -> 32.9 us (level)
  no operation moved by 1% of the time
where the time goes in v8:
time: 32.9 us; the launch traced here: 32.8 us
  Pallas kernels  31.1 us (95%)
  other arithmetic  1.11 us (3%)
  between operations  0.64 us (2%)
    pallas_call x1, Pallas kernels, body(): pl.pallas_call(kernel, out_shape=(shape,) * 3, in_specs=[hbm] * 4, out_sp...  31.1 us
    mul x1, other arithmetic, body(): return (field * held, resid * held)  1.11 us

profile of v8, /device:TPU:1, one launch (start us, length us, event | category | flops | bytes accessed | tf_op | source)
XLA Modules:
  0.0 32.8 jit_solution(7370446743847434655)
XLA Ops:
  0.6 31.1 %shard_map.59 = (f32[4,32,1024]{2,1,0:T(8,128)S(1)}, f32[4,32,1024]{2,1,0:T(8,128)S(1)}, f32[4,32,1024]{2,1,0:T(8,128)S(1)}) custom-call(s32[128]{0:T(128)} %counts.1, f32[4,32,1024]{2,1,0:T(8,128)} %source.1, f32[4,32,1024]{2,1,0:T(8,128)} %conductance.1, f32[4,32,1024]{2,1,0:T(8,128)} %initial.1), custom_call_target="tpu_custom_call" | custom-call | flops 30000000 | bytes 3000000 | tf_op jit(solution)/shard_map/pallas_call | solution.py:566
  31.7 1.1 %fusion = (f32[4,32,1024]{2,1,0:T(8,128)}, f32[4,32,1024]{2,1,0:T(8,128)}) fusion(f32[4,32,1024]{2,1,0:T(8,128)S(1)} %get-tuple-element.7, f32[4,32,1024]{2,1,0:T(8,128)S(1)} %get-tuple-element.6, f32[4,32,1024]{2,1,0:T(8,128)S(1)} %get-tuple-element.5), kind=kLoop, calls=%fused_computation | loop fusion | flops 262144 | bytes 2621440 | tf_op jit(solution)/shard_map/mul | solution.py:577

commit v9 on v8

--- a/solution.py
+++ b/solution.py
@@ -15,7 +15,7 @@
 FULL = (1, 1), (1, -1), (-1, 1), (-1, -1), (1, 0), (-1, 0), (0, 1), (0, -1)
 FAR = (1, 2), (1, -2), (-1, 2), (-1, -2), (0, 2), (0, -2)
 F32 = jnp.float32
-ROUNDS = 3 + 5 + 2 + 4
+ROUNDS = 3 + 5 + 2 + 6
 
 
 def lane_ids(rows):
@@ -63,11 +63,23 @@
     return faces, total, quarter
 
 
-def around(ref, base, count, rows, twist):
-    centre = ref[pl.ds(base, count), :]
+class Planes:
+    def __init__(self):
+        self.held = {}
+        self.step = 0
+
+    def load(self, ref, base, count, rows, ahead):
+        key = (id(ref), count, self.step + ahead)
+        if key not in self.held:
+            self.held[key] = ref[pl.ds(base + rows * ahead, count), :]
+        return self.held[key]
+
+
+def around(ref, base, count, rows, twist, planes):
+    centre = planes.load(ref, base, count, rows, 0)
     return centre, (
-        ref[pl.ds(base - rows, count), :],
-        ref[pl.ds(base + rows, count), :],
+        planes.load(ref, base, count, rows, -1),
+        planes.load(ref, base, count, rows, 1),
         ref[pl.ds(base - 1, count), :],
         ref[pl.ds(base + 1, count), :],
         turn(centre, twist),
@@ -86,13 +98,14 @@
 
     def step(index, carry):
         first = base + low + index * width
-        stores = []
+        stores, planes = [], Planes()
         for m in range(width):
-            stores += body(first + m)
+            planes.step = m
+            stores += body(first + m, planes)
             if (m + 1) % group == 0 or m == width - 1:
                 for ref, index_, value in stores:
                     ref[index_] = value
-                stores = []
+                stores, planes = [], Planes()
         return carry
 
     if high - low == width:
@@ -180,13 +193,13 @@
 
     pl.semaphore_wait(barrier, len(FULL))
 
-    swaps = [
-        start(
+    def swap(number):
+        return start(
             [(given[number].at[pl.ds(0, 3), :, theirs], raws[number].at[held], sibling)],
             raws[number].at[held],
         )
-        for number in range(3)
-    ]
+
+    swaps = [swap(0), swap(1)]
     locals_[0].wait()
     split = owners[me - half]
     own = jnp.where(half == 0, split, 4 - split)
@@ -197,9 +210,11 @@
     def bring(number, ref):
         locals_[1 + number].wait()
         swaps[number]()
+        if number == 0:
+            swaps.append(swap(2))
         raw = raws[number]
 
-        def step(t):
+        def step(t, planes):
             rows = pl.ds(pl.multiple_of(8 * t, 8), 8)
             out = []
             for q in range(4):
@@ -288,7 +303,7 @@
     bring(2, uf)
     land_u = exchange(((uf, 0, (1, 2, 3)),), fine_corner(uf, 3))
 
-    def coarse_c(i):
+    def coarse_c(i, planes):
         total = pair_rows(cf, (4 + 2 * i) * RF + 8, 16, RF)
         return [(c1, at(pl.multiple_of((8 + i) * R1 + 8, 8), 16), pair_lanes(total, 1))]
 
@@ -314,6 +329,25 @@
         ((c1, 1, (1, 2, 3, 4, 5, 6)),), [(c1, 1, d, 1, 6 - d) for d in range(1, 6)], c2
     )
 
+    fine_faces = [fine.at[n] for n in range(6)]
+
+    def fine_coeffs(*windows):
+        def body(p, planes):
+            out = []
+            for start_row, count in windows:
+                base = p * RF + start_row
+                centre, besides = around(cf, base, count, RF, 1, Planes())
+                z = lane_ids(count)
+                inside = (None, None, None, None, z != 0, z != 127)
+                faces, total, quarter = coefficients(centre, besides, inside)
+                out += [(fine, (n,) + at(base, count), faces[n]) for n in range(6)]
+                out.append((gf, at(base, count), 2.0 * quarter))
+                out.append((df, at(base, count), 1.25 * total))
+            return out
+
+        return body
+
+    loop(5, 19, 7, fine_coeffs((12, 24)), group=1)
     land_c()
     far_c2 = blocks2(c2, FAR)
 
@@ -338,36 +372,43 @@
 
     ends = (j == 0, j == 7, a == 0, a == 15)
     edges(cf, 4, 40, 16, RF, 4, (8, 39), *ends)
-    fine_faces = [fine.at[n] for n in range(6)]
-
-    def fine_coeffs(p):
-        base = p * RF + 4
-        centre, besides = around(cf, base, 40, RF, 1)
-        z = lane_ids(40)
-        inside = (None, None, None, None, z != 0, z != 127)
-        faces, total, quarter = coefficients(centre, besides, inside)
-        out = [(fine, (n,) + at(base, 40), faces[n]) for n in range(6)]
-        out.append((gf, at(base, 40), 2.0 * quarter))
-        out.append((df, at(base, 40), 1.25 * total))
-        return out
-
-    loop(2, 22, 4, fine_coeffs, group=1)
+    loop(5, 19, 7, fine_coeffs((4, 8), (36, 8)), group=1)
+    for low in (2, 19):
+        loop(low, low + 3, 3, fine_coeffs((4, 40)), group=1)
     cut(fine, 4, 40, 16, RF, 4, (8, 39), *ends)
+
+    def first_sweep(*windows):
+        def body(p, planes):
+            out = []
+            for start_row, count in windows:
+                base = p * RF + start_row
+                centre, besides = around(uf, base, count, RF, 1, planes if len(windows) == 1 else Planes())
+                right = gf[pl.ds(base, count), :] * sf[pl.ds(base, count), :]
+                value = 0.2 * centre + right + weighted(fine_faces, base, count, besides)
+                out += [(u1, at(base, count), value), (gf, at(base, count), right)]
+            return out
+
+        return body
+
+    loop(5, 19, 7, first_sweep((12, 24)))
     land_u()
+    loop(5, 19, 7, first_sweep((4, 8), (36, 8)))
+    for low in (2, 19):
+        loop(low, low + 3, 3, first_sweep((4, 40)))
 
     def sweep(src, dst, faces, right, low, high, width, rows, start, count, twist):
-        def step(p):
+        def step(p, planes):
             base = p * rows + start
-            centre, besides = around(src, base, count, rows, twist)
+            centre, besides = around(src, base, count, rows, twist, planes)
             value = 0.2 * centre + right[pl.ds(base, count), :] + weighted(faces, base, count, besides)
             return [(dst, at(base, count), value)]
 
         loop(low, high, width, step, group=5)
 
     def leftover(src, dst, faces, right, diag, low, high, width, rows, start, count, twist):
-        def step(p):
+        def step(p, planes):
             base = p * rows + start
-            centre, besides = around(src, base, count, rows, twist)
+            centre, besides = around(src, base, count, rows, twist, planes)
             value = diag[pl.ds(base, count), :] * (
                 right[pl.ds(base, count), :] + weighted(faces, base, count, besides) - 0.8 * centre
             )
@@ -375,18 +416,10 @@
 
         loop(low, high, width, step, group=4)
 
-    def first_sweep(p):
-        base = p * RF + 4
-        centre, besides = around(uf, base, 40, RF, 1)
-        right = gf[pl.ds(base, 40), :] * sf[pl.ds(base, 40), :]
-        value = 0.2 * centre + right + weighted(fine_faces, base, 40, besides)
-        return [(u1, at(base, 40), value), (gf, at(base, 40), right)]
-
-    loop(2, 22, 10, first_sweep, group=5)
     sweep(u1, u2, fine_faces, gf, 3, 21, 9, RF, 4, 40, 1)
     leftover(u2, u1, fine_faces, gf, df, 4, 20, 8, RF, 8, 32, 1)
 
-    def coarse_f(i):
+    def coarse_f(i, planes):
         total = pair_rows(u1, (4 + 2 * i) * RF + 8, 16, RF)
         return [(f1, at(pl.multiple_of((8 + i) * R1 + 8, 8), 16), pair_lanes(total, 1))]
 
@@ -402,9 +435,9 @@
     edges(c1, 0, 32, 8, R1, 8, (8, 23), *ends)
     mid_faces = [mid.at[n] for n in range(6)]
 
-    def mid_coeffs(p):
+    def mid_coeffs(p, planes):
         base = p * R1
-        centre, besides = around(c1, base, 32, R1, 2)
+        centre, besides = around(c1, base, 32, R1, 2, planes)
         z = lane_ids(32)
         inside = (None, None, None, None, z >= 2, z < 126)
         faces, total, quarter = coefficients(centre, besides, inside)
@@ -416,7 +449,7 @@
     loop(6, 18, 3, mid_coeffs, group=1)
     cut(mid, 0, 32, 8, R1, 8, (8, 23), *ends)
 
-    def guess(p):
+    def guess(p, planes):
         base = p * R1
         return [(g1, at(base, 32), w1[pl.ds(base, 32), :] * f1[pl.ds(base, 32), :])]
 
@@ -479,7 +512,7 @@
         pe2[pl.ds(32 * number, 16, stride=2), :] = value
         pe2[pl.ds(32 * number + 1, 16, stride=2), :] = value
 
-    def corrected1(p):
+    def corrected1(p, planes):
         value = e1[pl.ds(p * R1 + 4, 24), :] + pe2[pl.ds((p // 2 - 2) * 32 + 4, 24), :]
         return [(e1, at(p * R1 + 4, 24), value)]
 
@@ -487,13 +520,13 @@
     sweep(e1, e1b, mid_faces, g1, 5, 19, 14, R1, 4, 24, 2)
     sweep(e1b, e1, mid_faces, g1, 6, 18, 12, R1, 4, 24, 2)
 
-    def grown(i):
+    def grown(i, planes):
         value = e1[pl.ds((i + 6) * R1 + 4, 24), :]
         return [(pe1, (pl.ds(RF * i + odd, 24, stride=2), slice(None)), value) for odd in (0, 1)]
 
     loop(0, 12, 12, grown)
 
-    def corrected0(p):
+    def corrected0(p, planes):
         base = p * RF + 4
         return [(u2, at(base, 40), u2[pl.ds(base, 40), :] + pe1[pl.ds((p // 2) * RF + 4, 40), :])]
 
@@ -501,7 +534,7 @@
     sweep(u2, u1, fine_faces, gf, 2, 22, 10, RF, 4, 40, 1)
 
     def give(ref, stage, other, quads):
-        def step(t):
+        def step(t, planes):
             rows = pl.ds(pl.multiple_of(8 * t, 8), 8)
             out = []
             for q in quads:
@@ -530,17 +563,16 @@
     last.append(start([give(u2, stage_f, other_f, (0, 1))], other_f.at[:, :, pl.ds(0, 256)]))
     sweep(u1, u2, fine_faces, gf, 12, 21, 9, RF, 4, 40, 1)
     last.append(start([give(u2, stage_f, other_f, (2, 3))], other_f.at[:, :, pl.ds(256, 256)]))
-    leftover(u2, u1, fine_faces, gf, df, 4, 12, 8, RF, 8, 32, 1)
-    last.append(start([give(u1, stage_r, other_r, (0, 1))], other_r.at[:, :, pl.ds(0, 256)]))
-    leftover(u2, u1, fine_faces, gf, df, 12, 20, 8, RF, 8, 32, 1)
-    last.append(start([give(u1, stage_r, other_r, (2, 3))], other_r.at[:, :, pl.ds(256, 256)]))
+    for q in range(4):
+        leftover(u2, u1, fine_faces, gf, df, 4 + 4 * q, 8 + 4 * q, 4, RF, 8, 32, 1)
+        last.append(start([give(u1, stage_r, other_r, (q,))], other_r.at[:, :, pl.ds(128 * q, 128)]))
     keep(stage_f, out_field)
     last[0]()
     last[1]()
     take(other_f, out_field)
     keep(stage_r, out_resid)
-    last[2]()
-    last[3]()
+    for arrived in last[2:]:
+        arrived()
     take(other_r, out_resid)
     drain()
 

time: 32.9 us -> 33.2 us (level)
  no operation moved by 1% of the time
where the time goes in v9:
time: 33.2 us; the launch traced here: 33.1 us
  Pallas kernels  31.3 us (94%)
  other arithmetic  1.11 us (3%)
  between operations  0.64 us (2%)
    pallas_call x1, Pallas kernels, body(): pl.pallas_call(kernel, out_shape=(shape,) * 3, in_specs=[hbm] * 4, out_sp...  31.3 us
    mul x1, other arithmetic, body(): return (field * held, resid * held)  1.11 us

profile of v9, /device:TPU:1, one launch (start us, length us, event | category | flops | bytes accessed | tf_op | source)
XLA Modules:
  0.0 33.1 jit_solution(4842981524651103394)
XLA Ops:
  0.6 31.3 %shard_map.59 = (f32[4,32,1024]{2,1,0:T(8,128)S(1)}, f32[4,32,1024]{2,1,0:T(8,128)S(1)}, f32[4,32,1024]{2,1,0:T(8,128)S(1)}) custom-call(s32[128]{0:T(128)} %counts.1, f32[4,32,1024]{2,1,0:T(8,128)} %source.1, f32[4,32,1024]{2,1,0:T(8,128)} %conductance.1, f32[4,32,1024]{2,1,0:T(8,128)} %initial.1), custom_call_target="tpu_custom_call" | custom-call | flops 30000000 | bytes 3000000 | tf_op jit(solution)/shard_map/pallas_call | solution.py:598
  32.0 1.1 %fusion = (f32[4,32,1024]{2,1,0:T(8,128)}, f32[4,32,1024]{2,1,0:T(8,128)}) fusion(f32[4,32,1024]{2,1,0:T(8,128)S(1)} %get-tuple-element.7, f32[4,32,1024]{2,1,0:T(8,128)S(1)} %get-tuple-element.6, f32[4,32,1024]{2,1,0:T(8,128)S(1)} %get-tuple-element.5), kind=kLoop, calls=%fused_computation | loop fusion | flops 262144 | bytes 2621440 | tf_op jit(solution)/shard_map/mul | solution.py:609

commit v10 on v9

--- a/solution.py
+++ b/solution.py
@@ -199,7 +199,7 @@
             raws[number].at[held],
         )
 
-    swaps = [swap(0), swap(1)]
+    swaps = [swap(number) for number in range(3)]
     locals_[0].wait()
     split = owners[me - half]
     own = jnp.where(half == 0, split, 4 - split)
@@ -210,8 +210,6 @@
     def bring(number, ref):
         locals_[1 + number].wait()
         swaps[number]()
-        if number == 0:
-            swaps.append(swap(2))
         raw = raws[number]
 
         def step(t, planes):

time: 33.2 us -> 33.1 us (level)
  no operation moved by 1% of the time
where the time goes in v10:
time: 33.1 us; the launch traced here: 33 us
  Pallas kernels  31.3 us (95%)
  other arithmetic  1.11 us (3%)
  between operations  0.64 us (2%)
    pallas_call x1, Pallas kernels, body(): pl.pallas_call(kernel, out_shape=(shape,) * 3, in_specs=[hbm] * 4, out_sp...  31.3 us
    mul x1, other arithmetic, body(): return (field * held, resid * held)  1.11 us

profile of v10, /device:TPU:1, one launch (start us, length us, event | category | flops | bytes accessed | tf_op | source)
XLA Modules:
  0.0 33.0 jit_solution(11071146468407698039)
XLA Ops:
  0.6 31.3 %shard_map.59 = (f32[4,32,1024]{2,1,0:T(8,128)S(1)}, f32[4,32,1024]{2,1,0:T(8,128)S(1)}, f32[4,32,1024]{2,1,0:T(8,128)S(1)}) custom-call(s32[128]{0:T(128)} %counts.1, f32[4,32,1024]{2,1,0:T(8,128)} %source.1, f32[4,32,1024]{2,1,0:T(8,128)} %conductance.1, f32[4,32,1024]{2,1,0:T(8,128)} %initial.1), custom_call_target="tpu_custom_call" | custom-call | flops 30000000 | bytes 3000000 | tf_op jit(solution)/shard_map/pallas_call | solution.py:596
  31.9 1.1 %fusion = (f32[4,32,1024]{2,1,0:T(8,128)}, f32[4,32,1024]{2,1,0:T(8,128)}) fusion(f32[4,32,1024]{2,1,0:T(8,128)S(1)} %get-tuple-element.7, f32[4,32,1024]{2,1,0:T(8,128)S(1)} %get-tuple-element.6, f32[4,32,1024]{2,1,0:T(8,128)S(1)} %get-tuple-element.5), kind=kLoop, calls=%fused_computation | loop fusion | flops 262144 | bytes 2621440 | tf_op jit(solution)/shard_map/mul | solution.py:607

commit v11 on v8

--- a/solution.py
+++ b/solution.py
@@ -12,10 +12,10 @@
 R1, P1 = 32, 24
 R2 = 24
 LANES = 128
-FULL = (1, 1), (1, -1), (-1, 1), (-1, -1), (1, 0), (-1, 0), (0, 1), (0, -1)
+FULL = (1, 1), (1, -1), (1, 0), (-1, 1), (-1, -1), (-1, 0), (0, 1), (0, -1)
 FAR = (1, 2), (1, -2), (-1, 2), (-1, -2), (0, 2), (0, -2)
 F32 = jnp.float32
-ROUNDS = 3 + 5 + 2 + 4
+ROUNDS = 3 + 3 * (5 + 2) + 4
 
 
 def lane_ids(rows):
@@ -147,21 +147,45 @@
             device_id=(target,), device_id_type=pl.DeviceIdType.MESH,
         )
 
-    def start(copies, whole):
+    leaves = {1: a < 15, -1: a > 0}
+    comes = {1: a > 0, -1: a < 15}
+
+    def start(copies, whole, da=0, without=None):
         number = next(numbers)
-        for src, dst, target in copies:
-            describe(src, dst, number, target).start()
         everything = describe(whole, whole, number, sibling)
-        leaving.append(everything.wait_send)
-        return everything.wait_recv
+
+        def go():
+            for src, dst, target in copies:
+                describe(src, dst, number, target).start()
+
+        if da == 0:
+            go()
+            leaving.append(everything.wait_send)
+            return everything.wait_recv
+        pl.when(leaves[da])(go)
+        leaving.append(lambda: pl.when(leaves[da])(everything.wait_send))
+
+        def arrived():
+            pl.when(comes[da])(everything.wait_recv)
+            pl.when(jnp.logical_not(comes[da]))(without)
+
+        return arrived
 
     def drain(but=0):
         while len(leaving) > but:
             leaving.pop(0)()
 
     barrier = pltpu.get_barrier_semaphore()
-    for target in (sibling,) + tuple(device(da, dj) for da, dj in FULL[:6]) + (sibling_far,):
-        pl.semaphore_signal(barrier, inc=1, device_id=(target,), device_id_type=pl.DeviceIdType.MESH)
+
+    def here(*targets):
+        for target in targets:
+            pl.semaphore_signal(
+                barrier, inc=1, device_id=(target,), device_id_type=pl.DeviceIdType.MESH
+            )
+
+    here(sibling, sibling_far)
+    for da in (1, -1):
+        pl.when(leaves[da])(lambda: here(*[device(da, dj) for dj in (1, -1, 0)]))
 
     raws = (raw_c, raw_s, raw_u)
     given = (conductance, source, initial)
@@ -178,7 +202,7 @@
     for copy in locals_:
         copy.start()
 
-    pl.semaphore_wait(barrier, len(FULL))
+    pl.semaphore_wait(barrier, 2 + 3 * (a > 0).astype(jnp.int32) + 3 * (a < 15).astype(jnp.int32))
 
     swaps = [
         start(
@@ -252,24 +276,34 @@
 
     spare = list(post)
 
+    def ones(ref, *slabs):
+        for rows in slabs:
+            ref[rows, :] = jnp.ones((rows.size, LANES), F32)
+
     def exchange(strips, corners, block=None, where=FULL):
         out, got = spare.pop(0), spare.pop(0)
-        copies, filled = [], []
+        arrivals, filled = [], []
         offset = 0
-        for da, dj in where:
-            first_row = offset
-            for ref, first, count, stride in pieces(strips, corners, block, da, dj, near):
-                out[pl.ds(offset, count), :] = ref[slab(ref, first, count, stride)]
-                offset += count
-            offset += -offset % 8
-            rows = pl.ds(first_row, offset - first_row)
-            copies.append((out.at[rows], got.at[rows], device(da, dj)))
-            filled.append((first_row, da, dj))
+        for step_x in (1, -1, 0):
+            copies, group_row = [], offset
+            for da, dj in FULL:
+                if da != step_x:
+                    continue
+                first_row = offset
+                for ref, first, count, stride in pieces(strips, corners, block, da, dj, near):
+                    out[pl.ds(offset, count), :] = ref[slab(ref, first, count, stride)]
+                    offset += count
+                offset += -offset % 8
+                rows = pl.ds(first_row, offset - first_row)
+                copies.append((out.at[rows], got.at[rows], device(da, dj)))
+                filled.append((first_row, da, dj))
+            group = pl.ds(group_row, offset - group_row)
+            arrivals.append(start(copies, got.at[group], step_x, functools.partial(ones, got, group)))
         assert out.shape == (offset, LANES)
-        arrived = start(copies, got)
 
         def land():
-            arrived()
+            for arrived in arrivals:
+                arrived()
             for offset, da, dj in filled:
                 for ref, first, count, stride in pieces(strips, corners, block, da, dj, far):
                     ref[slab(ref, first, count, stride)] = got[pl.ds(offset, count), :]
@@ -303,11 +337,26 @@
         return total
 
     def blocks2(ref, where):
-        copies = [
-            (ref.at[pl.ds(own2, 8)], ref.at[pl.ds(there2(da, dj), 8)], device(da, dj))
-            for da, dj in where
-        ]
-        return start(copies, ref.at[pl.ds(0, 8 * len(where))])
+        arrivals = []
+        for step_x in (1, -1, 0):
+            places_ = [(da, dj) for da, dj in where if da == step_x]
+            copies = [
+                (ref.at[pl.ds(own2, 8)], ref.at[pl.ds(there2(da, dj), 8)], device(da, dj))
+                for da, dj in places_
+            ]
+            slabs = [pl.ds(there2(da, dj), 8) for da, dj in places_]
+            arrivals.append(
+                start(
+                    copies, ref.at[pl.ds(0, 8 * len(copies))], step_x,
+                    functools.partial(ones, ref, *slabs),
+                )
+            )
+
+        def arrived():
+            for part in arrivals:
+                part()
+
+        return arrived
 
     c2[pl.ds(own2, 8), :] = packed(c1)
     land_c1 = exchange(
@@ -397,7 +446,7 @@
         [(f1, 1, 1, 2, 3), (f1, 1, 2, 1, 3), (f1, 1, 3, 1, 2), (f1, 1, 4, 1, 1)] + fine_corner(u2, 3),
     )
 
-    drain(but=2)
+    drain(but=6)
     land_c1()
     edges(c1, 0, 32, 8, R1, 8, (8, 23), *ends)
     mid_faces = [mid.at[n] for n in range(6)]
@@ -454,7 +503,7 @@
         deep[n] = faces[n]
     deep[6] = 32.0 * quarter
 
-    drain(but=1)
+    drain(but=3)
     land_rest()
     loop(3, 21, 9, guess)
     sweep(g1, e1, mid_faces, g1, 4, 20, 8, R1, 4, 24, 2)

time: 32.9 us -> 27.8 us (0.84)
  the two profiles are of different devices: /device:TPU:1 before, /device:TPU:7 now
where the time goes in v11:
time: 27.8 us; the launch traced here: 27.7 us
  Pallas kernels  25.9 us (93%)
  other arithmetic  1.11 us (4%)
  between operations  0.64 us (2%)
    pallas_call x1, Pallas kernels, body(): pl.pallas_call(kernel, out_shape=(shape,) * 3, in_specs=[hbm] * 4, out_sp...  25.9 us
    mul x1, other arithmetic, body(): return (field * held, resid * held)  1.11 us

profile of v11, /device:TPU:7, one launch (start us, length us, event | category | flops | bytes accessed | tf_op | source)
XLA Modules:
  0.0 27.7 jit_solution(16637301969984080490)
XLA Ops:
  0.6 25.9 %shard_map.59 = (f32[4,32,1024]{2,1,0:T(8,128)S(1)}, f32[4,32,1024]{2,1,0:T(8,128)S(1)}, f32[4,32,1024]{2,1,0:T(8,128)S(1)}) custom-call(s32[128]{0:T(128)} %counts.1, f32[4,32,1024]{2,1,0:T(8,128)} %source.1, f32[4,32,1024]{2,1,0:T(8,128)} %conductance.1, f32[4,32,1024]{2,1,0:T(8,128)} %initial.1), custom_call_target="tpu_custom_call" | custom-call | flops 30000000 | bytes 3000000 | tf_op jit(solution)/shard_map/pallas_call | solution.py:615
  26.6 1.1 %fusion = (f32[4,32,1024]{2,1,0:T(8,128)}, f32[4,32,1024]{2,1,0:T(8,128)}) fusion(f32[4,32,1024]{2,1,0:T(8,128)S(1)} %get-tuple-element.7, f32[4,32,1024]{2,1,0:T(8,128)S(1)} %get-tuple-element.6, f32[4,32,1024]{2,1,0:T(8,128)S(1)} %get-tuple-element.5), kind=kLoop, calls=%fused_computation | loop fusion | flops 262144 | bytes 2621440 | tf_op jit(solution)/shard_map/mul | solution.py:626

commit v12 on v11

--- a/solution.py
+++ b/solution.py
@@ -150,26 +150,66 @@
     leaves = {1: a < 15, -1: a > 0}
     comes = {1: a > 0, -1: a < 15}
 
-    def start(copies, whole, da=0, without=None):
+    def inside(column):
+        return jnp.logical_and(column >= 0, column < 8)
+
+    def sized(messages, whole, sign, act):
+        sizes = {}
+        for column in range(8):
+            rows = sum(rows for rows, da, dj in messages if 0 <= column + sign * dj < 8)
+            sizes.setdefault(rows, []).append(column)
+        for rows, columns in sizes.items():
+            if len(columns) == 8:
+                act(rows)
+            else:
+                there = functools.reduce(jnp.logical_or, [j == column for column in columns])
+                pl.when(there)(functools.partial(act, rows))
+
+    def start(copies, ref, first_row, messages, without):
         number = next(numbers)
+        step_x = messages[0][1]
+
+        def some(rows):
+            part = ref.at[pl.ds(first_row, rows)]
+            return describe(part, part, number, sibling)
+
+        def go():
+            for src, dst, target, dj in copies:
+                begin = describe(src, dst, number, target).start
+                if dj == 0:
+                    begin()
+                else:
+                    pl.when(inside(j + dj))(begin)
+
+        def gone():
+            sized(messages, ref, 1, lambda rows: some(rows).wait_send())
+
+        def come():
+            sized(messages, ref, -1, lambda rows: some(rows).wait_recv())
+            for dj in sorted({dj for rows, da, dj in messages}):
+                if dj != 0:
+                    gaps = [n for n, item in enumerate(messages) if item[2] == dj]
+                    pl.when(jnp.logical_not(inside(j - dj)))(functools.partial(without, *gaps))
+
+        if step_x == 0:
+            go()
+            leaving.append(gone)
+            return come
+        pl.when(leaves[step_x])(go)
+        leaving.append(lambda: pl.when(leaves[step_x])(gone))
+
+        def arrived():
+            pl.when(comes[step_x])(come)
+            pl.when(jnp.logical_not(comes[step_x]))(functools.partial(without, *range(len(messages))))
+
+        return arrived
+
+    def hand(src, dst, whole):
+        number = next(numbers)
+        describe(src, dst, number, sibling).start()
         everything = describe(whole, whole, number, sibling)
-
-        def go():
-            for src, dst, target in copies:
-                describe(src, dst, number, target).start()
-
-        if da == 0:
-            go()
-            leaving.append(everything.wait_send)
-            return everything.wait_recv
-        pl.when(leaves[da])(go)
-        leaving.append(lambda: pl.when(leaves[da])(everything.wait_send))
-
-        def arrived():
-            pl.when(comes[da])(everything.wait_recv)
-            pl.when(jnp.logical_not(comes[da]))(without)
-
-        return arrived
+        leaving.append(everything.wait_send)
+        return everything.wait_recv
 
     def drain(but=0):
         while len(leaving) > but:
@@ -183,9 +223,16 @@
                 barrier, inc=1, device_id=(target,), device_id_type=pl.DeviceIdType.MESH
             )
 
-    here(sibling, sibling_far)
+    here(sibling)
+    pl.when(inside(j - 1 + 2 * half))(lambda: here(sibling_far))
     for da in (1, -1):
-        pl.when(leaves[da])(lambda: here(*[device(da, dj) for dj in (1, -1, 0)]))
+
+        def beside():
+            here(device(da, 0))
+            for dj in (1, -1):
+                pl.when(inside(j + dj))(lambda: here(device(da, dj)))
+
+        pl.when(leaves[da])(beside)
 
     raws = (raw_c, raw_s, raw_u)
     given = (conductance, source, initial)
@@ -202,13 +249,12 @@
     for copy in locals_:
         copy.start()
 
-    pl.semaphore_wait(barrier, 2 + 3 * (a > 0).astype(jnp.int32) + 3 * (a < 15).astype(jnp.int32))
+    around_x = 1 + (a > 0).astype(jnp.int32) + (a < 15).astype(jnp.int32)
+    around_y = 1 + (j > 0).astype(jnp.int32) + (j < 7).astype(jnp.int32)
+    pl.semaphore_wait(barrier, around_x * around_y - 1)
 
     swaps = [
-        start(
-            [(given[number].at[pl.ds(0, 3), :, theirs], raws[number].at[held], sibling)],
-            raws[number].at[held],
-        )
+        hand(given[number].at[pl.ds(0, 3), :, theirs], raws[number].at[held], raws[number].at[held])
         for number in range(3)
     ]
     locals_[0].wait()
@@ -276,16 +322,19 @@
 
     spare = list(post)
 
-    def ones(ref, *slabs):
-        for rows in slabs:
-            ref[rows, :] = jnp.ones((rows.size, LANES), F32)
+    def filler(ref, firsts, messages):
+        def without(*gaps):
+            for n in gaps:
+                ref[pl.ds(firsts[n], messages[n][0]), :] = jnp.ones((messages[n][0], LANES), F32)
+
+        return without
 
     def exchange(strips, corners, block=None, where=FULL):
         out, got = spare.pop(0), spare.pop(0)
         arrivals, filled = [], []
         offset = 0
         for step_x in (1, -1, 0):
-            copies, group_row = [], offset
+            copies, messages, group_row = [], [], offset
             for da, dj in FULL:
                 if da != step_x:
                     continue
@@ -295,10 +344,11 @@
                     offset += count
                 offset += -offset % 8
                 rows = pl.ds(first_row, offset - first_row)
-                copies.append((out.at[rows], got.at[rows], device(da, dj)))
+                copies.append((out.at[rows], got.at[rows], device(da, dj), dj))
+                messages.append((rows.size, da, dj))
                 filled.append((first_row, da, dj))
-            group = pl.ds(group_row, offset - group_row)
-            arrivals.append(start(copies, got.at[group], step_x, functools.partial(ones, got, group)))
+            firsts = [first for first, da, dj in filled if da == step_x]
+            arrivals.append(start(copies, got, group_row, messages, filler(got, firsts, messages)))
         assert out.shape == (offset, LANES)
 
         def land():
@@ -341,16 +391,12 @@
         for step_x in (1, -1, 0):
             places_ = [(da, dj) for da, dj in where if da == step_x]
             copies = [
-                (ref.at[pl.ds(own2, 8)], ref.at[pl.ds(there2(da, dj), 8)], device(da, dj))
+                (ref.at[pl.ds(own2, 8)], ref.at[pl.ds(there2(da, dj), 8)], device(da, dj), dj)
                 for da, dj in places_
             ]
-            slabs = [pl.ds(there2(da, dj), 8) for da, dj in places_]
-            arrivals.append(
-                start(
-                    copies, ref.at[pl.ds(0, 8 * len(copies))], step_x,
-                    functools.partial(ones, ref, *slabs),
-                )
-            )
+            firsts = [there2(da, dj) for da, dj in places_]
+            messages = [(8, da, dj) for da, dj in places_]
+            arrivals.append(start(copies, ref, 0, messages, filler(ref, firsts, messages)))
 
         def arrived():
             for part in arrivals:
@@ -564,7 +610,7 @@
 
         loop(0, 4, 4, step)
         lanes = pl.ds(128 * quads[0], 128 * len(quads))
-        return stage.at[pl.ds(1 - half, 3), :, lanes], other.at[:, :, lanes], sibling
+        return stage.at[pl.ds(1 - half, 3), :, lanes], other.at[:, :, lanes], other.at[:, :, lanes]
 
     def keep(stage, out):
         for s in range(4):
@@ -576,13 +622,13 @@
 
     last = []
     sweep(u1, u2, fine_faces, gf, 3, 12, 9, RF, 4, 40, 1)
-    last.append(start([give(u2, stage_f, other_f, (0, 1))], other_f.at[:, :, pl.ds(0, 256)]))
+    last.append(hand(*give(u2, stage_f, other_f, (0, 1))))
     sweep(u1, u2, fine_faces, gf, 12, 21, 9, RF, 4, 40, 1)
-    last.append(start([give(u2, stage_f, other_f, (2, 3))], other_f.at[:, :, pl.ds(256, 256)]))
+    last.append(hand(*give(u2, stage_f, other_f, (2, 3))))
     leftover(u2, u1, fine_faces, gf, df, 4, 12, 8, RF, 8, 32, 1)
-    last.append(start([give(u1, stage_r, other_r, (0, 1))], other_r.at[:, :, pl.ds(0, 256)]))
+    last.append(hand(*give(u1, stage_r, other_r, (0, 1))))
     leftover(u2, u1, fine_faces, gf, df, 12, 20, 8, RF, 8, 32, 1)
-    last.append(start([give(u1, stage_r, other_r, (2, 3))], other_r.at[:, :, pl.ds(256, 256)]))
+    last.append(hand(*give(u1, stage_r, other_r, (2, 3))))
     keep(stage_f, out_field)
     last[0]()
     last[1]()

time: 27.8 us -> 27.2 us (0.978)
  the two profiles are of different devices: /device:TPU:7 before, /device:TPU:71 now
where the time goes in v12:
time: 27.2 us; the launch traced here: 27.1 us
  Pallas kernels  25.4 us (93%)
  other arithmetic  1.11 us (4%)
  between operations  0.64 us (2%)
    pallas_call x1, Pallas kernels, body(): pl.pallas_call(kernel, out_shape=(shape,) * 3, in_specs=[hbm] * 4, out_sp...  25.4 us
    mul x1, other arithmetic, body(): return (field * held, resid * held)  1.11 us

profile of v12, /device:TPU:71, one launch (start us, length us, event | category | flops | bytes accessed | tf_op | source)
XLA Modules:
  0.0 27.1 jit_solution(13598035279801168751)
XLA Ops:
  0.6 25.4 %shard_map.59 = (f32[4,32,1024]{2,1,0:T(8,128)S(1)}, f32[4,32,1024]{2,1,0:T(8,128)S(1)}, f32[4,32,1024]{2,1,0:T(8,128)S(1)}) custom-call(s32[128]{0:T(128)} %counts.1, f32[4,32,1024]{2,1,0:T(8,128)} %source.1, f32[4,32,1024]{2,1,0:T(8,128)} %conductance.1, f32[4,32,1024]{2,1,0:T(8,128)} %initial.1), custom_call_target="tpu_custom_call" | custom-call | flops 30000000 | bytes 3000000 | tf_op jit(solution)/shard_map/pallas_call | solution.py:661
  26.0 1.1 %fusion = (f32[4,32,1024]{2,1,0:T(8,128)}, f32[4,32,1024]{2,1,0:T(8,128)}) fusion(f32[4,32,1024]{2,1,0:T(8,128)S(1)} %get-tuple-element.7, f32[4,32,1024]{2,1,0:T(8,128)S(1)} %get-tuple-element.6, f32[4,32,1024]{2,1,0:T(8,128)S(1)} %get-tuple-element.5), kind=kLoop, calls=%fused_computation | loop fusion | flops 262144 | bytes 2621440 | tf_op jit(solution)/shard_map/mul | solution.py:672

commit v13 on v12

--- a/solution.py
+++ b/solution.py
@@ -15,7 +15,7 @@
 FULL = (1, 1), (1, -1), (1, 0), (-1, 1), (-1, -1), (-1, 0), (0, 1), (0, -1)
 FAR = (1, 2), (1, -2), (-1, 2), (-1, -2), (0, 2), (0, -2)
 F32 = jnp.float32
-ROUNDS = 3 + 3 * (5 + 2) + 4
+ROUNDS = 3 + 3 * (5 + 2) + 6
 
 
 def lane_ids(rows):
@@ -63,11 +63,23 @@
     return faces, total, quarter
 
 
-def around(ref, base, count, rows, twist):
-    centre = ref[pl.ds(base, count), :]
+class Planes:
+    def __init__(self):
+        self.held = {}
+        self.step = 0
+
+    def load(self, ref, base, count, rows, ahead):
+        key = (id(ref), count, self.step + ahead)
+        if key not in self.held:
+            self.held[key] = ref[pl.ds(base + rows * ahead, count), :]
+        return self.held[key]
+
+
+def around(ref, base, count, rows, twist, planes):
+    centre = planes.load(ref, base, count, rows, 0)
     return centre, (
-        ref[pl.ds(base - rows, count), :],
-        ref[pl.ds(base + rows, count), :],
+        planes.load(ref, base, count, rows, -1),
+        planes.load(ref, base, count, rows, 1),
         ref[pl.ds(base - 1, count), :],
         ref[pl.ds(base + 1, count), :],
         turn(centre, twist),
@@ -86,13 +98,14 @@
 
     def step(index, carry):
         first = base + low + index * width
-        stores = []
+        stores, planes = [], Planes()
         for m in range(width):
-            stores += body(first + m)
+            planes.step = m
+            stores += body(first + m, planes)
             if (m + 1) % group == 0 or m == width - 1:
                 for ref, index_, value in stores:
                     ref[index_] = value
-                stores = []
+                stores, planes = [], Planes()
         return carry
 
     if high - low == width:
@@ -269,7 +282,7 @@
         swaps[number]()
         raw = raws[number]
 
-        def step(t):
+        def step(t, planes):
             rows = pl.ds(pl.multiple_of(8 * t, 8), 8)
             out = []
             for q in range(4):
@@ -372,7 +385,7 @@
     bring(2, uf)
     land_u = exchange(((uf, 0, (1, 2, 3)),), fine_corner(uf, 3))
 
-    def coarse_c(i):
+    def coarse_c(i, planes):
         total = pair_rows(cf, (4 + 2 * i) * RF + 8, 16, RF)
         return [(c1, at(pl.multiple_of((8 + i) * R1 + 8, 8), 16), pair_lanes(total, 1))]
 
@@ -409,6 +422,25 @@
         ((c1, 1, (1, 2, 3, 4, 5, 6)),), [(c1, 1, d, 1, 6 - d) for d in range(1, 6)], c2
     )
 
+    fine_faces = [fine.at[n] for n in range(6)]
+
+    def fine_coeffs(*windows):
+        def body(p, planes):
+            out = []
+            for start_row, count in windows:
+                base = p * RF + start_row
+                centre, besides = around(cf, base, count, RF, 1, Planes())
+                z = lane_ids(count)
+                inside = (None, None, None, None, z != 0, z != 127)
+                faces, total, quarter = coefficients(centre, besides, inside)
+                out += [(fine, (n,) + at(base, count), faces[n]) for n in range(6)]
+                out.append((gf, at(base, count), 2.0 * quarter))
+                out.append((df, at(base, count), 1.25 * total))
+            return out
+
+        return body
+
+    loop(5, 19, 7, fine_coeffs((12, 24)), group=1)
     land_c()
     far_c2 = blocks2(c2, FAR)
 
@@ -433,36 +465,43 @@
 
     ends = (j == 0, j == 7, a == 0, a == 15)
     edges(cf, 4, 40, 16, RF, 4, (8, 39), *ends)
-    fine_faces = [fine.at[n] for n in range(6)]
-
-    def fine_coeffs(p):
-        base = p * RF + 4
-        centre, besides = around(cf, base, 40, RF, 1)
-        z = lane_ids(40)
-        inside = (None, None, None, None, z != 0, z != 127)
-        faces, total, quarter = coefficients(centre, besides, inside)
-        out = [(fine, (n,) + at(base, 40), faces[n]) for n in range(6)]
-        out.append((gf, at(base, 40), 2.0 * quarter))
-        out.append((df, at(base, 40), 1.25 * total))
-        return out
-
-    loop(2, 22, 4, fine_coeffs, group=1)
+    loop(5, 19, 7, fine_coeffs((4, 8), (36, 8)), group=1)
+    for low in (2, 19):
+        loop(low, low + 3, 3, fine_coeffs((4, 40)), group=1)
     cut(fine, 4, 40, 16, RF, 4, (8, 39), *ends)
+
+    def first_sweep(*windows):
+        def body(p, planes):
+            out = []
+            for start_row, count in windows:
+                base = p * RF + start_row
+                centre, besides = around(uf, base, count, RF, 1, planes if len(windows) == 1 else Planes())
+                right = gf[pl.ds(base, count), :] * sf[pl.ds(base, count), :]
+                value = 0.2 * centre + right + weighted(fine_faces, base, count, besides)
+                out += [(u1, at(base, count), value), (gf, at(base, count), right)]
+            return out
+
+        return body
+
+    loop(5, 19, 7, first_sweep((12, 24)))
     land_u()
+    loop(5, 19, 7, first_sweep((4, 8), (36, 8)))
+    for low in (2, 19):
+        loop(low, low + 3, 3, first_sweep((4, 40)))
 
     def sweep(src, dst, faces, right, low, high, width, rows, start, count, twist):
-        def step(p):
+        def step(p, planes):
             base = p * rows + start
-            centre, besides = around(src, base, count, rows, twist)
+            centre, besides = around(src, base, count, rows, twist, planes)
             value = 0.2 * centre + right[pl.ds(base, count), :] + weighted(faces, base, count, besides)
             return [(dst, at(base, count), value)]
 
         loop(low, high, width, step, group=5)
 
     def leftover(src, dst, faces, right, diag, low, high, width, rows, start, count, twist):
-        def step(p):
+        def step(p, planes):
             base = p * rows + start
-            centre, besides = around(src, base, count, rows, twist)
+            centre, besides = around(src, base, count, rows, twist, planes)
             value = diag[pl.ds(base, count), :] * (
                 right[pl.ds(base, count), :] + weighted(faces, base, count, besides) - 0.8 * centre
             )
@@ -470,18 +509,10 @@
 
         loop(low, high, width, step, group=4)
 
-    def first_sweep(p):
-        base = p * RF + 4
-        centre, besides = around(uf, base, 40, RF, 1)
-        right = gf[pl.ds(base, 40), :] * sf[pl.ds(base, 40), :]
-        value = 0.2 * centre + right + weighted(fine_faces, base, 40, besides)
-        return [(u1, at(base, 40), value), (gf, at(base, 40), right)]
-
-    loop(2, 22, 10, first_sweep, group=5)
     sweep(u1, u2, fine_faces, gf, 3, 21, 9, RF, 4, 40, 1)
     leftover(u2, u1, fine_faces, gf, df, 4, 20, 8, RF, 8, 32, 1)
 
-    def coarse_f(i):
+    def coarse_f(i, planes):
         total = pair_rows(u1, (4 + 2 * i) * RF + 8, 16, RF)
         return [(f1, at(pl.multiple_of((8 + i) * R1 + 8, 8), 16), pair_lanes(total, 1))]
 
@@ -497,9 +528,9 @@
     edges(c1, 0, 32, 8, R1, 8, (8, 23), *ends)
     mid_faces = [mid.at[n] for n in range(6)]
 
-    def mid_coeffs(p):
+    def mid_coeffs(p, planes):
         base = p * R1
-        centre, besides = around(c1, base, 32, R1, 2)
+        centre, besides = around(c1, base, 32, R1, 2, planes)
         z = lane_ids(32)
         inside = (None, None, None, None, z >= 2, z < 126)
         faces, total, quarter = coefficients(centre, besides, inside)
@@ -511,7 +542,7 @@
     loop(6, 18, 3, mid_coeffs, group=1)
     cut(mid, 0, 32, 8, R1, 8, (8, 23), *ends)
 
-    def guess(p):
+    def guess(p, planes):
         base = p * R1
         return [(g1, at(base, 32), w1[pl.ds(base, 32), :] * f1[pl.ds(base, 32), :])]
 
@@ -574,7 +605,7 @@
         pe2[pl.ds(32 * number, 16, stride=2), :] = value
         pe2[pl.ds(32 * number + 1, 16, stride=2), :] = value
 
-    def corrected1(p):
+    def corrected1(p, planes):
         value = e1[pl.ds(p * R1 + 4, 24), :] + pe2[pl.ds((p // 2 - 2) * 32 + 4, 24), :]
         return [(e1, at(p * R1 + 4, 24), value)]
 
@@ -582,13 +613,13 @@
     sweep(e1, e1b, mid_faces, g1, 5, 19, 14, R1, 4, 24, 2)
     sweep(e1b, e1, mid_faces, g1, 6, 18, 12, R1, 4, 24, 2)
 
-    def grown(i):
+    def grown(i, planes):
         value = e1[pl.ds((i + 6) * R1 + 4, 24), :]
         return [(pe1, (pl.ds(RF * i + odd, 24, stride=2), slice(None)), value) for odd in (0, 1)]
 
     loop(0, 12, 12, grown)
 
-    def corrected0(p):
+    def corrected0(p, planes):
         base = p * RF + 4
         return [(u2, at(base, 40), u2[pl.ds(base, 40), :] + pe1[pl.ds((p // 2) * RF + 4, 40), :])]
 
@@ -596,7 +627,7 @@
     sweep(u2, u1, fine_faces, gf, 2, 22, 10, RF, 4, 40, 1)
 
     def give(ref, stage, other, quads):
-        def step(t):
+        def step(t, planes):
             rows = pl.ds(pl.multiple_of(8 * t, 8), 8)
             out = []
             for q in quads:
@@ -625,17 +656,16 @@
     last.append(hand(*give(u2, stage_f, other_f, (0, 1))))
     sweep(u1, u2, fine_faces, gf, 12, 21, 9, RF, 4, 40, 1)
     last.append(hand(*give(u2, stage_f, other_f, (2, 3))))
-    leftover(u2, u1, fine_faces, gf, df, 4, 12, 8, RF, 8, 32, 1)
-    last.append(hand(*give(u1, stage_r, other_r, (0, 1))))
-    leftover(u2, u1, fine_faces, gf, df, 12, 20, 8, RF, 8, 32, 1)
-    last.append(hand(*give(u1, stage_r, other_r, (2, 3))))
+    for q in range(4):
+        leftover(u2, u1, fine_faces, gf, df, 4 + 4 * q, 8 + 4 * q, 4, RF, 8, 32, 1)
+        last.append(hand(*give(u1, stage_r, other_r, (q,))))
     keep(stage_f, out_field)
     last[0]()
     last[1]()
     take(other_f, out_field)
     keep(stage_r, out_resid)
-    last[2]()
-    last[3]()
+    for arrived in last[2:]:
+        arrived()
     take(other_r, out_resid)
     drain()
 

time: 27.2 us -> 27.5 us (1.011)
  no operation moved by 1% of the time
where the time goes in v13:
time: 27.5 us; the launch traced here: 27.3 us
  Pallas kernels  25.6 us (93%)
  other arithmetic  1.11 us (4%)
  between operations  0.64 us (2%)
    pallas_call x1, Pallas kernels, body(): pl.pallas_call(kernel, out_shape=(shape,) * 3, in_specs=[hbm] * 4, out_sp...  25.6 us
    mul x1, other arithmetic, body(): return (field * held, resid * held)  1.11 us

profile of v13, /device:TPU:71, one launch (start us, length us, event | category | flops | bytes accessed | tf_op | source)
XLA Modules:
  0.0 27.3 jit_solution(8128837806830883200)
XLA Ops:
  0.6 25.6 %shard_map.59 = (f32[4,32,1024]{2,1,0:T(8,128)S(1)}, f32[4,32,1024]{2,1,0:T(8,128)S(1)}, f32[4,32,1024]{2,1,0:T(8,128)S(1)}) custom-call(s32[128]{0:T(128)} %counts.1, f32[4,32,1024]{2,1,0:T(8,128)} %source.1, f32[4,32,1024]{2,1,0:T(8,128)} %conductance.1, f32[4,32,1024]{2,1,0:T(8,128)} %initial.1), custom_call_target="tpu_custom_call" | custom-call | flops 30000000 | bytes 3000000 | tf_op jit(solution)/shard_map/pallas_call | solution.py:691
  26.2 1.1 %fusion = (f32[4,32,1024]{2,1,0:T(8,128)}, f32[4,32,1024]{2,1,0:T(8,128)}) fusion(f32[4,32,1024]{2,1,0:T(8,128)S(1)} %get-tuple-element.7, f32[4,32,1024]{2,1,0:T(8,128)S(1)} %get-tuple-element.6, f32[4,32,1024]{2,1,0:T(8,128)S(1)} %get-tuple-element.5), kind=kLoop, calls=%fused_computation | loop fusion | flops 262144 | bytes 2621440 | tf_op jit(solution)/shard_map/mul | solution.py:702

commit v14 on v12

--- a/solution.py
+++ b/solution.py
@@ -192,17 +192,22 @@
                     pl.when(jnp.logical_not(inside(j - dj)))(functools.partial(without, *gaps))
 
         if step_x == 0:
-            go()
             leaving.append(gone)
-            return come
-        pl.when(leaves[step_x])(go)
+            return go, come
         leaving.append(lambda: pl.when(leaves[step_x])(gone))
 
         def arrived():
             pl.when(comes[step_x])(come)
             pl.when(jnp.logical_not(comes[step_x]))(functools.partial(without, *range(len(messages))))
 
-        return arrived
+        return go, arrived
+
+    seam = a % 4 == 0
+
+    def depart(plus, minus):
+        pl.when(jnp.logical_and(leaves[-1], seam))(minus)
+        pl.when(leaves[1])(plus)
+        pl.when(jnp.logical_and(leaves[-1], jnp.logical_not(seam)))(minus)
 
     def hand(src, dst, whole):
         number = next(numbers)
@@ -348,7 +353,14 @@
                 messages.append((rows.size, da, dj))
                 filled.append((first_row, da, dj))
             firsts = [first for first, da, dj in filled if da == step_x]
-            arrivals.append(start(copies, got, group_row, messages, filler(got, firsts, messages)))
+            go, arrived = start(copies, got, group_row, messages, filler(got, firsts, messages))
+            arrivals.append(arrived)
+            if step_x == 1:
+                plus = go
+            elif step_x == -1:
+                depart(plus, go)
+            else:
+                go()
         assert out.shape == (offset, LANES)
 
         def land():
@@ -396,7 +408,14 @@
             ]
             firsts = [there2(da, dj) for da, dj in places_]
             messages = [(8, da, dj) for da, dj in places_]
-            arrivals.append(start(copies, ref, 0, messages, filler(ref, firsts, messages)))
+            go, arrived = start(copies, ref, 0, messages, filler(ref, firsts, messages))
+            arrivals.append(arrived)
+            if step_x == 1:
+                plus = go
+            elif step_x == -1:
+                depart(plus, go)
+            else:
+                go()
 
         def arrived():
             for part in arrivals:

time: 27.2 us -> 27.3 us (level)
  the two profiles are of different devices: /device:TPU:71 before, /device:TPU:97 now
where the time goes in v14:
time: 27.3 us; the launch traced here: 27.2 us
  Pallas kernels  25.4 us (93%)
  other arithmetic  1.11 us (4%)
  between operations  0.64 us (2%)
    pallas_call x1, Pallas kernels, body(): pl.pallas_call(kernel, out_shape=(shape,) * 3, in_specs=[hbm] * 4, out_sp...  25.4 us
    mul x1, other arithmetic, body(): return (field * held, resid * held)  1.11 us

profile of v14, /device:TPU:97, one launch (start us, length us, event | category | flops | bytes accessed | tf_op | source)
XLA Modules:
  0.0 27.2 jit_solution(396148271324518929)
XLA Ops:
  0.6 25.4 %shard_map.59 = (f32[4,32,1024]{2,1,0:T(8,128)S(1)}, f32[4,32,1024]{2,1,0:T(8,128)S(1)}, f32[4,32,1024]{2,1,0:T(8,128)S(1)}) custom-call(s32[128]{0:T(128)} %counts.1, f32[4,32,1024]{2,1,0:T(8,128)} %source.1, f32[4,32,1024]{2,1,0:T(8,128)} %conductance.1, f32[4,32,1024]{2,1,0:T(8,128)} %initial.1), custom_call_target="tpu_custom_call" | custom-call | flops 30000000 | bytes 3000000 | tf_op jit(solution)/shard_map/pallas_call | solution.py:680
  26.0 1.1 %fusion = (f32[4,32,1024]{2,1,0:T(8,128)}, f32[4,32,1024]{2,1,0:T(8,128)}) fusion(f32[4,32,1024]{2,1,0:T(8,128)S(1)} %get-tuple-element.7, f32[4,32,1024]{2,1,0:T(8,128)S(1)} %get-tuple-element.6, f32[4,32,1024]{2,1,0:T(8,128)S(1)} %get-tuple-element.5), kind=kLoop, calls=%fused_computation | loop fusion | flops 262144 | bytes 2621440 | tf_op jit(solution)/shard_map/mul | solution.py:691

commit v15 on v12

--- a/solution.py
+++ b/solution.py
@@ -120,7 +120,7 @@
 def kernel(
     counts, source, conductance, initial, out_field, out_resid, out_held,
     owners, raw_c, raw_u, raw_s, cf, uf, sf, u1, u2, fine, gf, df,
-    c1, f1, e1, e1b, pe2, mid, w1, g1, d1, r1, c2, f2, e2, e2b, deep, g2, pe1,
+    c1, f1, e1, e1b, mid, w1, g1, d1, r1, c2, f2, e2, e2b, deep, g2,
     stage_f, stage_r, other_f, other_r, *rest,
 ):
     post, local_sem, send_sem, recv_sem = rest[:-3], rest[-3], rest[-2], rest[-1]
@@ -564,35 +564,31 @@
             (0.2 * centre + g2[...]) + (parts[0] + parts[1]) + (parts[2] + parts[3]) + (parts[4] + parts[5])
         )
 
+    def spread(ref, first, count, rows, value):
+        slabs = [slab(ref, first + offset, count, 2) for offset in (0, 1, rows, rows + 1)]
+        return [(ref, where, ref[where] + value) for where in slabs]
+
     lanes16 = lane_ids(16) % 4
     hops = ((1, 2), (-1, 2), (1, -2), (-1, -2))
+    added = []
     for number in range(8):
         block, i = (number + 6) // 4, (number + 6) % 4
         value = jnp.where(lanes16 == i, e2b[pl.ds(zero + (R2 + R2 * block + 4), 16), :], 0.0)
         value = value + turn(value, hops[i][0])
         value = value + turn(value, hops[i][1])
-        pe2[pl.ds(32 * number, 16, stride=2), :] = value
-        pe2[pl.ds(32 * number + 1, 16, stride=2), :] = value
-
-    def corrected1(p):
-        value = e1[pl.ds(p * R1 + 4, 24), :] + pe2[pl.ds((p // 2 - 2) * 32 + 4, 24), :]
-        return [(e1, at(p * R1 + 4, 24), value)]
-
-    loop(4, 20, 16, corrected1)
+        added += spread(e1, (4 + 2 * number) * R1, 16, R1, value)
+        if number % 4 == 3:
+            for ref, where, total in added:
+                ref[where] = total
+            added = []
+
     sweep(e1, e1b, mid_faces, g1, 5, 19, 14, R1, 4, 24, 2)
     sweep(e1b, e1, mid_faces, g1, 6, 18, 12, R1, 4, 24, 2)
 
     def grown(i):
-        value = e1[pl.ds((i + 6) * R1 + 4, 24), :]
-        return [(pe1, (pl.ds(RF * i + odd, 24, stride=2), slice(None)), value) for odd in (0, 1)]
-
-    loop(0, 12, 12, grown)
-
-    def corrected0(p):
-        base = p * RF + 4
-        return [(u2, at(base, 40), u2[pl.ds(base, 40), :] + pe1[pl.ds((p // 2) * RF + 4, 40), :])]
-
-    loop(1, 23, 11, corrected0)
+        return spread(u2, 2 * i * RF, 24, RF, e1[pl.ds((i + 6) * R1 + 4, 24), :])
+
+    loop(0, 12, 6, grown, group=3)
     sweep(u2, u1, fine_faces, gf, 2, 22, 10, RF, 4, 40, 1)
 
     def give(ref, stage, other, quads):
@@ -650,8 +646,8 @@
     deep_field = vmem(7 * R2, LANES)
     scratch = [pltpu.SMEM(box_counts.shape, jnp.int32)] + [vmem(6, 32, 512)] * 3
     scratch += [fine_field] * 5 + [vmem(6, PF * RF, LANES)] + [fine_field] * 2
-    scratch += [mid_field] * 4 + [vmem(8 * 32, LANES), vmem(6, P1 * R1, LANES)] + [mid_field] * 4
-    scratch += [deep_field] * 4 + [vmem(7, 5 * R2, LANES), vmem(5 * R2, LANES), vmem(12 * RF, LANES)]
+    scratch += [mid_field] * 4 + [vmem(6, P1 * R1, LANES)] + [mid_field] * 4
+    scratch += [deep_field] * 4 + [vmem(7, 5 * R2, LANES), vmem(5 * R2, LANES)]
     scratch += [vmem(4, 32, 512)] * 2 + [vmem(3, 32, 512)] * 2
     for big, middle, small in ((160, 80, 8), (96, 48, 8), (104, 56, 24), (32, 16, 8), (144, 72, 16)):
         scratch += [vmem(2 * big + 2 * middle + 4 * small, LANES)] * 2

time: 27.2 us -> 27.2 us (level)
  no operation moved by 1% of the time
where the time goes in v15:
time: 27.2 us; the launch traced here: 27.1 us
  Pallas kernels  25.3 us (93%)
  other arithmetic  1.11 us (4%)
  between operations  0.64 us (2%)
    pallas_call x1, Pallas kernels, body(): pl.pallas_call(kernel, out_shape=(shape,) * 3, in_specs=[hbm] * 4, out_sp...  25.3 us
    mul x1, other arithmetic, body(): return (field * held, resid * held)  1.11 us

profile of v15, /device:TPU:71, one launch (start us, length us, event | category | flops | bytes accessed | tf_op | source)
XLA Modules:
  0.0 27.1 jit_solution(2038528527254032616)
XLA Ops:
  0.6 25.3 %shard_map.59 = (f32[4,32,1024]{2,1,0:T(8,128)S(1)}, f32[4,32,1024]{2,1,0:T(8,128)S(1)}, f32[4,32,1024]{2,1,0:T(8,128)S(1)}) custom-call(s32[128]{0:T(128)} %counts.1, f32[4,32,1024]{2,1,0:T(8,128)} %source.1, f32[4,32,1024]{2,1,0:T(8,128)} %conductance.1, f32[4,32,1024]{2,1,0:T(8,128)} %initial.1), custom_call_target="tpu_custom_call" | custom-call | flops 30000000 | bytes 3000000 | tf_op jit(solution)/shard_map/pallas_call | solution.py:657
  25.9 1.1 %fusion = (f32[4,32,1024]{2,1,0:T(8,128)}, f32[4,32,1024]{2,1,0:T(8,128)}) fusion(f32[4,32,1024]{2,1,0:T(8,128)S(1)} %get-tuple-element.7, f32[4,32,1024]{2,1,0:T(8,128)S(1)} %get-tuple-element.6, f32[4,32,1024]{2,1,0:T(8,128)S(1)} %get-tuple-element.5), kind=kLoop, calls=%fused_computation | loop fusion | flops 262144 | bytes 2621440 | tf_op jit(solution)/shard_map/mul | solution.py:668

commit v16 on v15

--- a/solution.py
+++ b/solution.py
@@ -204,9 +204,10 @@
 
         return arrived
 
-    def hand(src, dst, whole):
+    def hand(copies, whole):
         number = next(numbers)
-        describe(src, dst, number, sibling).start()
+        for src, dst in copies:
+            describe(src, dst, number, sibling).start()
         everything = describe(whole, whole, number, sibling)
         leaving.append(everything.wait_send)
         return everything.wait_recv
@@ -223,16 +224,16 @@
                 barrier, inc=1, device_id=(target,), device_id_type=pl.DeviceIdType.MESH
             )
 
-    here(sibling)
-    pl.when(inside(j - 1 + 2 * half))(lambda: here(sibling_far))
     for da in (1, -1):
 
         def beside():
-            here(device(da, 0))
             for dj in (1, -1):
                 pl.when(inside(j + dj))(lambda: here(device(da, dj)))
+            here(device(da, 0))
 
         pl.when(leaves[da])(beside)
+    pl.when(inside(j - 1 + 2 * half))(lambda: here(sibling_far))
+    here(sibling)
 
     raws = (raw_c, raw_s, raw_u)
     given = (conductance, source, initial)
@@ -254,7 +255,10 @@
     pl.semaphore_wait(barrier, around_x * around_y - 1)
 
     swaps = [
-        hand(given[number].at[pl.ds(0, 3), :, theirs], raws[number].at[held], raws[number].at[held])
+        hand(
+            [(given[number].at[s, :, theirs], raws[number].at[3 * half + s]) for s in range(3)],
+            raws[number].at[held],
+        )
         for number in range(3)
     ]
     locals_[0].wait()
@@ -606,7 +610,7 @@
 
         loop(0, 4, 4, step)
         lanes = pl.ds(128 * quads[0], 128 * len(quads))
-        return stage.at[pl.ds(1 - half, 3), :, lanes], other.at[:, :, lanes], other.at[:, :, lanes]
+        return [(stage.at[pl.ds(1 - half, 3), :, lanes], other.at[:, :, lanes])], other.at[:, :, lanes]
 
     def keep(stage, out):
         for s in range(4):

time: 27.2 us -> 27.2 us (level)
  no operation moved by 1% of the time
where the time goes in v16:
time: 27.2 us; the launch traced here: 27.1 us
  Pallas kernels  25.3 us (93%)
  other arithmetic  1.11 us (4%)
  between operations  0.64 us (2%)
    pallas_call x1, Pallas kernels, body(): pl.pallas_call(kernel, out_shape=(shape,) * 3, in_specs=[hbm] * 4, out_sp...  25.3 us
    mul x1, other arithmetic, body(): return (field * held, resid * held)  1.11 us

profile of v16, /device:TPU:71, one launch (start us, length us, event | category | flops | bytes accessed | tf_op | source)
XLA Modules:
  0.0 27.1 jit_solution(1779130649309974835)
XLA Ops:
  0.6 25.3 %shard_map.59 = (f32[4,32,1024]{2,1,0:T(8,128)S(1)}, f32[4,32,1024]{2,1,0:T(8,128)S(1)}, f32[4,32,1024]{2,1,0:T(8,128)S(1)}) custom-call(s32[128]{0:T(128)} %counts.1, f32[4,32,1024]{2,1,0:T(8,128)} %source.1, f32[4,32,1024]{2,1,0:T(8,128)} %conductance.1, f32[4,32,1024]{2,1,0:T(8,128)} %initial.1), custom_call_target="tpu_custom_call" | custom-call | flops 30000000 | bytes 3000000 | tf_op jit(solution)/shard_map/pallas_call | solution.py:661
  26.0 1.1 %fusion = (f32[4,32,1024]{2,1,0:T(8,128)}, f32[4,32,1024]{2,1,0:T(8,128)}) fusion(f32[4,32,1024]{2,1,0:T(8,128)S(1)} %get-tuple-element.7, f32[4,32,1024]{2,1,0:T(8,128)S(1)} %get-tuple-element.6, f32[4,32,1024]{2,1,0:T(8,128)S(1)} %get-tuple-element.5), kind=kLoop, calls=%fused_computation | loop fusion | flops 262144 | bytes 2621440 | tf_op jit(solution)/shard_map/mul | solution.py:672

commit v17 on v16

--- a/solution.py
+++ b/solution.py
@@ -645,12 +645,12 @@
 
 
 def body(source, conductance, initial, box_counts):
-    fine_field = vmem(PF * RF, LANES)
-    mid_field = vmem(P1 * R1, LANES)
+    fine_field = vmem((PF + 1) * RF, LANES)
+    mid_field = vmem((P1 + 1) * R1, LANES)
     deep_field = vmem(7 * R2, LANES)
     scratch = [pltpu.SMEM(box_counts.shape, jnp.int32)] + [vmem(6, 32, 512)] * 3
-    scratch += [fine_field] * 5 + [vmem(6, PF * RF, LANES)] + [fine_field] * 2
-    scratch += [mid_field] * 4 + [vmem(6, P1 * R1, LANES)] + [mid_field] * 4
+    scratch += [fine_field] * 5 + [vmem(6, (PF + 1) * RF, LANES)] + [fine_field] * 2
+    scratch += [mid_field] * 4 + [vmem(6, (P1 + 1) * R1, LANES)] + [mid_field] * 4
     scratch += [deep_field] * 4 + [vmem(7, 5 * R2, LANES), vmem(5 * R2, LANES)]
     scratch += [vmem(4, 32, 512)] * 2 + [vmem(3, 32, 512)] * 2
     for big, middle, small in ((160, 80, 8), (96, 48, 8), (104, 56, 24), (32, 16, 8), (144, 72, 16)):

time: 27.2 us -> 27.4 us (level)
  no operation moved by 1% of the time
where the time goes in v17:
time: 27.4 us; the launch traced here: 27.3 us
  Pallas kernels  25.5 us (93%)
  other arithmetic  1.11 us (4%)
  between operations  0.64 us (2%)
    pallas_call x1, Pallas kernels, body(): pl.pallas_call(kernel, out_shape=(shape,) * 3, in_specs=[hbm] * 4, out_sp...  25.5 us
    mul x1, other arithmetic, body(): return (field * held, resid * held)  1.11 us

profile of v17, /device:TPU:71, one launch (start us, length us, event | category | flops | bytes accessed | tf_op | source)
XLA Modules:
  0.0 27.3 jit_solution(7666514813262769339)
XLA Ops:
  0.6 25.5 %shard_map.59 = (f32[4,32,1024]{2,1,0:T(8,128)S(1)}, f32[4,32,1024]{2,1,0:T(8,128)S(1)}, f32[4,32,1024]{2,1,0:T(8,128)S(1)}) custom-call(s32[128]{0:T(128)} %counts.1, f32[4,32,1024]{2,1,0:T(8,128)} %source.1, f32[4,32,1024]{2,1,0:T(8,128)} %conductance.1, f32[4,32,1024]{2,1,0:T(8,128)} %initial.1), custom_call_target="tpu_custom_call" | custom-call | flops 30000000 | bytes 3000000 | tf_op jit(solution)/shard_map/pallas_call | solution.py:661
  26.2 1.1 %fusion = (f32[4,32,1024]{2,1,0:T(8,128)}, f32[4,32,1024]{2,1,0:T(8,128)}) fusion(f32[4,32,1024]{2,1,0:T(8,128)S(1)} %get-tuple-element.7, f32[4,32,1024]{2,1,0:T(8,128)S(1)} %get-tuple-element.6, f32[4,32,1024]{2,1,0:T(8,128)S(1)} %get-tuple-element.5), kind=kLoop, calls=%fused_computation | loop fusion | flops 262144 | bytes 2621440 | tf_op jit(solution)/shard_map/mul | solution.py:672
